TPU v7x, 32 devices: a whole 2x2x4 slice. The times are simulated.
32 devices in a mesh: ctx: 8 (over y, x, core), head: 4 (over z).
Axes of the slice: x: 2, y: 2, z: 4, core: 2. Of those that a mesh axis runs over, the one named last changes fastest.
Arguments:
- query: bfloat16 [4096, 4096], P(('ctx', 'head')), may hold values from -12 to 12
- key: bfloat16 [4096, 1024], P(('ctx', 'head')), may hold values from -4 to 4
- value: bfloat16 [4096, 1024], P(('ctx', 'head')), may hold values from -5 to 5
- d_out: bfloat16 [4096, 4096], P(('ctx', 'head')), may hold values from -5 to 5
- stretch_ids: int32 [16], replicated, may hold values from 0 to 15, as said below
Outputs:
- grad_query: bfloat16 [4096, 4096], P(('ctx', 'head'))
- grad_key: bfloat16 [4096, 1024], P(('ctx', 'head'))
- grad_value: bfloat16 [4096, 1024], P(('ctx', 'head'))
Inputs may be any that keep to these rules, and one draw needn't show every extreme that they name: `stretch_ids`: a permutation in which slots 2r and 2r+1 hold blocks c and 15 - c for some c, in either order.
All inputs are finite; a program needn't handle non-finite values.
Results may differ from a plain program's by a relative error of at most 0.028.
Values may be sent and summed in bfloat16 or wider, within the bound.
No kernel may reach another device: no remote copies, remote signals or barrier semaphores. Data moves between devices by JAX's collectives and lax.ppermute only.
A program may use at most 128 MiB of HBM per device.

v0:
```python
import jax
import jax.numpy as jnp
from jax import lax
from jax.sharding import PartitionSpec as P

QUERY_HEAD_COUNT = 32
KEY_VALUE_HEADS = 8
HEAD_SIZE = 128
WINDOW = 4


def from_behind(shard, axis, by):
    devices = lax.axis_size(axis)
    return lax.ppermute(shard, axis, [(i, (i + by) % devices) for i in range(devices)])


def add_rows(total, update, start, mesh_axis):
    current = lax.dynamic_slice_in_dim(total, start, update.shape[mesh_axis], mesh_axis)
    return lax.dynamic_update_slice_in_dim(total, current + update, start, mesh_axis)


def body(query, key, value, d_out, stretch_ids):
    token_count_local = query.shape[0]
    head_partitions = lax.axis_size("head")
    ctx_devices = lax.axis_size("ctx")
    group_width = QUERY_HEAD_COUNT // KEY_VALUE_HEADS
    local_key_value = KEY_VALUE_HEADS // head_partitions
    scale = HEAD_SIZE ** (-0.5)

    def split_heads(array):
        return array.reshape(token_count_local, head_partitions, array.shape[1] // head_partitions)

    q_in, k_in, v_in, d_in = (
        lax.all_to_all(split_heads(query), "head", split_axis=1, concat_axis=0, tiled=True),
        lax.all_to_all(split_heads(key), "head", split_axis=1, concat_axis=0, tiled=True),
        lax.all_to_all(split_heads(value), "head", split_axis=1, concat_axis=0, tiled=True),
        lax.all_to_all(split_heads(d_out), "head", split_axis=1, concat_axis=0, tiled=True),
    )
    row_count = token_count_local * head_partitions
    stretch_rows = row_count // 2
    query_heads = q_in.reshape(row_count, local_key_value, group_width, HEAD_SIZE)
    grad_heads = d_in.reshape(row_count, local_key_value, group_width, HEAD_SIZE)
    key_value = jnp.stack(
        (
            k_in.reshape(row_count, local_key_value, HEAD_SIZE),
            v_in.reshape(row_count, local_key_value, HEAD_SIZE),
        ),
        axis=1,
    )
    slot_count = stretch_ids.shape[0]
    ctx_rank = lax.axis_index("ctx")

    def positions(start, count):
        rank_index = start + jnp.arange(count, dtype=jnp.int32)
        slots = rank_index // stretch_rows
        match = slots[:, None] == jnp.arange(slot_count, dtype=jnp.int32)[None, :]
        picked = jnp.sum(jnp.where(match, stretch_ids[None, :], 0), axis=1)
        return picked * stretch_rows + rank_index % stretch_rows

    query_pos = positions(ctx_rank * row_count, row_count)

    def low_slot(rank):
        pair = lax.dynamic_slice_in_dim(stretch_ids, 2 * rank, 2)
        return (jnp.where(pair[0] < pair[1], 0, 1).astype(jnp.int32), jnp.minimum(pair[0], pair[1]))

    own_low, own_stretch = low_slot(ctx_rank)

    def tiles(turn):
        if turn == 0:
            return (
                ctx_rank,
                [(own_low, own_low), (1 - own_low, own_low), (1 - own_low, 1 - own_low)],
            )
        source = (ctx_rank - turn) % ctx_devices
        source_low, source_stretch = low_slot(source)
        earlier = own_stretch > source_stretch
        extra_query = jnp.where(earlier, own_low, 1 - own_low)
        extra_key = jnp.where(earlier, source_low, 1 - source_low)
        return (source, [(1 - own_low, source_low), (extra_query, extra_key)])

    def quarter(piece, source, query_slot, key_slot):
        query_start = query_slot * stretch_rows
        key_start = key_slot * stretch_rows
        q_part = lax.dynamic_slice_in_dim(query_heads, query_start, stretch_rows, 0)
        k_part = lax.dynamic_slice_in_dim(piece, key_start, stretch_rows, 0)
        logits = (
            jnp.einsum("rkgd,nkd->kgrn", q_part, k_part[:, 0], preferred_element_type=jnp.float32)
            * scale
        )
        q_pos = lax.dynamic_slice_in_dim(query_pos, query_start, stretch_rows, 0)
        k_pos = positions(source * row_count + key_start, stretch_rows)
        visible = q_pos[:, None] >= k_pos[None, :]
        return (logits, visible, q_part, k_part, query_start, key_start)

    blocks = [key_value]
    for turn in range(1, WINDOW):
        blocks.append(from_behind(blocks[-1], "ctx", 1))
    run_max = jnp.full((local_key_value, group_width, row_count), -1e30, jnp.float32)
    run_total = jnp.zeros((local_key_value, group_width, row_count), jnp.float32)
    run_out = jnp.zeros((local_key_value, group_width, row_count, HEAD_SIZE), jnp.float32)
    for turn in range(WINDOW):
        source, pairs = tiles(turn)
        for query_slot, key_slot in pairs:
            logits, visible, q_part, k_part, query_start, key_start = quarter(
                blocks[turn], source, query_slot, key_slot
            )
            old_max = lax.dynamic_slice_in_dim(run_max, query_start, stretch_rows, 2)
            old_total = lax.dynamic_slice_in_dim(run_total, query_start, stretch_rows, 2)
            old_out = lax.dynamic_slice_in_dim(run_out, query_start, stretch_rows, 2)
            new_max = jnp.maximum(old_max, jnp.max(jnp.where(visible, logits, -1e30), axis=-1))
            weights = jnp.where(visible, jnp.exp(logits - new_max[..., None]), 0.0)
            factor = jnp.exp(old_max - new_max)
            new_total = factor * old_total + jnp.sum(weights, axis=-1)
            new_out = factor[..., None] * old_out + jnp.einsum(
                "kgrn,nkd->kgrd",
                weights.astype(jnp.bfloat16),
                k_part[:, 1],
                preferred_element_type=jnp.float32,
            )
            run_max = lax.dynamic_update_slice_in_dim(run_max, new_max, query_start, 2)
            run_total = lax.dynamic_update_slice_in_dim(run_total, new_total, query_start, 2)
            run_out = lax.dynamic_update_slice_in_dim(run_out, new_out, query_start, 2)
    log_total = run_max + jnp.log(run_total)
    attn_out = run_out / run_total[..., None]
    row_dot = jnp.einsum(
        "rkgd,kgrd->kgr", grad_heads.astype(jnp.float32), attn_out, precision=lax.Precision.HIGHEST
    )
    query_grads = jnp.zeros((row_count, local_key_value, group_width, HEAD_SIZE), jnp.float32)
    carried = None
    kv_grads = None
    for turn in range(WINDOW):
        source, pairs = tiles(turn)
        block_grads = jnp.zeros((row_count, 2, local_key_value, HEAD_SIZE), jnp.float32)
        for query_slot, key_slot in pairs:
            logits, visible, q_part, k_part, query_start, key_start = quarter(
                blocks[turn], source, query_slot, key_slot
            )
            g_part = lax.dynamic_slice_in_dim(grad_heads, query_start, stretch_rows, 0)
            lse_part = lax.dynamic_slice_in_dim(log_total, query_start, stretch_rows, 2)
            dot_part = lax.dynamic_slice_in_dim(row_dot, query_start, stretch_rows, 2)
            probs = jnp.where(visible, jnp.exp(logits - lse_part[..., None]), 0.0)
            probs_low = probs.astype(jnp.bfloat16)
            value_gradient = jnp.einsum(
                "kgrn,rkgd->nkd", probs_low, g_part, preferred_element_type=jnp.float32
            )
            grad_p = jnp.einsum(
                "rkgd,nkd->kgrn", g_part, k_part[:, 1], preferred_element_type=jnp.float32
            )
            grad_s = (probs * (grad_p - dot_part[..., None]) * scale).astype(jnp.bfloat16)
            grad_q = jnp.einsum(
                "kgrn,nkd->rkgd", grad_s, k_part[:, 0], preferred_element_type=jnp.float32
            )
            key_gradient = jnp.einsum(
                "kgrn,rkgd->nkd", grad_s, q_part, preferred_element_type=jnp.float32
            )
            query_grads = add_rows(query_grads, grad_q, query_start, 0)
            block_grads = add_rows(
                block_grads, jnp.stack((key_gradient, value_gradient), axis=1), key_start, 0
            )
        if turn == 0:
            carried = block_grads
        else:
            carried = (
                from_behind(carried.astype(jnp.bfloat16), "ctx", 1).astype(carried.dtype)
                + block_grads
            )
    kv_grads = from_behind(carried.astype(jnp.bfloat16), "ctx", -(WINDOW - 1)).astype(carried.dtype)
    query_send = query_grads.astype(jnp.bfloat16).reshape(
        row_count, 1, local_key_value * group_width * HEAD_SIZE
    )
    key_send = (
        kv_grads[:, 0].astype(jnp.bfloat16).reshape(row_count, 1, local_key_value * HEAD_SIZE)
    )
    value_send = (
        kv_grads[:, 1].astype(jnp.bfloat16).reshape(row_count, 1, local_key_value * HEAD_SIZE)
    )
    back_query, returned_key, returned_value = (
        lax.all_to_all(query_send, "head", split_axis=0, concat_axis=1, tiled=True),
        lax.all_to_all(key_send, "head", split_axis=0, concat_axis=1, tiled=True),
        lax.all_to_all(value_send, "head", split_axis=0, concat_axis=1, tiled=True),
    )
    return (
        back_query.reshape(token_count_local, QUERY_HEAD_COUNT * HEAD_SIZE),
        returned_key.reshape(token_count_local, KEY_VALUE_HEADS * HEAD_SIZE),
        returned_value.reshape(token_count_local, KEY_VALUE_HEADS * HEAD_SIZE),
    )


def solution(mesh):
    return jax.shard_map(
        body,
        mesh=mesh,
        in_specs=(
            P(("ctx", "head"), None),
            P(("ctx", "head"), None),
            P(("ctx", "head"), None),
            P(("ctx", "head"), None),
            P(),
        ),
        out_specs=(P(("ctx", "head"), None), P(("ctx", "head"), None), P(("ctx", "head"), None)),
        check_vma=False,
    )
```

profile of v0, /device:TPU:2, one launch (start us, length us, event | category | flops | bytes accessed | tf_op | source)
XLA Modules:
  0.0 273.9 jit_solution(4917157756322870769)
XLA Ops:
  2.4 5.0 %all-to-all-start = ((bf16[128,4,256]{2,0,1:T(8,128)(2,1)}), bf16[128,4,256]{2,0,1:T(8,128)(2,1)S(1)}, u32[]{:S(2)}, u32[]{:S(2)}) async-start(bf16[128,4,256]{2,0,1:T(8,128)(2,1)} %bitcast.718), calls=%async_computation | async-start | bytes 524288 | tf_op jit(solution)/shard_map/all_to_all | solution.py:35
  22.8 5.1 %all-to-all-start.1 = ((bf16[128,4,256]{2,0,1:T(8,128)(2,1)}), bf16[128,4,256]{2,0,1:T(8,128)(2,1)S(1)}, u32[]{:S(2)}, u32[]{:S(2)}) async-start(bf16[128,4,256]{2,0,1:T(8,128)(2,1)} %bitcast.717), calls=%async_computation.1 | async-start | bytes 524288 | tf_op jit(solution)/shard_map/all_to_all | solution.py:36
  29.1 7.1 %all-to-all-done.1 = bf16[128,4,256]{2,0,1:T(8,128)(2,1)S(1)} async-done(((bf16[128,4,256]{2,0,1:T(8,128)(2,1)}), bf16[128,4,256]{2,0,1:T(8,128)(2,1)S(1)}, u32[]{:S(2)}, u32[]{:S(2)}) %all-to-all-start.1) | async-done | bytes 262176 | tf_op jit(solution)/shard_map/all_to_all | solution.py:36
  36.2 3.5 %all-to-all-start.3 = ((bf16[128,4,1024]{2,0,1:T(8,128)(2,1)}), bf16[128,4,1024]{2,0,1:T(8,128)(2,1)S(1)}, u32[]{:S(2)}, u32[]{:S(2)}) async-start(bf16[128,4,1024]{2,0,1:T(8,128)(2,1)} %bitcast.715), calls=%async_computation.3 | async-start | bytes 2097152 | tf_op jit(solution)/shard_map/all_to_all | solution.py:37
  42.8 21.1 %all-to-all-done.3 = bf16[128,4,1024]{2,0,1:T(8,128)(2,1)S(1)} async-done(((bf16[128,4,1024]{2,0,1:T(8,128)(2,1)}), bf16[128,4,1024]{2,0,1:T(8,128)(2,1)S(1)}, u32[]{:S(2)}, u32[]{:S(2)}) %all-to-all-start.3) | async-done | bytes 1048608 | tf_op jit(solution)/shard_map/all_to_all | solution.py:37
  63.9 3.5 %all-to-all-start.2 = ((bf16[128,4,1024]{2,0,1:T(8,128)(2,1)}), bf16[128,4,1024]{2,0,1:T(8,128)(2,1)S(1)}, u32[]{:S(2)}, u32[]{:S(2)}) async-start(bf16[128,4,1024]{2,0,1:T(8,128)(2,1)} %bitcast.716), calls=%async_computation.2 | async-start | bytes 2097152 | tf_op jit(solution)/shard_map/all_to_all | solution.py:34
  69.2 7.0 %collective-permute-done = bf16[512,2,2,128]{3,0,2,1:T(8,128)(2,1)S(1)} collective-permute-done((bf16[512,2,2,128]{3,0,2,1:T(8,128)(2,1)S(1)}, bf16[512,2,2,128]{3,0,2,1:T(8,128)(2,1)S(1)}, u32[]{:S(2)}, u32[]{:S(2)}) %collective-permute-start) | collective-permute-done | bytes 524320 | tf_op jit(solution)/shard_map/ppermute | solution.py:14
  78.1 6.9 %collective-permute-done.1 = bf16[512,2,2,128]{3,0,2,1:T(8,128)(2,1)} collective-permute-done((bf16[512,2,2,128]{3,0,2,1:T(8,128)(2,1)S(1)}, bf16[512,2,2,128]{3,0,2,1:T(8,128)(2,1)}, u32[]{:S(2)}, u32[]{:S(2)}) %collective-permute-start.1) | collective-permute-done | bytes 524320 | tf_op jit(solution)/shard_map/ppermute | solution.py:14
  85.8 6.8 %all-to-all-done.2 = bf16[128,4,1024]{2,0,1:T(8,128)(2,1)S(1)} async-done(((bf16[128,4,1024]{2,0,1:T(8,128)(2,1)}), bf16[128,4,1024]{2,0,1:T(8,128)(2,1)S(1)}, u32[]{:S(2)}, u32[]{:S(2)}) %all-to-all-start.2) | async-done | bytes 1048608 | tf_op jit(solution)/shard_map/all_to_all | solution.py:34
  95.6 3.0 %constant_dynamic-slice_fusion.1 = (bf16[256,2,4,128]{3,2,1,0:T(4,128)(2,1)}, bf16[256,2,4,128]{3,2,1,0:T(4,128)(2,1)}, bf16[256,2,4,128]{3,2,1,0:T(4,128)(2,1)}...) fusion(bf16[512,2,4,128]{3,2,1,0:T(4,128)(2,1)S(1)} %reshape.45, ...), kind=kLoop, calls=%fused_computation.350 | loop fusion | bytes 10485780 | tf_op jit(solution)/shard_map/dynamic_slice | solution.py:138
  134.1 3.1 %fusion.23 = bf16[2,4,256,256]{2,3,1,0:T(8,128)(2,1)} fusion(f32[2,256,256,4]{2,1,3,0:T(8,128)S(1)} %copy-done.15, f32[2,4,256]{2,1,0:T(4,128)S(1)} %copy.629, f32[2,4,256]{2,1,0:T(4,128)} %copy-done.80, pred[256,256]{0,1:T(8,128)(4,1)S(1)} %get-tuple-element.83, bf16[512,2,2,128]{3,0,2,1:T(8,128)(2,1)} %copy-done.45, s32[]{:T(128)S(6)} %select_n.566, ...), kind=kOutput, calls=%fused_computation.31 | convolution fusion | flops 137887744 | bytes 3883016 | tf_op jit(solution)/shard_map/rkgd,nkd->kgrn/dot_general | solution.py:146
  137.2 2.9 %fusion.20 = bf16[2,4,256,256]{2,3,1,0:T(8,128)(2,1)} fusion(f32[2,256,256,4]{2,1,3,0:T(8,128)S(1)} %copy-done.17, f32[2,4,256]{2,1,0:T(4,128)S(1)} %copy.629, f32[2,4,256]{2,1,0:T(4,128)S(1)} %copy-done.81, pred[256,256]{0,1:T(8,128)(4,1)S(1)} %get-tuple-element.80, bf16[512,2,2,128]{3,0,2,1:T(8,128)(2,1)} %copy-done.45, s32[]{:T(128)S(6)} %select_n.574, ...), kind=kOutput, calls=%fused_computation.27 | convolution fusion | flops 137887744 | bytes 3883016 | tf_op jit(solution)/shard_map/rkgd,nkd->kgrn/dot_general | solution.py:146
  144.1 2.5 convolution_bitcast_fusion.25
  192.9 3.3 %reduce.2 = bf16[512,1024]{0,1:T(8,128)(2,1)} reduce(bf16[512,1,1024]{0,2,1:T(8,128)(2,1)} %bitcast.722, bf16[]{:T(256)} %broadcast.870), dimensions={1}, to_apply=%copy.452.reduce_sub_computation | reduce | bytes 2097154 | tf_op jit(solution)/shard_map/reshape | solution.py:168
  198.5 3.7 %reshape.509 = bf16[4,2,65536]{2,1,0:T(2,128)(2,1)} reshape(bf16[512,1024]{1,0:T(8,128)(2,1)} %copy.741) | data formatting | bytes 2097152
  202.2 4.6 %all-to-all-start.4 = ((bf16[4,2,65536]{2,1,0:T(2,128)(2,1)}), bf16[4,2,65536]{2,1,0:T(2,128)(2,1)}, u32[]{:S(2)}, u32[]{:S(2)}) async-start(bf16[4,2,65536]{2,1,0:T(2,128)(2,1)} %reshape.509), calls=%async_computation.4 | async-start | bytes 2097152 | tf_op jit(solution)/shard_map/all_to_all | solution.py:178
  214.1 5.9 %collective-permute-done.4 = bf16[512,2,2,128]{0,3,2,1:T(8,128)(2,1)S(1)} collective-permute-done((bf16[512,2,2,128]{0,3,2,1:T(8,128)(2,1)S(1)}, bf16[512,2,2,128]{0,3,2,1:T(8,128)(2,1)S(1)}, u32[]{:S(2)}, u32[]{:S(2)}) %collective-permute-start.4) | collective-permute-done | bytes 524320 | tf_op jit(solution)/shard_map/ppermute | solution.py:14
  221.2 7.6 %collective-permute-done.5 = bf16[512,2,2,128]{0,3,2,1:T(8,128)(2,1)S(1)} collective-permute-done((bf16[512,2,2,128]{0,3,2,1:T(8,128)(2,1)S(1)}, bf16[512,2,2,128]{0,3,2,1:T(8,128)(2,1)S(1)}, u32[]{:S(2)}, u32[]{:S(2)}) %collective-permute-start.5) | collective-permute-done | bytes 524320 | tf_op jit(solution)/shard_map/ppermute | solution.py:14
  229.2 12.3 %collective-permute-done.6 = bf16[512,2,2,128]{0,3,2,1:T(8,128)(2,1)S(1)} collective-permute-done((bf16[512,2,2,128]{0,3,2,1:T(8,128)(2,1)S(1)}, bf16[512,2,2,128]{0,3,2,1:T(8,128)(2,1)S(1)}, u32[]{:S(2)}, u32[]{:S(2)}) %collective-permute-start.6) | collective-permute-done | bytes 524320 | tf_op jit(solution)/shard_map/ppermute | solution.py:14
  243.3 5.1 %all-to-all-start.6 = ((bf16[4,2,16384]{2,1,0:T(2,128)(2,1)}), bf16[4,2,16384]{2,1,0:T(2,128)(2,1)S(1)}, u32[]{:S(2)}, u32[]{:S(2)}) async-start(bf16[4,2,16384]{2,1,0:T(2,128)(2,1)} %reshape.513), calls=%async_computation.6 | async-start | bytes 524288 | tf_op jit(solution)/shard_map/all_to_all | solution.py:180
  250.0 7.2 %all-to-all-done.6 = bf16[4,2,16384]{2,1,0:T(2,128)(2,1)S(1)} async-done(((bf16[4,2,16384]{2,1,0:T(2,128)(2,1)}), bf16[4,2,16384]{2,1,0:T(2,128)(2,1)S(1)}, u32[]{:S(2)}, u32[]{:S(2)}) %all-to-all-start.6) | async-done | bytes 262176 | tf_op jit(solution)/shard_map/all_to_all | solution.py:180
  257.2 4.1 %all-to-all-start.5 = ((bf16[4,2,16384]{2,1,0:T(2,128)(2,1)}), bf16[4,2,16384]{2,1,0:T(2,128)(2,1)}, u32[]{:S(2)}, u32[]{:S(2)}) async-start(bf16[4,2,16384]{2,1,0:T(2,128)(2,1)} %reshape.511), calls=%async_computation.5 | async-start | bytes 524288 | tf_op jit(solution)/shard_map/all_to_all | solution.py:179
  261.3 2.6 reshape.510
  267.7 3.7 %all-to-all-done.5 = bf16[4,2,16384]{2,1,0:T(2,128)(2,1)} async-done(((bf16[4,2,16384]{2,1,0:T(2,128)(2,1)}), bf16[4,2,16384]{2,1,0:T(2,128)(2,1)}, u32[]{:S(2)}, u32[]{:S(2)}) %all-to-all-start.5) | async-done | bytes 262176 | tf_op jit(solution)/shard_map/all_to_all | solution.py:179
  (359 shorter events, 123.2 us)
Async XLA Ops:
  0.6 27.3 %copy-start.55 = (bf16[128,4096]{1,0:T(8,128)(2,1)S(1)}, bf16[128,4096]{1,0:T(8,128)(2,1)}, u32[]{:S(2)}) copy-start(bf16[128,4096]{1,0:T(8,128)(2,1)} %param.8) | copy-start | bytes 3145732
  2.4 26.6 %copy-start.79 = (s32[16]{0:T(128)S(1)}, s32[16]{0:T(128)}, u32[]{:S(2)}) copy-start(s32[16]{0:T(128)} %param.9) | copy-start | bytes 196
  2.4 20.4 %all-to-all-start = ((bf16[128,4,256]{2,0,1:T(8,128)(2,1)}), bf16[128,4,256]{2,0,1:T(8,128)(2,1)S(1)}, u32[]{:S(2)}, u32[]{:S(2)}) async-start(bf16[128,4,256]{2,0,1:T(8,128)(2,1)} %bitcast.718), calls=%async_computation | async-start | bytes 524288 | tf_op jit(solution)/shard_map/all_to_all | solution.py:35
  22.8 13.4 %all-to-all-start.1 = ((bf16[128,4,256]{2,0,1:T(8,128)(2,1)}), bf16[128,4,256]{2,0,1:T(8,128)(2,1)S(1)}, u32[]{:S(2)}, u32[]{:S(2)}) async-start(bf16[128,4,256]{2,0,1:T(8,128)(2,1)} %bitcast.717), calls=%async_computation.1 | async-start | bytes 524288 | tf_op jit(solution)/shard_map/all_to_all | solution.py:36
  28.0 11.9 %copy-start.56 = (bf16[128,4096]{1,0:T(8,128)(2,1)S(1)}, bf16[128,4096]{1,0:T(8,128)(2,1)}, u32[]{:S(2)}) copy-start(bf16[128,4096]{1,0:T(8,128)(2,1)} %param.5) | copy-start | bytes 3145732
  36.2 27.7 %all-to-all-start.3 = ((bf16[128,4,1024]{2,0,1:T(8,128)(2,1)}), bf16[128,4,1024]{2,0,1:T(8,128)(2,1)S(1)}, u32[]{:S(2)}, u32[]{:S(2)}) async-start(bf16[128,4,1024]{2,0,1:T(8,128)(2,1)} %bitcast.715), calls=%async_computation.3 | async-start | bytes 2097152 | tf_op jit(solution)/shard_map/all_to_all | solution.py:37
  63.9 28.7 %all-to-all-start.2 = ((bf16[128,4,1024]{2,0,1:T(8,128)(2,1)}), bf16[128,4,1024]{2,0,1:T(8,128)(2,1)S(1)}, u32[]{:S(2)}, u32[]{:S(2)}) async-start(bf16[128,4,1024]{2,0,1:T(8,128)(2,1)} %bitcast.716), calls=%async_computation.2 | async-start | bytes 2097152 | tf_op jit(solution)/shard_map/all_to_all | solution.py:34
  67.6 17.4 %copy-start.45 = (bf16[512,2,2,128]{3,0,2,1:T(8,128)(2,1)}, bf16[512,2,2,128]{3,0,2,1:T(8,128)(2,1)S(1)}, u32[]{:S(2)}) copy-start(bf16[512,2,2,128]{3,0,2,1:T(8,128)(2,1)S(1)} %copy_dynamic-update-slice_fusion) | copy-start | bytes 1572868
  67.6 8.7 %collective-permute-start = (bf16[512,2,2,128]{3,0,2,1:T(8,128)(2,1)S(1)}, bf16[512,2,2,128]{3,0,2,1:T(8,128)(2,1)S(1)}, u32[]{:S(2)}, u32[]{:S(2)}) collective-permute-start(bf16[512,2,2,128]{3,0,2,1:T(8,128)(2,1)S(1)} %copy_dynamic-update-slice_fusion), channel_id=1, source_target_pairs={{0,4},{4,8},{8,12},{12,16},{16,20},{20,24},{24,28},{28,0},{1,5},{5... | collective-permute-start | bytes 1572872 | tf_op jit(solution)/shard_map/ppermute | solution.py:14
  76.3 8.7 %collective-permute-start.1 = (bf16[512,2,2,128]{3,0,2,1:T(8,128)(2,1)S(1)}, bf16[512,2,2,128]{3,0,2,1:T(8,128)(2,1)}, u32[]{:S(2)}, u32[]{:S(2)}) collective-permute-start(bf16[512,2,2,128]{3,0,2,1:T(8,128)(2,1)S(1)} %collective-permute-done), channel_id=1, source_target_pairs={{0,4},{4,8},{8,12},{12,16},{16,20},{20,24},{24,28},{28,0},{1,5},{5... | collective-permute-start | bytes 1572872 | tf_op jit(solution)/shard_map/ppermute | solution.py:14
  85.0 32.6 %collective-permute-start.2 = (bf16[512,2,2,128]{3,0,2,1:T(8,128)(2,1)}, bf16[512,2,2,128]{3,0,2,1:T(8,128)(2,1)}, u32[]{:S(2)}, u32[]{:S(2)}) collective-permute-start(bf16[512,2,2,128]{3,0,2,1:T(8,128)(2,1)} %collective-permute-done.1), channel_id=1, source_target_pairs={{0,4},{4,8},{8,12},{12,16},{16,20},{20,24},{24,28},{28,0},{1,5},{5... | collective-permute-start | bytes 1572872 | tf_op jit(solution)/shard_map/ppermute | solution.py:14
  98.6 25.0 %copy-start.65 = (bf16[256,2,4,128]{3,2,1,0:T(4,128)(2,1)}, bf16[256,2,4,128]{3,2,1,0:T(4,128)(2,1)S(1)}, u32[]{:S(2)}) copy-start(bf16[256,2,4,128]{3,2,1,0:T(4,128)(2,1)S(1)} %get-tuple-element.52) | copy-start | bytes 1572868
  99.1 9.8 %copy-start.18 = (f32[2,256,256,4]{2,1,3,0:T(8,128)}, f32[2,256,256,4]{2,1,3,0:T(8,128)S(1)}, u32[]{:S(2)}) copy-start(f32[2,256,256,4]{2,1,3,0:T(8,128)S(1)} %get-tuple-element.98) | copy-start | bytes 6291460
  100.2 22.1 %copy-start.14 = (f32[2,256,256,4]{2,1,3,0:T(8,128)}, f32[2,256,256,4]{2,1,3,0:T(8,128)S(1)}, u32[]{:S(2)}) copy-start(f32[2,256,256,4]{2,1,3,0:T(8,128)S(1)} %get-tuple-element.100) | copy-start | bytes 6291460
  100.7 22.9 %copy-start.16 = (f32[2,256,256,4]{2,1,3,0:T(8,128)}, f32[2,256,256,4]{2,1,3,0:T(8,128)S(1)}, u32[]{:S(2)}) copy-start(f32[2,256,256,4]{2,1,3,0:T(8,128)S(1)} %get-tuple-element.102) | copy-start | bytes 6291460
  102.6 10.3 %copy-start.7 = (f32[2,256,256,4]{2,1,3,0:T(8,128)}, f32[2,256,256,4]{2,1,3,0:T(8,128)S(1)}, u32[]{:S(2)}) copy-start(f32[2,256,256,4]{2,1,3,0:T(8,128)S(1)} %get-tuple-element.106) | copy-start | bytes 6291460
  105.9 9.9 %copy-start.12 = (f32[2,256,256,4]{2,1,3,0:T(8,128)}, f32[2,256,256,4]{2,1,3,0:T(8,128)S(1)}, u32[]{:S(2)}) copy-start(f32[2,256,256,4]{2,1,3,0:T(8,128)S(1)} %get-tuple-element.110) | copy-start | bytes 6291460
  152.6 57.4 %collective-permute-start.3 = (bf16[512,2,2,128]{0,3,2,1:T(8,128)(2,1)}, bf16[512,2,2,128]{0,3,2,1:T(8,128)(2,1)}, u32[]{:S(2)}, u32[]{:S(2)}) collective-permute-start(bf16[512,2,2,128]{0,3,2,1:T(8,128)(2,1)} %convert_element_type.151), channel_id=1, source_target_pairs={{0,4},{4,8},{8,12},{12,16},{16,20},{20,24},{24,28},{28,0},{1,5},{5... | collective-permute-start | bytes 1572872 | tf_op jit(solution)/shard_map/ppermute | solution.py:14
  202.2 41.1 %all-to-all-start.4 = ((bf16[4,2,65536]{2,1,0:T(2,128)(2,1)}), bf16[4,2,65536]{2,1,0:T(2,128)(2,1)}, u32[]{:S(2)}, u32[]{:S(2)}) async-start(bf16[4,2,65536]{2,1,0:T(2,128)(2,1)} %reshape.509), calls=%async_computation.4 | async-start | bytes 2097152 | tf_op jit(solution)/shard_map/all_to_all | solution.py:178
  211.4 8.7 %collective-permute-start.4 = (bf16[512,2,2,128]{0,3,2,1:T(8,128)(2,1)S(1)}, bf16[512,2,2,128]{0,3,2,1:T(8,128)(2,1)S(1)}, u32[]{:S(2)}, u32[]{:S(2)}) collective-permute-start(bf16[512,2,2,128]{0,3,2,1:T(8,128)(2,1)S(1)} %add_convert_fusion.2), channel_id=1, source_target_pairs={{0,4},{4,8},{8,12},{12,16},{16,20},{20,24},{24,28},{28,0},{1,5},{5... | collective-permute-start | bytes 1572872 | tf_op jit(solution)/shard_map/ppermute | solution.py:14
  220.2 8.7 %collective-permute-start.5 = (bf16[512,2,2,128]{0,3,2,1:T(8,128)(2,1)S(1)}, bf16[512,2,2,128]{0,3,2,1:T(8,128)(2,1)S(1)}, u32[]{:S(2)}, u32[]{:S(2)}) collective-permute-start(bf16[512,2,2,128]{0,3,2,1:T(8,128)(2,1)S(1)} %add_convert_fusion.1), channel_id=1, source_target_pairs={{0,4},{4,8},{8,12},{12,16},{16,20},{20,24},{24,28},{28,0},{1,5},{5... | collective-permute-start | bytes 1572872 | tf_op jit(solution)/shard_map/ppermute | solution.py:14
  229.0 12.5 %collective-permute-start.6 = (bf16[512,2,2,128]{0,3,2,1:T(8,128)(2,1)S(1)}, bf16[512,2,2,128]{0,3,2,1:T(8,128)(2,1)S(1)}, u32[]{:S(2)}, u32[]{:S(2)}) collective-permute-start(bf16[512,2,2,128]{0,3,2,1:T(8,128)(2,1)S(1)} %add_convert_fusion), channel_id=1, source_target_pairs={{0,20},{4,24},{8,28},{12,0},{16,4},{20,8},{24,12},{28,16},{1,21},{... | collective-permute-start | bytes 1572872 | tf_op jit(solution)/shard_map/ppermute | solution.py:14
  243.3 14.0 %all-to-all-start.6 = ((bf16[4,2,16384]{2,1,0:T(2,128)(2,1)}), bf16[4,2,16384]{2,1,0:T(2,128)(2,1)S(1)}, u32[]{:S(2)}, u32[]{:S(2)}) async-start(bf16[4,2,16384]{2,1,0:T(2,128)(2,1)} %reshape.513), calls=%async_computation.6 | async-start | bytes 524288 | tf_op jit(solution)/shard_map/all_to_all | solution.py:180
  257.2 14.2 %all-to-all-start.5 = ((bf16[4,2,16384]{2,1,0:T(2,128)(2,1)}), bf16[4,2,16384]{2,1,0:T(2,128)(2,1)}, u32[]{:S(2)}, u32[]{:S(2)}) async-start(bf16[4,2,16384]{2,1,0:T(2,128)(2,1)} %reshape.511), calls=%async_computation.5 | async-start | bytes 524288 | tf_op jit(solution)/shard_map/all_to_all | solution.py:179
  (77 other events, 205.2 us)
where the time goes:
time: 279 us; the launch traced here: 274 us
  waiting for transfers between devices  85.8 us (31%)
  matrix products  67.7 us (24%)
  local copies, waits for them, and re-layouts  51.2 us (18%)
  starting transfers between devices  32.9 us (12%)
  other arithmetic  23.4 us (8%)
  between operations  12.9 us (5%)
    ppermute x7, waiting for transfers between devices, from_behind(): lax.ppermute(shard, axis, [(i, (i + by) % devices) for i in range(devices)])  39.8 us
    unnamed x203, local copies, waits for them, and re-layouts  32.2 us
    all_to_all x1, waiting for transfers between devices, body(): lax.all_to_all(split_heads(d_out), 'head', split_axis=1, concat_axis=0, t...  21.1 us
    dot_general x9, matrix products, body(): jnp.einsum('rkgd,nkd->kgrn', g_part, k_part[:, 1], preferred_element_type...  18.6 us
    dot_general x9, matrix products, body(): jnp.einsum('kgrn,rkgd->nkd', probs_low, g_part, preferred_element_type=jn...  13.9 us
    dot_general x9, matrix products, body(): jnp.einsum('kgrn,nkd->kgrd', weights.astype(jnp.bfloat16), k_part[:, 1],...  12.2 us
    dot_general x9, matrix products, quarter(): jnp.einsum('rkgd,nkd->kgrn', q_part, k_part[:, 0], preferred_element_type...  8.56 us
    dot_general x9, matrix products, body(): jnp.einsum('kgrn,nkd->rkgd', grad_s, k_part[:, 0], preferred_element_type...  7.31 us
  transfers between devices with their start and end apart: 14, of which 10 were waited for; matrix products, arithmetic and copies ran while one was open for 34% of the time, Pallas kernels for 0%

commit v1 on v0

v1 whole, which is shorter than its diff:
```python
import jax
import jax.numpy as jnp
from jax import lax
from jax.experimental import pallas as pl
from jax.experimental.pallas import tpu as pltpu
from jax.sharding import PartitionSpec as P

QUERY_HEAD_COUNT = 32
KEY_VALUE_HEADS = 8
HEAD_SIZE = 128
WINDOW = 4
SCALE = HEAD_SIZE ** (-0.5)
LOG2_E = 1.4426950408889634
NT = (((1,), (1,)), ((), ()))
NN = (((1,), (0,)), ((), ()))
TN = (((0,), (0,)), ((), ()))


def dot(a, b, dims):
    return lax.dot_general(a, b, dims, preferred_element_type=jnp.float32)


def fold(x, op):
    return op(x.reshape(x.shape[0] // 8, 8, x.shape[1]), axis=0)


def attention_kernel(
    ranks, splits, heads, rows,
    ids_ref, q_ref, g_ref, kv_ref, dq_ref, dkv_ref,
    tile_ref, st_ref, dp_ref, dqt_ref, dk_ref, dv_ref,
):
    rank = pl.program_id(0)
    z = ids_ref[2 * ranks]
    half = splits // 2
    slot = z // half
    own = ids_ref[2 * rank + slot]

    @pl.when(rank == 0)
    def _():
        dk_ref[...] = jnp.zeros_like(dk_ref)
        dv_ref[...] = jnp.zeros_like(dv_ref)

    count = jnp.int32(0)
    for back in range(WINDOW):
        key_rank = lax.rem(rank - back + ranks, ranks)
        for key_slot in range(2):
            tile_ref[count] = key_rank * 2 + key_slot
            count = count + jnp.where(ids_ref[2 * key_rank + key_slot] < own, 1, 0)

    def stack(ref):
        return jnp.concatenate(
            [ref[0, :, h * HEAD_SIZE : (h + 1) * HEAD_SIZE] for h in range(heads)], axis=0
        )

    qs = stack(q_ref)
    gs = stack(g_ref)

    def keys(which, key_rank, key_slot):
        return jnp.concatenate(
            [kv_ref[key_slot * half + i, which, key_rank] for i in range(half)], axis=0
        )

    def place(i):
        t = tile_ref[i]
        return t // 2, lax.rem(t, 2)

    width = heads * rows
    key_pos = lax.broadcasted_iota(jnp.int32, (half * rows, width), 0)
    row_pos = lax.rem(lax.broadcasted_iota(jnp.int32, (half * rows, width), 1), rows)
    row_pos = row_pos + lax.rem(z, half) * rows

    s_own = jnp.where(key_pos <= row_pos, dot(keys(0, rank, slot), qs, NT), -1e30)
    st_ref[0] = s_own

    def scores(i, top):
        s = dot(keys(0, *place(i)), qs, NT)
        st_ref[i + 1] = s
        return jnp.maximum(top, fold(s, jnp.max))

    top = lax.fori_loop(0, count, scores, fold(s_own, jnp.max))
    top = jnp.max(top, axis=0, keepdims=True) * (SCALE * LOG2_E)

    def weights(i, total):
        p = jnp.exp2(st_ref[i] * (SCALE * LOG2_E) - top)
        st_ref[i] = p
        return total + fold(p, jnp.sum)

    total = lax.fori_loop(0, count + 1, weights, jnp.zeros((8, width), jnp.float32))
    inverse = 1.0 / jnp.sum(total, axis=0, keepdims=True)

    def add(ref, key_rank, key_slot, update):
        for i in range(half):
            ref[key_slot * half + i, key_rank] += update[i * rows : (i + 1) * rows]

    def values(i, key_rank, key_slot, delta):
        p = st_ref[i] * inverse
        st_ref[i] = p
        dp = dot(keys(1, key_rank, key_slot), gs, NT)
        dp_ref[i] = dp
        add(dv_ref, key_rank, key_slot, dot(p.astype(jnp.bfloat16), gs, NN))
        return delta + fold(p * dp, jnp.sum)

    delta = values(0, rank, slot, jnp.zeros((8, width), jnp.float32))
    delta = lax.fori_loop(0, count, lambda i, d: values(i + 1, *place(i), d), delta)
    delta = jnp.sum(delta, axis=0, keepdims=True)

    def grads(i, key_rank, key_slot):
        ds = (st_ref[i] * (dp_ref[i] - delta)).astype(jnp.bfloat16)
        add(dk_ref, key_rank, key_slot, dot(ds, qs, NN))
        return dot(keys(0, key_rank, key_slot), ds, TN)

    dqt_ref[...] = grads(0, rank, slot)

    def others(i, carry):
        dqt_ref[...] += grads(i + 1, *place(i))
        return carry

    lax.fori_loop(0, count, others, 0)
    dq = (dqt_ref[...] * SCALE).T.astype(jnp.bfloat16)
    for h in range(heads):
        dq_ref[0, :, h * HEAD_SIZE : (h + 1) * HEAD_SIZE] = dq[h * rows : (h + 1) * rows]

    @pl.when(rank == ranks - 1)
    def _():
        dkv_ref[:, 0] = (dk_ref[...] * SCALE).astype(jnp.bfloat16)
        dkv_ref[:, 1] = dv_ref[...].astype(jnp.bfloat16)


def attention(ids, q, g, kv):
    ranks, rows, width = q.shape
    splits = kv.shape[0]
    heads = width // HEAD_SIZE
    stretch = splits // 2 * rows
    tiles = 2 * WINDOW
    row_block = pl.BlockSpec((1, rows, width), lambda r: (r, 0, 0))
    whole = pl.BlockSpec(kv.shape, lambda r: (0, 0, 0, 0, 0), pipeline_mode=pl.Buffered(1))
    flops = 10 * ranks * 5 * stretch * heads * rows * HEAD_SIZE

    def kernel(*refs):
        attention_kernel(ranks, splits, heads, rows, *refs)

    return pl.pallas_call(
        kernel,
        grid=(ranks,),
        in_specs=[pl.BlockSpec(memory_space=pltpu.SMEM), row_block, row_block, whole],
        out_specs=(row_block, whole),
        out_shape=(
            jax.ShapeDtypeStruct(q.shape, jnp.bfloat16),
            jax.ShapeDtypeStruct(kv.shape, jnp.bfloat16),
        ),
        scratch_shapes=[
            pltpu.SMEM((tiles + 1,), jnp.int32),
            pltpu.VMEM((tiles + 1, stretch, heads * rows), jnp.float32),
            pltpu.VMEM((tiles + 1, stretch, heads * rows), jnp.float32),
            pltpu.VMEM((HEAD_SIZE, heads * rows), jnp.float32),
            pltpu.VMEM((splits, ranks, rows, HEAD_SIZE), jnp.float32),
            pltpu.VMEM((splits, ranks, rows, HEAD_SIZE), jnp.float32),
        ],
        compiler_params=pltpu.CompilerParams(vmem_limit_bytes=60 * 1024 * 1024),
        cost_estimate=pl.CostEstimate(flops=flops, bytes_accessed=10 * q.size, transcendentals=0),
    )(ids, q, g, kv)


def body(query, key, value, d_out, stretch_ids):
    rows = query.shape[0]
    ranks = lax.axis_size("ctx")
    copies = ranks // KEY_VALUE_HEADS
    z = lax.axis_index("head")

    def by_device(array):
        return array.reshape(rows, ranks, array.shape[1] // ranks).swapaxes(0, 1)

    def to_heads(array):
        return lax.all_to_all(array, "ctx", split_axis=0, concat_axis=0, tiled=True)

    def by_key_head(array):
        split = array.reshape(rows, KEY_VALUE_HEADS, HEAD_SIZE).swapaxes(0, 1)
        return jnp.repeat(split, copies, axis=0)

    kv = to_heads(jnp.stack((by_key_head(key), by_key_head(value)), axis=1)).swapaxes(0, 1)
    kv = lax.all_gather(kv, "head", axis=0, tiled=False)
    q = to_heads(by_device(query))
    g = to_heads(by_device(d_out))
    ids = jnp.concatenate((stretch_ids, z.astype(jnp.int32)[None]))
    dq, dkv = attention(ids, q, g, kv)
    dq = to_heads(dq).swapaxes(0, 1).reshape(rows, QUERY_HEAD_COUNT * HEAD_SIZE)
    dkv = lax.psum_scatter(dkv, "head", scatter_dimension=0, tiled=False)
    dkv = lax.all_to_all(dkv, "ctx", split_axis=1, concat_axis=1, tiled=True)
    if copies > 1:
        shape = (2, KEY_VALUE_HEADS, copies, rows, HEAD_SIZE)
        dkv = jnp.sum(dkv.reshape(shape).astype(jnp.float32), axis=2).astype(jnp.bfloat16)
    dkv = dkv.swapaxes(1, 2).reshape(2, rows, KEY_VALUE_HEADS * HEAD_SIZE)
    return dq, dkv[0], dkv[1]


def solution(mesh):
    spec = P(("ctx", "head"), None)
    return jax.shard_map(
        body,
        mesh=mesh,
        in_specs=(spec, spec, spec, spec, P()),
        out_specs=(spec, spec, spec),
        check_vma=False,
    )
```

time: 279 us -> 180 us (0.65)
  the two profiles are of different devices: /device:TPU:2 before, /device:TPU:0 now
where the time goes in v1:
time: 180 us; the launch traced here: 179 us
  waiting for transfers between devices  87.7 us (49%)
  Pallas kernels  33.6 us (19%)
  blocking collectives  14.8 us (8%)
  starting transfers between devices  14.5 us (8%)
  between operations  14.2 us (8%)
  local copies, waits for them, and re-layouts  13.2 us (7%)
    reduce_scatter x1, waiting for transfers between devices, body(): dkv = lax.psum_scatter(dkv, 'head', scatter_dimension=0, tiled=False)  46.2 us
    pallas_call x1, Pallas kernels, attention(): pl.pallas_call(kernel, grid=(ranks,), in_specs=[pl.BlockSpec(memory_space...  33.6 us
    all_to_all x3, waiting for transfers between devices, to_heads(): return lax.all_to_all(array, 'ctx', split_axis=0, concat_axis=0, tiled=True)  28 us
    all_to_all x1, blocking collectives, to_heads(): return lax.all_to_all(array, 'ctx', split_axis=0, concat_axis=0, tiled=True)  14.8 us
    all_to_all x3, starting transfers between devices, to_heads(): return lax.all_to_all(array, 'ctx', split_axis=0, concat_axis=0, tiled=True)  10.8 us
    all_to_all x1, waiting for transfers between devices, body(): dkv = lax.all_to_all(dkv, 'ctx', split_axis=1, concat_axis=1, tiled=True)  7.77 us
    unnamed x17, local copies, waits for them, and re-layouts  6.6 us
    all_gather x1, waiting for transfers between devices, body(): kv = lax.all_gather(kv, 'head', axis=0, tiled=False)  5.62 us
  transfers between devices with their start and end apart: 6, of which 5 were waited for; matrix products, arithmetic and copies ran while one was open for 5% of the time, Pallas kernels for 0%

profile of v1, /device:TPU:0, one launch (start us, length us, event | category | flops | bytes accessed | tf_op | source)
XLA Modules:
  0.0 178.7 jit_solution(16860926836590163210)
XLA Ops:
  7.2 1.1 copy.37
  8.3 1.1 copy.38
  9.8 14.8 %all_to_all.25 = bf16[8,2,128,128]{3,2,1,0:T(8,128)(2,1)S(1)} all-to-all(bf16[8,2,128,128]{3,2,1,0:T(8,128)(2,1)S(1)} %copy.39), channel_id=1, replica_groups=mesh['ctx'=8,'head'=4] {'ctx'}, dimensions={0} | all-to-all | bytes 1048576 | tf_op jit(solution)/shard_map/all_to_all | solution.py:174
  24.7 0.8 copy.40
  25.5 0.7 copy.33
  26.2 1.3 copy.34
  27.5 3.6 %all-to-all-start = ((bf16[8,128,512]{2,1,0:T(8,128)(2,1)}), bf16[8,128,512]{2,1,0:T(8,128)(2,1)S(1)}, u32[]{:S(2)}, u32[]{:S(2)}) async-start(bf16[8,128,512]{2,1,0:T(8,128)(2,1)} %bitcast.2), calls=%async_computation | async-start | bytes 2097152 | tf_op jit(solution)/shard_map/all_to_all | solution.py:174
  31.1 0.7 copy.35
  31.8 1.3 copy.36
  33.1 13.3 %all-to-all-done.refs_1_ = bf16[8,128,512]{2,1,0:T(8,128)(2,1)S(1)} async-done(((bf16[8,128,512]{2,1,0:T(8,128)(2,1)}), bf16[8,128,512]{2,1,0:T(8,128)(2,1)S(1)}, u32[]{:S(2)}, u32[]{:S(2)}) %all-to-all-start) | async-done | bytes 1048608 | tf_op jit(solution)/shard_map/all_to_all | solution.py:174
  46.4 3.6 %all-to-all-start.1 = ((bf16[8,128,512]{2,1,0:T(8,128)(2,1)}), bf16[8,128,512]{2,1,0:T(8,128)(2,1)S(1)}, u32[]{:S(2)}, u32[]{:S(2)}) async-start(bf16[8,128,512]{2,1,0:T(8,128)(2,1)} %bitcast.4), calls=%async_computation.1 | async-start | bytes 2097152 | tf_op jit(solution)/shard_map/all_to_all | solution.py:174
  50.1 0.6 pad_add_fusion.refs_0_
  50.6 14.7 %all-to-all-done.1.refs_2_ = bf16[8,128,512]{2,1,0:T(8,128)(2,1)S(1)} async-done(((bf16[8,128,512]{2,1,0:T(8,128)(2,1)}), bf16[8,128,512]{2,1,0:T(8,128)(2,1)S(1)}, u32[]{:S(2)}, u32[]{:S(2)}) %all-to-all-start.1) | async-done | bytes 1048608 | tf_op jit(solution)/shard_map/all_to_all | solution.py:174
  65.3 5.6 %all-gather.3.cloned.1.call-done = bf16[8,8,128,128]{3,2,1,0:T(8,128)(2,1)} async-done(((bf16[2,8,128,128]{3,2,1,0:T(8,128)(2,1)}), bf16[8,8,128,128]{3,2,1,0:T(8,128)(2,1)}) %all-gather.3.cloned.1.call-update) | async-done | bytes 2097168 | tf_op jit(solution)/shard_map/all_gather | solution.py:181
  71.0 33.6 %shard_map.76 = (bf16[8,128,512]{2,1,0:T(8,128)(2,1)}, bf16[4,2,8,128,128]{4,3,2,1,0:T(8,128)(2,1)}) custom-call(s32[17]{0:T(128)} %pad_add_fusion.refs_0_, bf16[8,128,512]{2,1,0:T(8,128)(2,1)} %copy-done.2, bf16[8,128,512]{2,1,0:T(8,128)(2,1)} %copy-done.3, bf16[4,2,8,128,128]{4,3,2,1,0:T(8,128)(2,1)} %bitcast.34), custom_call_target="tpu_custom_call" | custom-call | flops 6710886400 | bytes 5242880 | tf_op jit(solution)/shard_map/pallas_call | solution.py:142
  104.6 3.7 %all-to-all-start.3 = ((bf16[8,128,512]{2,1,0:T(8,128)(2,1)}), bf16[8,128,512]{2,1,0:T(8,128)(2,1)S(1)}, u32[]{:S(2)}, u32[]{:S(2)}) async-start(bf16[8,128,512]{2,1,0:T(8,128)(2,1)} %get-tuple-element.5), calls=%async_computation.3 | async-start | bytes 2097152 | tf_op jit(solution)/shard_map/all_to_all | solution.py:174
  108.3 46.2 %reduce-scatter.2.cloned.1.call-done = bf16[1,2,8,128,128]{4,3,2,1,0:T(8,128)(2,1)} async-done(((bf16[4,2,8,128,128]{4,3,2,1,0:T(8,128)(2,1)}), bf16[1,2,8,128,128]{4,3,2,1,0:T(8,128)(2,1)}) %reduce-scatter.2.cloned.1.call-update) | async-done | bytes 524304 | tf_op jit(solution)/shard_map/reduce_scatter | solution.py:187
  154.5 1.9 %copy.42 = bf16[2,8,128,128]{3,2,0,1:T(8,128)(2,1)} copy(bf16[2,8,128,128]{3,2,1,0:T(8,128)(2,1)} %bitcast.33) | data formatting | bytes 1048576 | tf_op jit(solution)/shard_map/reduce_scatter | solution.py:187
  156.4 3.7 %all-to-all-start.4 = ((bf16[2,8,128,128]{3,2,0,1:T(8,128)(2,1)}), bf16[2,8,128,128]{3,2,0,1:T(8,128)(2,1)S(1)}, u32[]{:S(2)}, u32[]{:S(2)}) async-start(bf16[2,8,128,128]{3,2,0,1:T(8,128)(2,1)} %copy.42), calls=%async_computation.5 | async-start | bytes 1048576 | tf_op jit(solution)/shard_map/all_to_all | solution.py:188
  160.0 0.7 copy.41
  160.7 1.3 copy.44
  162.0 7.8 %all-to-all-done.4 = bf16[2,8,128,128]{3,2,0,1:T(8,128)(2,1)S(1)} async-done(((bf16[2,8,128,128]{3,2,0,1:T(8,128)(2,1)}), bf16[2,8,128,128]{3,2,0,1:T(8,128)(2,1)S(1)}, u32[]{:S(2)}, u32[]{:S(2)}) %all-to-all-start.4) | async-done | bytes 524320 | tf_op jit(solution)/shard_map/all_to_all | solution.py:188
  170.1 0.9 copy.46
  171.0 0.8 copy.45
  (19 shorter events, 0.8 us)
Async XLA Ops:
  7.2 63.8 %all-gather.3.cloned.1.call-start = ((), (), s32[]{:S(2)}) async-start(), calls=%async_computation.7 | async-start | bytes 2621440 | tf_op jit(solution)/shard_map/all_gather | solution.py:181
  9.5 16.0 %copy-start = (bf16[128,4096]{1,0:T(8,128)(2,1)S(1)}, bf16[128,4096]{1,0:T(8,128)(2,1)}, u32[]{:S(2)}) copy-start(bf16[128,4096]{1,0:T(8,128)(2,1)} %param.5) | copy-start | bytes 3145732
  26.2 4.9 %copy-start.1 = (bf16[128,4096]{1,0:T(8,128)(2,1)S(1)}, bf16[128,4096]{1,0:T(8,128)(2,1)}, u32[]{:S(2)}) copy-start(bf16[128,4096]{1,0:T(8,128)(2,1)} %param.8) | copy-start | bytes 3145732
  27.5 18.9 %all-to-all-start = ((bf16[8,128,512]{2,1,0:T(8,128)(2,1)}), bf16[8,128,512]{2,1,0:T(8,128)(2,1)S(1)}, u32[]{:S(2)}, u32[]{:S(2)}) async-start(bf16[8,128,512]{2,1,0:T(8,128)(2,1)} %bitcast.2), calls=%async_computation | async-start | bytes 2097152 | tf_op jit(solution)/shard_map/all_to_all | solution.py:174
  31.8 18.3 %copy-start.4 = (s32[16]{0:T(128)S(1)}, s32[16]{0:T(128)}, u32[]{:S(2)}) copy-start(s32[16]{0:T(128)} %param.9) | copy-start | bytes 196
  46.4 24.5 %copy-start.2 = (bf16[8,128,512]{2,1,0:T(8,128)(2,1)}, bf16[8,128,512]{2,1,0:T(8,128)(2,1)S(1)}, u32[]{:S(2)}) copy-start(bf16[8,128,512]{2,1,0:T(8,128)(2,1)S(1)} %all-to-all-done.refs_1_) | copy-start | bytes 3145732
  46.4 18.9 %all-to-all-start.1 = ((bf16[8,128,512]{2,1,0:T(8,128)(2,1)}), bf16[8,128,512]{2,1,0:T(8,128)(2,1)S(1)}, u32[]{:S(2)}, u32[]{:S(2)}) async-start(bf16[8,128,512]{2,1,0:T(8,128)(2,1)} %bitcast.4), calls=%async_computation.1 | async-start | bytes 2097152 | tf_op jit(solution)/shard_map/all_to_all | solution.py:174
  50.0 104.5 %reduce-scatter.2.cloned.1.call-start = ((), (), s32[]{:S(2)}) async-start(), calls=%async_computation.6 | async-start | bytes 2621440 | tf_op jit(solution)/shard_map/reduce_scatter | solution.py:187
  65.3 5.6 %copy-start.3 = (bf16[8,128,512]{2,1,0:T(8,128)(2,1)}, bf16[8,128,512]{2,1,0:T(8,128)(2,1)S(1)}, u32[]{:S(2)}) copy-start(bf16[8,128,512]{2,1,0:T(8,128)(2,1)S(1)} %all-to-all-done.1.refs_2_) | copy-start | bytes 3145732
  104.6 51.8 %all-to-all-start.3 = ((bf16[8,128,512]{2,1,0:T(8,128)(2,1)}), bf16[8,128,512]{2,1,0:T(8,128)(2,1)S(1)}, u32[]{:S(2)}, u32[]{:S(2)}) async-start(bf16[8,128,512]{2,1,0:T(8,128)(2,1)} %get-tuple-element.5), calls=%async_computation.3 | async-start | bytes 2097152 | tf_op jit(solution)/shard_map/all_to_all | solution.py:174
  156.4 13.4 %all-to-all-start.4 = ((bf16[2,8,128,128]{3,2,0,1:T(8,128)(2,1)}), bf16[2,8,128,128]{3,2,0,1:T(8,128)(2,1)S(1)}, u32[]{:S(2)}, u32[]{:S(2)}) async-start(bf16[2,8,128,128]{3,2,0,1:T(8,128)(2,1)} %copy.42), calls=%async_computation.5 | async-start | bytes 1048576 | tf_op jit(solution)/shard_map/all_to_all | solution.py:188
Sparse Core Ops, SparseCore 0:
  25.6 45.2 all-gather.2
  104.7 49.7 reduce-scatter.1

commit v2 on v1

v2 whole, which is shorter than its diff:
```python
import jax
import jax.numpy as jnp
from jax import lax
from jax.experimental import pallas as pl
from jax.experimental.pallas import tpu as pltpu
from jax.sharding import PartitionSpec as P

QUERY_HEAD_COUNT = 32
KEY_VALUE_HEADS = 8
HEAD_SIZE = 128
WINDOW = 4
TILES = 2 * WINDOW
SCALE = HEAD_SIZE ** (-0.5)
LOG2_E = 1.4426950408889634
NT = (((1,), (1,)), ((), ()))
NN = (((1,), (0,)), ((), ()))
TN = (((0,), (0,)), ((), ()))
LOW = jnp.bfloat16
VMEM_LIMIT = 60 * 1024 * 1024


def dot(a, b, dims):
    return lax.dot_general(a, b, dims, preferred_element_type=jnp.float32)


def fold(x, op):
    return op(x.reshape(x.shape[0] // 8, 8, x.shape[1]), axis=0)


def stack(ref):
    heads = ref.shape[2] // HEAD_SIZE
    return jnp.concatenate(
        [ref[0, :, h * HEAD_SIZE : (h + 1) * HEAD_SIZE] for h in range(heads)], axis=0
    )


def list_tiles(ids_ref, tile_ref, ranks, splits):
    rank = pl.program_id(0)
    slot = ids_ref[2 * ranks] // (splits // 2)
    own = ids_ref[2 * rank + slot]
    tile_ref[0] = rank * 2 + slot
    count = jnp.int32(1)
    for back in range(WINDOW):
        key_rank = lax.rem(rank - back + ranks, ranks)
        for key_slot in range(2):
            tile_ref[count] = key_rank * 2 + key_slot
            count = count + jnp.where(ids_ref[2 * key_rank + key_slot] < own, 1, 0)
    return count


def load_chunks(ids_ref, chunk_refs, all_ref, sem_ref, ranks, splits):
    z = ids_ref[2 * ranks]
    return [
        pltpu.make_async_copy(
            chunk, all_ref.at[lax.rem(z - s + splits, splits)], sem_ref.at[s]
        )
        for s, chunk in enumerate(chunk_refs)
    ]


def tile_rows(all_ref, tile_ref, i, half):
    t = tile_ref[i]
    return jnp.concatenate(
        [all_ref[lax.rem(t, 2) * half + j, t // 2] for j in range(half)], axis=0
    )


def add_tile(all_ref, tile_ref, i, half, rows, update):
    t = tile_ref[i]
    for j in range(half):
        all_ref[lax.rem(t, 2) * half + j, t // 2] += update[j * rows : (j + 1) * rows]


def probs_kernel(ranks, splits, heads, rows, ids_ref, q_ref, *refs):
    k_chunks, (p_ref, tile_ref, st_ref, k_ref, sem_ref) = refs[:splits], refs[splits:]
    half = splits // 2
    width = heads * rows

    @pl.when(pl.program_id(0) == 0)
    def _():
        copies = load_chunks(ids_ref, k_chunks, k_ref, sem_ref, ranks, splits)
        for copy in copies:
            copy.start()
        for copy in copies:
            copy.wait()

    count = list_tiles(ids_ref, tile_ref, ranks, splits)
    qs = stack(q_ref)
    key_pos = lax.broadcasted_iota(jnp.int32, (half * rows, width), 0)
    row_pos = lax.rem(lax.broadcasted_iota(jnp.int32, (half * rows, width), 1), rows)
    row_pos = row_pos + lax.rem(ids_ref[2 * ranks], half) * rows
    s_own = jnp.where(
        key_pos <= row_pos, dot(tile_rows(k_ref, tile_ref, 0, half), qs, NT), -1e30
    )
    st_ref[0] = s_own

    def scores(i, top):
        s = dot(tile_rows(k_ref, tile_ref, i, half), qs, NT)
        st_ref[i] = s
        return jnp.maximum(top, fold(s, jnp.max))

    top = lax.fori_loop(1, count, scores, fold(s_own, jnp.max))
    top = jnp.max(top, axis=0, keepdims=True) * (SCALE * LOG2_E)

    def weights(i, total):
        p = jnp.exp2(st_ref[i] * (SCALE * LOG2_E) - top)
        st_ref[i] = p
        return total + fold(p, jnp.sum)

    total = lax.fori_loop(0, count, weights, jnp.zeros((8, width), jnp.float32))
    inverse = 1.0 / jnp.sum(total, axis=0, keepdims=True)

    def normal(i, carry):
        p_ref[0, i] = (st_ref[i] * inverse).astype(LOW)
        return carry

    lax.fori_loop(0, count, normal, 0)


def value_kernel(ranks, splits, heads, rows, ids_ref, g_ref, p_ref, *refs):
    out_refs, (tile_ref, dv_ref) = refs[:splits], refs[splits:]
    half = splits // 2

    @pl.when(pl.program_id(0) == 0)
    def _():
        dv_ref[...] = jnp.zeros_like(dv_ref)

    count = list_tiles(ids_ref, tile_ref, ranks, splits)
    gs = stack(g_ref)

    def values(i, carry):
        add_tile(dv_ref, tile_ref, i, half, rows, dot(p_ref[0, i], gs, NN))
        return carry

    lax.fori_loop(0, count, values, 0)

    @pl.when(pl.program_id(0) == ranks - 1)
    def _():
        z = ids_ref[2 * ranks]
        for s, out in enumerate(out_refs):
            out[...] = dv_ref[lax.rem(z + s, splits)].astype(LOW)


def grads_kernel(ranks, splits, heads, rows, ids_ref, q_ref, g_ref, p_ref, *refs):
    k_chunks, v_chunks, dq_ref = refs[:splits], refs[splits : 2 * splits], refs[2 * splits]
    out_refs = refs[2 * splits + 1 : 3 * splits + 1]
    tile_ref, dp_ref, dqt_ref, k_ref, v_ref, dk_ref, sem_ref = refs[3 * splits + 1 :]
    half = splits // 2
    width = heads * rows

    @pl.when(pl.program_id(0) == 0)
    def _():
        copies = load_chunks(ids_ref, k_chunks, k_ref, sem_ref.at[0], ranks, splits)
        copies += load_chunks(ids_ref, v_chunks, v_ref, sem_ref.at[1], ranks, splits)
        for copy in copies:
            copy.start()
        dk_ref[...] = jnp.zeros_like(dk_ref)
        for copy in copies:
            copy.wait()

    count = list_tiles(ids_ref, tile_ref, ranks, splits)
    qs = stack(q_ref)
    gs = stack(g_ref)

    def deltas(i, delta):
        dp = dot(tile_rows(v_ref, tile_ref, i, half), gs, NT)
        dp_ref[i] = dp
        return delta + fold(p_ref[0, i].astype(jnp.float32) * dp, jnp.sum)

    delta = lax.fori_loop(0, count, deltas, jnp.zeros((8, width), jnp.float32))
    delta = jnp.sum(delta, axis=0, keepdims=True)
    dqt_ref[...] = jnp.zeros_like(dqt_ref)

    def grads(i, carry):
        ds = (p_ref[0, i].astype(jnp.float32) * (dp_ref[i] - delta)).astype(LOW)
        add_tile(dk_ref, tile_ref, i, half, rows, dot(ds, qs, NN))
        dqt_ref[...] += dot(tile_rows(k_ref, tile_ref, i, half), ds, TN)
        return carry

    lax.fori_loop(0, count, grads, 0)
    dq = (dqt_ref[...] * SCALE).T.astype(LOW)
    for h in range(heads):
        dq_ref[0, :, h * HEAD_SIZE : (h + 1) * HEAD_SIZE] = dq[h * rows : (h + 1) * rows]

    @pl.when(pl.program_id(0) == ranks - 1)
    def _():
        z = ids_ref[2 * ranks]
        for s, out in enumerate(out_refs):
            out[...] = (dk_ref[lax.rem(z + s, splits)] * SCALE).astype(LOW)


class Attention:
    def __init__(self, ids, q, splits):
        self.ids, self.splits = ids, splits
        self.ranks, self.rows, self.width = q.shape
        self.heads = self.width // HEAD_SIZE
        self.stretch = splits // 2 * self.rows
        self.chunk = (self.ranks, self.rows, HEAD_SIZE)
        self.smem = pl.BlockSpec(memory_space=pltpu.SMEM)
        self.any = pl.BlockSpec(memory_space=pl.ANY)
        self.row_block = pl.BlockSpec((1, self.rows, self.width), lambda r: (r, 0, 0))
        self.probs_shape = (self.ranks, TILES, self.stretch, self.heads * self.rows)
        self.probs_block = pl.BlockSpec((1,) + self.probs_shape[1:], lambda r: (r, 0, 0, 0))
        self.chunk_block = pl.BlockSpec(
            self.chunk, lambda r: (0, 0, 0), pipeline_mode=pl.Buffered(1)
        )
        self.chunk_out = jax.ShapeDtypeStruct(self.chunk, LOW)
        self.tile_list = pltpu.SMEM((TILES + 1,), jnp.int32)
        self.scores = pltpu.VMEM(self.probs_shape[1:], jnp.float32)
        self.all_low = pltpu.VMEM((splits,) + self.chunk, LOW)
        self.all_wide = pltpu.VMEM((splits,) + self.chunk, jnp.float32)

    def call(self, kernel, matmuls, *operands, **kwargs):
        def bound(*refs):
            kernel(self.ranks, self.splits, self.heads, self.rows, *refs)

        tile = 2 * self.stretch * self.heads * self.rows * HEAD_SIZE
        cost = pl.CostEstimate(
            flops=matmuls * 5 * self.ranks * tile, bytes_accessed=1 << 24, transcendentals=0
        )
        return pl.pallas_call(
            bound,
            grid=(self.ranks,),
            compiler_params=pltpu.CompilerParams(vmem_limit_bytes=VMEM_LIMIT),
            cost_estimate=cost,
            **kwargs,
        )(self.ids, *operands)

    def probs(self, q, k):
        return self.call(
            probs_kernel, 4, q, *k,
            in_specs=[self.smem, self.row_block] + [self.any] * self.splits,
            out_specs=self.probs_block,
            out_shape=jax.ShapeDtypeStruct(self.probs_shape, LOW),
            scratch_shapes=[
                self.tile_list, self.scores, self.all_low,
                pltpu.SemaphoreType.DMA((self.splits,)),
            ],
        )

    def value_grads(self, g, p):
        return self.call(
            value_kernel, 2, g, p,
            in_specs=[self.smem, self.row_block, self.probs_block],
            out_specs=[self.chunk_block] * self.splits,
            out_shape=[self.chunk_out] * self.splits,
            scratch_shapes=[self.tile_list, self.all_wide],
        )

    def grads(self, q, g, p, k, v):
        out = self.call(
            grads_kernel, 4, q, g, p, *k, *v,
            in_specs=[self.smem, self.row_block, self.row_block, self.probs_block]
            + [self.any] * (2 * self.splits),
            out_specs=[self.row_block] + [self.chunk_block] * self.splits,
            out_shape=[jax.ShapeDtypeStruct(q.shape, LOW)] + [self.chunk_out] * self.splits,
            scratch_shapes=[
                self.tile_list, self.scores,
                pltpu.VMEM((HEAD_SIZE, self.heads * self.rows), jnp.float32),
                self.all_low, self.all_low, self.all_wide,
                pltpu.SemaphoreType.DMA((2, self.splits)),
            ],
        )
        return out[0], out[1:]


def body(query, key, value, d_out, stretch_ids):
    rows = query.shape[0]
    ranks = lax.axis_size("ctx")
    splits = lax.axis_size("head")
    copies = ranks // KEY_VALUE_HEADS
    z = lax.axis_index("head")

    def by_device(array):
        return array.reshape(rows, ranks, array.shape[1] // ranks).swapaxes(0, 1)

    def to_heads(array):
        return lax.all_to_all(array, "ctx", split_axis=0, concat_axis=0, tiled=True)

    def by_key_head(array):
        split = array.reshape(rows, KEY_VALUE_HEADS, HEAD_SIZE).swapaxes(0, 1)
        return jnp.repeat(split, copies, axis=0)

    def shift(array, by):
        return lax.ppermute(array, "head", [(i, (i + by) % splits) for i in range(splits)])

    def gather(array):
        return [array] + [shift(array, s) for s in range(1, splits)]

    def scatter(chunks):
        total = chunks[0].astype(jnp.float32)
        for s in range(1, splits):
            total = total + shift(chunks[s], s).astype(jnp.float32)
        return total.astype(LOW)

    kv = to_heads(jnp.stack((by_key_head(key), by_key_head(value)), axis=1))
    ids = jnp.concatenate((stretch_ids, z.astype(jnp.int32)[None]))
    q_in, k_own, v_own = lax.optimization_barrier((by_device(query), kv[:, 0], kv[:, 1]))
    k = gather(k_own)
    q, g_in = lax.optimization_barrier((to_heads(q_in), by_device(d_out)))
    k, v_own = lax.optimization_barrier((k, v_own))
    v = gather(v_own)
    g = to_heads(g_in)
    part = Attention(ids, q, splits)
    p = part.probs(q, k)
    dv, q = lax.optimization_barrier((part.value_grads(g, p), q))
    dv = scatter(dv)
    dq, dk = part.grads(q, g, p, k, v)
    dk = scatter(dk)
    dq = to_heads(dq).swapaxes(0, 1).reshape(rows, QUERY_HEAD_COUNT * HEAD_SIZE)
    dkv = to_heads(jnp.stack((dk, dv), axis=1))
    if copies > 1:
        shape = (KEY_VALUE_HEADS, copies, 2, rows, HEAD_SIZE)
        dkv = jnp.sum(dkv.reshape(shape).astype(jnp.float32), axis=1).astype(LOW)
    dkv = dkv.transpose(1, 2, 0, 3).reshape(2, rows, KEY_VALUE_HEADS * HEAD_SIZE)
    return dq, dkv[0], dkv[1]


def solution(mesh):
    spec = P(("ctx", "head"), None)
    return jax.shard_map(
        body,
        mesh=mesh,
        in_specs=(spec, spec, spec, spec, P()),
        out_specs=(spec, spec, spec),
        check_vma=False,
    )
```

time: 180 us -> 214 us (1.19)
  starting transfers between devices: 14.5 us -> 47.3 us
  Pallas kernels: 33.6 us -> 49.9 us
  between operations: 14.2 us -> 0.89 us
  waiting for transfers between devices: 87.7 us -> 84.9 us
    ppermute x0 -> x12, waiting for transfers between devices: none -> 52.4 us  [shift(): lax.ppermute(array, 'head', [(i, (i + by) % splits) for i in range(splits)])]
    reduce_scatter x1 -> x0, waiting for transfers between devices: 46.2 us -> none  [body(): dkv = lax.psum_scatter(dkv, 'head', scatter_dimension=0, tiled=False)]
    ppermute x0 -> x12, starting transfers between devices: none -> 31.4 us  [shift(): lax.ppermute(array, 'head', [(i, (i + by) % splits) for i in range(splits)])]
    pallas_call x1 -> x3, Pallas kernels: 33.6 us -> 49.9 us  [call(): pl.pallas_call(bound, grid=(self.ranks,), compiler_params=pltpu.CompilerP...]
    all_to_all x1 -> x0, waiting for transfers between devices: 7.77 us -> none  [body(): dkv = lax.all_to_all(dkv, 'ctx', split_axis=1, concat_axis=1, tiled=True)]
    all_gather x1 -> x0, waiting for transfers between devices: 5.62 us -> none  [body(): kv = lax.all_gather(kv, 'head', axis=0, tiled=False)]
    all_to_all x3 -> x4, starting transfers between devices: 10.8 us -> 15.9 us  [to_heads(): return lax.all_to_all(array, 'ctx', split_axis=0, concat_axis=0, tiled=True)]
    all_to_all x3 -> x4, waiting for transfers between devices: 28 us -> 32.5 us  [to_heads(): return lax.all_to_all(array, 'ctx', split_axis=0, concat_axis=0, tiled=True)]
  transfers between devices with their start and end apart: 6 -> 16, of which waited for: 5 -> 10; matrix products, arithmetic and copies ran while one was open for 5% -> 5% of each run, Pallas kernels for 0% -> 13%
where the time goes in v2:
time: 214 us; the launch traced here: 213 us
  waiting for transfers between devices  84.9 us (40%)
  Pallas kernels  49.9 us (23%)
  starting transfers between devices  47.3 us (22%)
  local copies, waits for them, and re-layouts  14.2 us (7%)
  blocking collectives  13.5 us (6%)
    ppermute x12, waiting for transfers between devices, shift(): lax.ppermute(array, 'head', [(i, (i + by) % splits) for i in range(splits)])  52.4 us
    pallas_call x3, Pallas kernels, call(): pl.pallas_call(bound, grid=(self.ranks,), compiler_params=pltpu.CompilerP...  49.9 us
    all_to_all x4, waiting for transfers between devices, to_heads(): return lax.all_to_all(array, 'ctx', split_axis=0, concat_axis=0, tiled=True)  32.5 us
    ppermute x12, starting transfers between devices, shift(): lax.ppermute(array, 'head', [(i, (i + by) % splits) for i in range(splits)])  31.4 us
    all_to_all x4, starting transfers between devices, to_heads(): return lax.all_to_all(array, 'ctx', split_axis=0, concat_axis=0, tiled=True)  15.9 us
    all_to_all x1, blocking collectives, to_heads(): return lax.all_to_all(array, 'ctx', split_axis=0, concat_axis=0, tiled=True)  13.5 us
    unnamed x31, local copies, waits for them, and re-layouts  9.5 us
  transfers between devices with their start and end apart: 16, of which 10 were waited for; matrix products, arithmetic and copies ran while one was open for 5% of the time, Pallas kernels for 13%

profile of v2, /device:TPU:0, one launch (start us, length us, event | category | flops | bytes accessed | tf_op | source)
XLA Modules:
  0.0 212.6 jit_solution(17190589536703075506)
XLA Ops:
  4.0 5.2 %all-to-all-start = ((bf16[8,2,128,128]{3,2,1,0:T(8,128)(2,1)}), bf16[8,2,128,128]{3,2,1,0:T(8,128)(2,1)S(1)}, u32[]{:S(2)}, u32[]{:S(2)}) async-start(bf16[8,2,128,128]{3,2,1,0:T(8,128)(2,1)} %copy.26), calls=%async_computation | async-start | bytes 1048576 | tf_op jit(solution)/shard_map/all_to_all | solution.py:278
  12.1 6.8 %all-to-all-done = bf16[8,2,128,128]{3,2,1,0:T(8,128)(2,1)S(1)} async-done(((bf16[8,2,128,128]{3,2,1,0:T(8,128)(2,1)}), bf16[8,2,128,128]{3,2,1,0:T(8,128)(2,1)S(1)}, u32[]{:S(2)}, u32[]{:S(2)}) %all-to-all-start) | async-done | bytes 524320 | tf_op jit(solution)/shard_map/all_to_all | solution.py:278
  18.9 3.6 %all-to-all-start.1 = ((bf16[8,128,512]{2,1,0:T(8,128)(2,1)}), bf16[8,128,512]{2,1,0:T(8,128)(2,1)S(1)}, u32[]{:S(2)}, u32[]{:S(2)}) async-start(bf16[8,128,512]{2,1,0:T(8,128)(2,1)} %bitcast.2), calls=%async_computation.1 | async-start | bytes 2097152 | tf_op jit(solution)/shard_map/all_to_all | solution.py:278
  22.5 1.6 copy.29
  25.5 12.4 %all-to-all-done.1.refs_1_ = bf16[8,128,512]{2,1,0:T(8,128)(2,1)S(1)} async-done(((bf16[8,128,512]{2,1,0:T(8,128)(2,1)}), bf16[8,128,512]{2,1,0:T(8,128)(2,1)S(1)}, u32[]{:S(2)}, u32[]{:S(2)}) %all-to-all-start.1) | async-done | bytes 1048608 | tf_op jit(solution)/shard_map/all_to_all | solution.py:278
  37.9 3.6 %all-to-all-start.2 = ((bf16[8,128,512]{2,1,0:T(8,128)(2,1)}), bf16[8,128,512]{2,1,0:T(8,128)(2,1)S(1)}, u32[]{:S(2)}, u32[]{:S(2)}) async-start(bf16[8,128,512]{2,1,0:T(8,128)(2,1)} %bitcast.12), calls=%async_computation.2 | async-start | bytes 2097152 | tf_op jit(solution)/shard_map/all_to_all | solution.py:278
  41.4 3.7 %collective-permute-start.2 = (bf16[8,128,128]{2,1,0:T(8,128)(2,1)S(1)}, bf16[8,128,128]{2,1,0:T(8,128)(2,1)S(1)}, u32[]{:S(2)}, u32[]{:S(2)}) collective-permute-start(bf16[8,128,128]{2,1,0:T(8,128)(2,1)S(1)} %get-tuple-element.32.refs_2_.refs_4_), channel_id=1, source_target_pairs={{0,3},{1,0},{2,1},{3,2},{4,7},{5,4},{6,5},{7,6},{8,11},{9,8},{10,9... | collective-permute-start | bytes 786440 | tf_op jit(solution)/shard_map/ppermute | solution.py:285
  46.8 5.1 %collective-permute-done.2.refs_5_.refs_7_ = bf16[8,128,128]{2,1,0:T(8,128)(2,1)S(1)} collective-permute-done((bf16[8,128,128]{2,1,0:T(8,128)(2,1)S(1)}, bf16[8,128,128]{2,1,0:T(8,128)(2,1)S(1)}, u32[]{:S(2)}, u32[]{:S(2)}) %collective-permute-start.2) | collective-permute-done | bytes 262176 | tf_op jit(solution)/shard_map/ppermute | solution.py:285
  51.8 16.1 %collective-permute-done.1.refs_4_.refs_6_ = bf16[8,128,128]{2,1,0:T(8,128)(2,1)S(1)} collective-permute-done((bf16[8,128,128]{2,1,0:T(8,128)(2,1)S(1)}, bf16[8,128,128]{2,1,0:T(8,128)(2,1)S(1)}, u32[]{:S(2)}, u32[]{:S(2)}) %collective-permute-start.1) | collective-permute-done | bytes 262176 | tf_op jit(solution)/shard_map/ppermute | solution.py:285
  68.0 2.7 %collective-permute-start.4 = (bf16[8,128,128]{2,1,0:T(8,128)(2,1)S(1)}, bf16[8,128,128]{2,1,0:T(8,128)(2,1)}, u32[]{:S(2)}, u32[]{:S(2)}) collective-permute-start(bf16[8,128,128]{2,1,0:T(8,128)(2,1)S(1)} %get-tuple-element.41.refs_8_), channel_id=1, source_target_pairs={{0,2},{1,3},{2,0},{3,1},{4,6},{5,7},{6,4},{7,5},{8,10},{9,11},{10,... | collective-permute-start | bytes 786440 | tf_op jit(solution)/shard_map/ppermute | solution.py:285
  70.7 2.0 collective-permute-start.3
  72.8 15.3 %shard_map.76.refs_2_.refs_3_ = bf16[8,8,256,512]{3,2,1,0:T(8,128)(2,1)} custom-call(s32[17]{0:T(128)} %pad_add_fusion.refs_0_, bf16[8,128,512]{2,1,0:T(8,128)(2,1)} %copy-done.1, bf16[8,128,128]{2,1,0:T(8,128)(2,1)} %copy-done.3, bf16[8,128,128]{2,1,0:T(8,128)(2,1)} %copy-done.6, bf16[8,128,128]{2,1,0:T(8,128)(2,1)} %copy-done.5, bf16[8,128,128]{2,1,0:T(8,128)(2,1)} %copy-done.4), custom_call_target="tpu_custom_call" | custom-call | flops 5368709120 | bytes 16777216 | tf_op jit(solution)/shard_map/pallas_call | solution.py:221
  89.1 13.2 %shard_map.77 = (bf16[8,128,128]{2,1,0:T(8,128)(2,1)}, bf16[8,128,128]{2,1,0:T(8,128)(2,1)}, bf16[8,128,128]{2,1,0:T(8,128)(2,1)}, bf16[8,128,128]{2,1,0:T(8,128)(2,1)}) custom-call(s32[17]{0:T(128)} %pad_add_fusion.refs_0_, bf16[8,128,512]{2,1,0:T(8,128)(2,1)} %copy-done, bf16[8,8,256,512]{3,2,1,0:T(8,128)(2,1)} %shard_map.76.refs_2_.refs_3_), custom_call_target="tpu_custom_call" | custom-call | flops 2684354560 | bytes 16777216 | tf_op jit(solution)/shard_map/pallas_call | solution.py:221
  102.3 21.4 %shard_map.78 = (bf16[8,128,512]{2,1,0:T(8,128)(2,1)}, bf16[8,128,128]{2,1,0:T(8,128)(2,1)}, bf16[8,128,128]{2,1,0:T(8,128)(2,1)}, bf16[8,128,128]{2,1,0:T(8,128)(2,1)}, bf16[8,128,128]{2,1,0:T(8,128)(2,1)}) custom-call(s32[17]{0:T(128)} %pad_add_fusion.refs_0_, bf16[8,128,512]{2,1,0:T(8,128)(2,1)} %copy-done.1, bf16[8,128,512]{2,1,0:T(8,128)(2,1)} %copy-done, ...), custom_call_target="tpu_custom_call" | custom-call | flops 5368709120 | bytes 16777216 | tf_op jit(solution)/shard_map/pallas_call | solution.py:221
  123.8 15.4 %collective-permute-start.7 = (bf16[8,128,128]{2,1,0:T(8,128)(2,1)}, bf16[8,128,128]{2,1,0:T(8,128)(2,1)S(1)}, u32[]{:S(2)}, u32[]{:S(2)}) collective-permute-start(bf16[8,128,128]{2,1,0:T(8,128)(2,1)} %get-tuple-element.45), channel_id=1, source_target_pairs={{0,2},{1,3},{2,0},{3,1},{4,6},{5,7},{6,4},{7,5},{8,10},{9,11},{10,... | collective-permute-start | bytes 786440 | tf_op jit(solution)/shard_map/ppermute | solution.py:285
  141.2 5.0 %collective-permute-done.6 = bf16[8,128,128]{2,1,0:T(8,128)(2,1)S(1)} collective-permute-done((bf16[8,128,128]{2,1,0:T(8,128)(2,1)}, bf16[8,128,128]{2,1,0:T(8,128)(2,1)S(1)}, u32[]{:S(2)}, u32[]{:S(2)}) %collective-permute-start.6) | collective-permute-done | bytes 262176 | tf_op jit(solution)/shard_map/ppermute | solution.py:285
  146.2 4.4 %collective-permute-start.11 = (bf16[8,128,128]{2,1,0:T(8,128)(2,1)S(1)}, bf16[8,128,128]{2,1,0:T(8,128)(2,1)S(1)}, u32[]{:S(2)}, u32[]{:S(2)}) collective-permute-start(bf16[8,128,128]{2,1,0:T(8,128)(2,1)S(1)} %copy-done.8), channel_id=1, source_target_pairs={{0,3},{1,0},{2,1},{3,2},{4,7},{5,4},{6,5},{7,6},{8,11},{9,8},{10,9... | collective-permute-start | bytes 786440 | tf_op jit(solution)/shard_map/ppermute | solution.py:285
  150.6 6.9 %collective-permute-done.7 = bf16[8,128,128]{2,1,0:T(8,128)(2,1)S(1)} collective-permute-done((bf16[8,128,128]{2,1,0:T(8,128)(2,1)}, bf16[8,128,128]{2,1,0:T(8,128)(2,1)S(1)}, u32[]{:S(2)}, u32[]{:S(2)}) %collective-permute-start.7) | collective-permute-done | bytes 262176 | tf_op jit(solution)/shard_map/ppermute | solution.py:285
  157.5 2.2 %collective-permute-done.8 = bf16[8,128,128]{2,1,0:T(8,128)(2,1)S(1)} collective-permute-done((bf16[8,128,128]{2,1,0:T(8,128)(2,1)}, bf16[8,128,128]{2,1,0:T(8,128)(2,1)S(1)}, u32[]{:S(2)}, u32[]{:S(2)}) %collective-permute-start.8) | collective-permute-done | bytes 262176 | tf_op jit(solution)/shard_map/ppermute | solution.py:285
  160.8 2.3 %collective-permute-done.9 = bf16[8,128,128]{2,1,0:T(8,128)(2,1)S(1)} collective-permute-done((bf16[8,128,128]{2,1,0:T(8,128)(2,1)S(1)}, bf16[8,128,128]{2,1,0:T(8,128)(2,1)S(1)}, u32[]{:S(2)}, u32[]{:S(2)}) %collective-permute-start.9) | collective-permute-done | bytes 262176 | tf_op jit(solution)/shard_map/ppermute | solution.py:285
  163.1 14.9 %collective-permute-done.10 = bf16[8,128,128]{2,1,0:T(8,128)(2,1)S(1)} collective-permute-done((bf16[8,128,128]{2,1,0:T(8,128)(2,1)S(1)}, bf16[8,128,128]{2,1,0:T(8,128)(2,1)S(1)}, u32[]{:S(2)}, u32[]{:S(2)}) %collective-permute-start.10) | collective-permute-done | bytes 262176 | tf_op jit(solution)/shard_map/ppermute | solution.py:285
  178.2 13.5 %all_to_all.25 = bf16[8,2,128,128]{3,2,1,0:T(8,128)(2,1)S(1)} all-to-all(bf16[8,2,128,128]{3,2,1,0:T(8,128)(2,1)S(1)} %copy.32), channel_id=1, replica_groups=mesh['ctx'=8,'head'=4] {'ctx'}, dimensions={0} | all-to-all | bytes 1048576 | tf_op jit(solution)/shard_map/all_to_all | solution.py:278
  191.7 3.6 %all-to-all-start.3 = ((bf16[8,128,512]{2,1,0:T(8,128)(2,1)}), bf16[8,128,512]{2,1,0:T(8,128)(2,1)S(1)}, u32[]{:S(2)}, u32[]{:S(2)}) async-start(bf16[8,128,512]{2,1,0:T(8,128)(2,1)} %get-tuple-element.42), calls=%async_computation.3 | async-start | bytes 2097152 | tf_op jit(solution)/shard_map/all_to_all | solution.py:278
  197.3 13.3 %all-to-all-done.3 = bf16[8,128,512]{2,1,0:T(8,128)(2,1)S(1)} async-done(((bf16[8,128,512]{2,1,0:T(8,128)(2,1)}), bf16[8,128,512]{2,1,0:T(8,128)(2,1)S(1)}, u32[]{:S(2)}, u32[]{:S(2)}) %all-to-all-start.3) | async-done | bytes 1048608 | tf_op jit(solution)/shard_map/all_to_all | solution.py:278
  (56 shorter events, 17.8 us)
Async XLA Ops:
  0.6 45.5 %copy-start.11 = (s32[16]{0:T(128)S(1)}, s32[16]{0:T(128)}, u32[]{:S(2)}) copy-start(s32[16]{0:T(128)} %param.9) | copy-start | bytes 196
  4.0 14.9 %all-to-all-start = ((bf16[8,2,128,128]{3,2,1,0:T(8,128)(2,1)}), bf16[8,2,128,128]{3,2,1,0:T(8,128)(2,1)S(1)}, u32[]{:S(2)}, u32[]{:S(2)}) async-start(bf16[8,2,128,128]{3,2,1,0:T(8,128)(2,1)} %copy.26), calls=%async_computation | async-start | bytes 1048576 | tf_op jit(solution)/shard_map/all_to_all | solution.py:278
  18.9 53.8 %copy-start.3 = (bf16[8,128,128]{2,1,0:T(8,128)(2,1)}, bf16[8,128,128]{2,1,0:T(8,128)(2,1)S(1)}, u32[]{:S(2)}) copy-start(bf16[8,128,128]{2,1,0:T(8,128)(2,1)S(1)} %get-tuple-element.32.refs_2_.refs_4_) | copy-start | bytes 786436
  18.9 83.3 %copy-start.2 = (bf16[8,128,128]{2,1,0:T(8,128)(2,1)}, bf16[8,128,128]{2,1,0:T(8,128)(2,1)S(1)}, u32[]{:S(2)}) copy-start(bf16[8,128,128]{2,1,0:T(8,128)(2,1)S(1)} %get-tuple-element.41.refs_8_) | copy-start | bytes 786436
  18.9 18.9 %all-to-all-start.1 = ((bf16[8,128,512]{2,1,0:T(8,128)(2,1)}), bf16[8,128,512]{2,1,0:T(8,128)(2,1)S(1)}, u32[]{:S(2)}, u32[]{:S(2)}) async-start(bf16[8,128,512]{2,1,0:T(8,128)(2,1)} %bitcast.2), calls=%async_computation.1 | async-start | bytes 2097152 | tf_op jit(solution)/shard_map/all_to_all | solution.py:278
  37.9 34.9 %copy-start.1 = (bf16[8,128,512]{2,1,0:T(8,128)(2,1)}, bf16[8,128,512]{2,1,0:T(8,128)(2,1)S(1)}, u32[]{:S(2)}) copy-start(bf16[8,128,512]{2,1,0:T(8,128)(2,1)S(1)} %all-to-all-done.1.refs_1_) | copy-start | bytes 3145732
  37.9 50.2 %all-to-all-start.2 = ((bf16[8,128,512]{2,1,0:T(8,128)(2,1)}), bf16[8,128,512]{2,1,0:T(8,128)(2,1)S(1)}, u32[]{:S(2)}, u32[]{:S(2)}) async-start(bf16[8,128,512]{2,1,0:T(8,128)(2,1)} %bitcast.12), calls=%async_computation.2 | async-start | bytes 2097152 | tf_op jit(solution)/shard_map/all_to_all | solution.py:278
  41.4 10.4 %collective-permute-start.2 = (bf16[8,128,128]{2,1,0:T(8,128)(2,1)S(1)}, bf16[8,128,128]{2,1,0:T(8,128)(2,1)S(1)}, u32[]{:S(2)}, u32[]{:S(2)}) collective-permute-start(bf16[8,128,128]{2,1,0:T(8,128)(2,1)S(1)} %get-tuple-element.32.refs_2_.refs_4_), channel_id=1, source_target_pairs={{0,3},{1,0},{2,1},{3,2},{4,7},{5,4},{6,5},{7,6},{8,11},{9,8},{10,9... | collective-permute-start | bytes 786440 | tf_op jit(solution)/shard_map/ppermute | solution.py:285
  45.1 22.8 %collective-permute-start.1 = (bf16[8,128,128]{2,1,0:T(8,128)(2,1)S(1)}, bf16[8,128,128]{2,1,0:T(8,128)(2,1)S(1)}, u32[]{:S(2)}, u32[]{:S(2)}) collective-permute-start(bf16[8,128,128]{2,1,0:T(8,128)(2,1)S(1)} %get-tuple-element.32.refs_2_.refs_4_), channel_id=1, source_target_pairs={{0,2},{1,3},{2,0},{3,1},{4,6},{5,7},{6,4},{7,5},{8,10},{9,11},{10,... | collective-permute-start | bytes 786440 | tf_op jit(solution)/shard_map/ppermute | solution.py:285
  45.1 22.8 %collective-permute-start = (bf16[8,128,128]{2,1,0:T(8,128)(2,1)S(1)}, bf16[8,128,128]{2,1,0:T(8,128)(2,1)S(1)}, u32[]{:S(2)}, u32[]{:S(2)}) collective-permute-start(bf16[8,128,128]{2,1,0:T(8,128)(2,1)S(1)} %get-tuple-element.32.refs_2_.refs_4_), channel_id=1, source_target_pairs={{0,1},{1,2},{2,3},{3,0},{4,5},{5,6},{6,7},{7,4},{8,9},{9,10},{10,1... | collective-permute-start | bytes 786440 | tf_op jit(solution)/shard_map/ppermute | solution.py:285
  67.9 34.3 %collective-permute-start.5 = (bf16[8,128,128]{2,1,0:T(8,128)(2,1)S(1)}, bf16[8,128,128]{2,1,0:T(8,128)(2,1)}, u32[]{:S(2)}, u32[]{:S(2)}) collective-permute-start(bf16[8,128,128]{2,1,0:T(8,128)(2,1)S(1)} %get-tuple-element.41.refs_8_), channel_id=1, source_target_pairs={{0,3},{1,0},{2,1},{3,2},{4,7},{5,4},{6,5},{7,6},{8,11},{9,8},{10,9... | collective-permute-start | bytes 786440 | tf_op jit(solution)/shard_map/ppermute | solution.py:285
  68.0 34.3 %collective-permute-start.4 = (bf16[8,128,128]{2,1,0:T(8,128)(2,1)S(1)}, bf16[8,128,128]{2,1,0:T(8,128)(2,1)}, u32[]{:S(2)}, u32[]{:S(2)}) collective-permute-start(bf16[8,128,128]{2,1,0:T(8,128)(2,1)S(1)} %get-tuple-element.41.refs_8_), channel_id=1, source_target_pairs={{0,2},{1,3},{2,0},{3,1},{4,6},{5,7},{6,4},{7,5},{8,10},{9,11},{10,... | collective-permute-start | bytes 786440 | tf_op jit(solution)/shard_map/ppermute | solution.py:285
  70.7 31.6 %collective-permute-start.3 = (bf16[8,128,128]{2,1,0:T(8,128)(2,1)S(1)}, bf16[8,128,128]{2,1,0:T(8,128)(2,1)}, u32[]{:S(2)}, u32[]{:S(2)}) collective-permute-start(bf16[8,128,128]{2,1,0:T(8,128)(2,1)S(1)} %get-tuple-element.41.refs_8_), channel_id=1, source_target_pairs={{0,1},{1,2},{2,3},{3,0},{4,5},{5,6},{6,7},{7,4},{8,9},{9,10},{10,1... | collective-permute-start | bytes 786440 | tf_op jit(solution)/shard_map/ppermute | solution.py:285
  102.2 37.7 %copy-start.10 = (bf16[8,128,128]{2,1,0:T(8,128)(2,1)S(1)}, bf16[8,128,128]{2,1,0:T(8,128)(2,1)}, u32[]{:S(2)}) copy-start(bf16[8,128,128]{2,1,0:T(8,128)(2,1)} %get-tuple-element.48) | copy-start | bytes 786436
  102.2 39.0 %copy-start.9 = (bf16[8,128,128]{2,1,0:T(8,128)(2,1)S(1)}, bf16[8,128,128]{2,1,0:T(8,128)(2,1)}, u32[]{:S(2)}) copy-start(bf16[8,128,128]{2,1,0:T(8,128)(2,1)} %get-tuple-element.49) | copy-start | bytes 786436
  102.2 44.0 %copy-start.8 = (bf16[8,128,128]{2,1,0:T(8,128)(2,1)S(1)}, bf16[8,128,128]{2,1,0:T(8,128)(2,1)}, u32[]{:S(2)}) copy-start(bf16[8,128,128]{2,1,0:T(8,128)(2,1)} %get-tuple-element.50) | copy-start | bytes 786436
  102.3 75.7 %copy-start.7 = (bf16[8,128,128]{2,1,0:T(8,128)(2,1)S(1)}, bf16[8,128,128]{2,1,0:T(8,128)(2,1)}, u32[]{:S(2)}) copy-start(bf16[8,128,128]{2,1,0:T(8,128)(2,1)} %get-tuple-element.47) | copy-start | bytes 786436
  123.7 22.5 %collective-permute-start.6 = (bf16[8,128,128]{2,1,0:T(8,128)(2,1)}, bf16[8,128,128]{2,1,0:T(8,128)(2,1)S(1)}, u32[]{:S(2)}, u32[]{:S(2)}) collective-permute-start(bf16[8,128,128]{2,1,0:T(8,128)(2,1)} %get-tuple-element.44), channel_id=1, source_target_pairs={{0,1},{1,2},{2,3},{3,0},{4,5},{5,6},{6,7},{7,4},{8,9},{9,10},{10,1... | collective-permute-start | bytes 786440 | tf_op jit(solution)/shard_map/ppermute | solution.py:285
  123.8 33.7 %collective-permute-start.7 = (bf16[8,128,128]{2,1,0:T(8,128)(2,1)}, bf16[8,128,128]{2,1,0:T(8,128)(2,1)S(1)}, u32[]{:S(2)}, u32[]{:S(2)}) collective-permute-start(bf16[8,128,128]{2,1,0:T(8,128)(2,1)} %get-tuple-element.45), channel_id=1, source_target_pairs={{0,2},{1,3},{2,0},{3,1},{4,6},{5,7},{6,4},{7,5},{8,10},{9,11},{10,... | collective-permute-start | bytes 786440 | tf_op jit(solution)/shard_map/ppermute | solution.py:285
  139.2 20.5 %collective-permute-start.8 = (bf16[8,128,128]{2,1,0:T(8,128)(2,1)}, bf16[8,128,128]{2,1,0:T(8,128)(2,1)S(1)}, u32[]{:S(2)}, u32[]{:S(2)}) collective-permute-start(bf16[8,128,128]{2,1,0:T(8,128)(2,1)} %get-tuple-element.46), channel_id=1, source_target_pairs={{0,3},{1,0},{2,1},{3,2},{4,7},{5,4},{6,5},{7,6},{8,11},{9,8},{10,9... | collective-permute-start | bytes 786440 | tf_op jit(solution)/shard_map/ppermute | solution.py:285
  139.9 23.2 %collective-permute-start.9 = (bf16[8,128,128]{2,1,0:T(8,128)(2,1)S(1)}, bf16[8,128,128]{2,1,0:T(8,128)(2,1)S(1)}, u32[]{:S(2)}, u32[]{:S(2)}) collective-permute-start(bf16[8,128,128]{2,1,0:T(8,128)(2,1)S(1)} %copy-done.10), channel_id=1, source_target_pairs={{0,1},{1,2},{2,3},{3,0},{4,5},{5,6},{6,7},{7,4},{8,9},{9,10},{10,1... | collective-permute-start | bytes 786440 | tf_op jit(solution)/shard_map/ppermute | solution.py:285
  141.2 36.7 %collective-permute-start.10 = (bf16[8,128,128]{2,1,0:T(8,128)(2,1)S(1)}, bf16[8,128,128]{2,1,0:T(8,128)(2,1)S(1)}, u32[]{:S(2)}, u32[]{:S(2)}) collective-permute-start(bf16[8,128,128]{2,1,0:T(8,128)(2,1)S(1)} %copy-done.9), channel_id=1, source_target_pairs={{0,2},{1,3},{2,0},{3,1},{4,6},{5,7},{6,4},{7,5},{8,10},{9,11},{10,... | collective-permute-start | bytes 786440 | tf_op jit(solution)/shard_map/ppermute | solution.py:285
  146.2 31.8 %collective-permute-start.11 = (bf16[8,128,128]{2,1,0:T(8,128)(2,1)S(1)}, bf16[8,128,128]{2,1,0:T(8,128)(2,1)S(1)}, u32[]{:S(2)}, u32[]{:S(2)}) collective-permute-start(bf16[8,128,128]{2,1,0:T(8,128)(2,1)S(1)} %copy-done.8), channel_id=1, source_target_pairs={{0,3},{1,0},{2,1},{3,2},{4,7},{5,4},{6,5},{7,6},{8,11},{9,8},{10,9... | collective-permute-start | bytes 786440 | tf_op jit(solution)/shard_map/ppermute | solution.py:285
  191.7 18.9 %all-to-all-start.3 = ((bf16[8,128,512]{2,1,0:T(8,128)(2,1)}), bf16[8,128,512]{2,1,0:T(8,128)(2,1)S(1)}, u32[]{:S(2)}, u32[]{:S(2)}) async-start(bf16[8,128,512]{2,1,0:T(8,128)(2,1)} %get-tuple-element.42), calls=%async_computation.3 | async-start | bytes 2097152 | tf_op jit(solution)/shard_map/all_to_all | solution.py:278
  (4 other events, 31.6 us)

commit v3 on v1

v3 whole, which is shorter than its diff:
```python
import jax
import jax.numpy as jnp
from jax import lax
from jax.experimental import pallas as pl
from jax.experimental.pallas import tpu as pltpu
from jax.sharding import PartitionSpec as P

QUERY_HEAD_COUNT = 32
KEY_VALUE_HEADS = 8
GROUP = QUERY_HEAD_COUNT // KEY_VALUE_HEADS
HEAD_SIZE = 128
WINDOW = 4
TILES = 3 + 2 * (WINDOW - 1)
SCALE = HEAD_SIZE ** (-0.5)
LOG2_E = 1.4426950408889634
NT = (((1,), (1,)), ((), ()))
NN = (((1,), (0,)), ((), ()))
TN = (((0,), (0,)), ((), ()))
LOW = jnp.bfloat16
WIDE = jnp.float32
VMEM_LIMIT = 60 * 1024 * 1024
SCORE_BYTES = 24 * 1024 * 1024


def dot(a, b, dims):
    return lax.dot_general(a, b, dims, preferred_element_type=WIDE)


def fold(x, op):
    return op(x.reshape(x.shape[0] // 8, 8, x.shape[1]), axis=0)


def list_tiles(ids_ref, tile_ref):
    def slots(turn):
        first, second = ids_ref[2 * turn], ids_ref[2 * turn + 1]
        return jnp.where(first < second, 0, 1), jnp.minimum(first, second)

    def put(i, query_slot, turn, key_slot):
        tile_ref[3 * i] = query_slot
        tile_ref[3 * i + 1] = turn
        tile_ref[3 * i + 2] = key_slot

    low, stretch = slots(0)
    put(0, 0, 0, 0)
    put(1, 1, 0, 1)
    put(2, 1 - low, 0, low)
    for turn in range(1, WINDOW):
        key_low, key_stretch = slots(turn)
        later = stretch > key_stretch
        put(2 * turn + 1, 1 - low, turn, key_low)
        put(
            2 * turn + 2,
            jnp.where(later, low, 1 - low),
            turn,
            jnp.where(later, key_low, 1 - key_low),
        )


def attention_kernel(splits, heads, rows, at_once, head, ids_ref, *refs):
    chunk_ref, block_refs = refs[0], refs[1 : 1 + WINDOW]
    refs = refs[1 + WINDOW :]
    dq_out, dkv_outs = refs[0], refs[1 : 1 + WINDOW]
    (
        tile_ref, x_ref, kv_ref, qs_ref, gs_ref, st_ref, dp_ref, dqt_ref, dkv_ref,
        top_ref, total_ref, delta_ref, sem_ref,
    ) = refs[1 + WINDOW :]
    half = splits // 2
    stretch = half * rows
    width = at_once * stretch
    z = ids_ref[2 * WINDOW]
    step = pl.program_id(0) if heads > at_once else 0

    def place(block):
        return lax.rem(z - block + splits, splits)

    def lanes(h):
        return pl.ds(pl.multiple_of((step * at_once + h) * HEAD_SIZE, HEAD_SIZE), HEAD_SIZE)

    @pl.when(pl.program_id(0) == 0)
    def _():
        copies = [
            pltpu.make_async_copy(chunk_ref.at[s], x_ref.at[s], sem_ref.at[s])
            for s in range(splits)
        ]
        copies += [
            pltpu.make_async_copy(
                block.at[:, :, pl.ds(2 * head * HEAD_SIZE, 2 * HEAD_SIZE)],
                kv_ref.at[t],
                sem_ref.at[splits + t],
            )
            for t, block in enumerate(block_refs)
        ]
        for copy in copies:
            copy.start()
        list_tiles(ids_ref, tile_ref)
        dkv_ref[...] = jnp.zeros_like(dkv_ref)
        for copy in copies:
            copy.wait()

    for slot in range(2):
        for j in range(half):
            for h in range(at_once):
                at = pl.ds(h * stretch + j * rows, rows)
                qs_ref[slot, at] = x_ref[slot * half + j, 0, :, lanes(h)]
                gs_ref[slot, at] = x_ref[slot * half + j, 1, :, lanes(h)]

    def part(which):
        return pl.ds(which * HEAD_SIZE, HEAD_SIZE)

    def tile(i):
        return tile_ref[3 * i], tile_ref[3 * i + 1], tile_ref[3 * i + 2]

    def keys(which, turn, key_slot):
        return jnp.concatenate(
            [kv_ref[turn, place(key_slot * half + j), :, part(which)] for j in range(half)], axis=0
        )

    def add_keys(which, turn, key_slot, update):
        for j in range(half):
            at = place(key_slot * half + j)
            dkv_ref[turn, at, :, part(which)] += update[j * rows : (j + 1) * rows]

    key_pos = lax.broadcasted_iota(jnp.int32, (stretch, width), 0)
    row_pos = lax.rem(lax.broadcasted_iota(jnp.int32, (stretch, width), 1), stretch)
    for slot in range(2):
        s = jnp.where(key_pos <= row_pos, dot(keys(0, 0, slot), qs_ref[slot], NT), -1e30)
        st_ref[slot] = s
        top_ref[slot] = fold(s, jnp.max)

    def scores(i, carry):
        slot, turn, key_slot = tile(i)
        s = dot(keys(0, turn, key_slot), qs_ref[slot], NT)
        st_ref[i] = s
        top_ref[slot] = jnp.maximum(top_ref[slot], fold(s, jnp.max))
        return carry

    lax.fori_loop(2, TILES, scores, 0)
    top_ref[...] = jnp.broadcast_to(
        jnp.max(top_ref[...], axis=1, keepdims=True) * (SCALE * LOG2_E), top_ref.shape
    )
    total_ref[...] = jnp.zeros_like(total_ref)
    delta_ref[...] = jnp.zeros_like(delta_ref)
    dqt_ref[...] = jnp.zeros_like(dqt_ref)

    def weights(i, carry):
        slot, _, _ = tile(i)
        p = jnp.exp2(st_ref[i] * (SCALE * LOG2_E) - top_ref[slot, 0:1])
        st_ref[i] = p
        total_ref[slot] += fold(p, jnp.sum)
        return carry

    lax.fori_loop(0, TILES, weights, 0)
    total_ref[...] = jnp.broadcast_to(
        1.0 / jnp.sum(total_ref[...], axis=1, keepdims=True), total_ref.shape
    )

    def values(i, carry):
        slot, turn, key_slot = tile(i)
        p = st_ref[i] * total_ref[slot, 0:1]
        st_ref[i] = p
        dp = dot(keys(1, turn, key_slot), gs_ref[slot], NT)
        dp_ref[i] = dp
        add_keys(1, turn, key_slot, dot(p.astype(LOW), gs_ref[slot], NN))
        delta_ref[slot] += fold(p * dp, jnp.sum)
        return carry

    lax.fori_loop(0, TILES, values, 0)
    delta_ref[...] = jnp.broadcast_to(
        jnp.sum(delta_ref[...], axis=1, keepdims=True), delta_ref.shape
    )

    def grads(i, carry):
        slot, turn, key_slot = tile(i)
        ds = (st_ref[i] * (dp_ref[i] - delta_ref[slot, 0:1])).astype(LOW)
        add_keys(0, turn, key_slot, dot(ds, qs_ref[slot], NN))
        dqt_ref[slot] += dot(keys(0, turn, key_slot), ds, TN)
        return carry

    lax.fori_loop(0, TILES, grads, 0)

    for slot in range(2):
        dq = (dqt_ref[slot] * SCALE).T.astype(LOW)
        for j in range(half):
            for h in range(at_once):
                at = h * stretch + j * rows
                dq_out[slot * half + j, :, lanes(h)] = dq[at : at + rows]

    @pl.when(pl.program_id(0) == heads // at_once - 1)
    def _():
        for t, out in enumerate(dkv_outs):
            out[:, :, part(0)] = (dkv_ref[t, :, :, part(0)] * SCALE).astype(LOW)
            out[:, :, part(1)] = dkv_ref[t, :, :, part(1)].astype(LOW)


def attention(ids, chunk, blocks, head):
    splits, _, rows, lanes = chunk.shape
    heads = lanes // HEAD_SIZE
    stretch = splits // 2 * rows
    at_once = heads
    while 2 * TILES * 4 * stretch * stretch * at_once > SCORE_BYTES and at_once % 2 == 0:
        at_once //= 2
    width = at_once * stretch

    def kernel(*refs):
        attention_kernel(splits, heads, rows, at_once, head, *refs)

    def whole(shape):
        return pl.BlockSpec(shape, lambda i: (0,) * len(shape), pipeline_mode=pl.Buffered(1))

    dq_shape, dkv_shape = (splits, rows, lanes), (splits, rows, 2 * HEAD_SIZE)
    out = pl.pallas_call(
        kernel,
        grid=(heads // at_once,),
        in_specs=[pl.BlockSpec(memory_space=pltpu.SMEM)]
        + [pl.BlockSpec(memory_space=pl.ANY)] * (1 + WINDOW),
        out_specs=[whole(dq_shape)] + [whole(dkv_shape)] * WINDOW,
        out_shape=[jax.ShapeDtypeStruct(dq_shape, LOW)]
        + [jax.ShapeDtypeStruct(dkv_shape, LOW)] * WINDOW,
        scratch_shapes=[
            pltpu.SMEM((3 * TILES,), jnp.int32),
            pltpu.VMEM(chunk.shape, LOW),
            pltpu.VMEM((WINDOW, splits, rows, 2 * HEAD_SIZE), LOW),
            pltpu.VMEM((2, width, HEAD_SIZE), LOW),
            pltpu.VMEM((2, width, HEAD_SIZE), LOW),
            pltpu.VMEM((TILES, stretch, width), WIDE),
            pltpu.VMEM((TILES, stretch, width), WIDE),
            pltpu.VMEM((2, HEAD_SIZE, width), WIDE),
            pltpu.VMEM((WINDOW, splits, rows, 2 * HEAD_SIZE), WIDE),
            pltpu.VMEM((2, 8, width), WIDE),
            pltpu.VMEM((2, 8, width), WIDE),
            pltpu.VMEM((2, 8, width), WIDE),
            pltpu.SemaphoreType.DMA((splits + WINDOW,)),
        ],
        compiler_params=pltpu.CompilerParams(vmem_limit_bytes=VMEM_LIMIT),
        cost_estimate=pl.CostEstimate(
            flops=16 * 2 * 5 * TILES * stretch * stretch * heads * HEAD_SIZE // 4,
            bytes_accessed=1 << 22,
            transcendentals=0,
        ),
    )(ids, chunk, *blocks)
    return out[0], out[1:]


def in_columns(parts, z, places, outs):
    rows = parts[0].shape[-2]

    def kernel(z_ref, *refs):
        part_refs, out_refs = refs[: len(parts)], refs[len(parts) :]
        for index, part in enumerate(part_refs):
            for piece, out, column in places(z_ref[0], index, part):
                width = piece.shape[-1]
                start = pl.multiple_of(column * width, HEAD_SIZE)
                out_refs[out][:, pl.ds(start, width)] = piece

    size = sum(part.size for part in parts) // rows // outs
    return pl.pallas_call(
        kernel,
        in_specs=[pl.BlockSpec(memory_space=pltpu.SMEM)]
        + [pl.BlockSpec(memory_space=pltpu.VMEM)] * len(parts),
        out_specs=[pl.BlockSpec(memory_space=pltpu.VMEM)] * outs,
        out_shape=[jax.ShapeDtypeStruct((rows, size), LOW)] * outs,
        compiler_params=pltpu.CompilerParams(vmem_limit_bytes=VMEM_LIMIT),
    )(z.astype(jnp.int32)[None], *parts)


def body(query, key, value, d_out, stretch_ids):
    rows = query.shape[0]
    ranks = lax.axis_size("ctx")
    splits = lax.axis_size("head")
    local = KEY_VALUE_HEADS // splits
    z = lax.axis_index("head")
    rank = lax.axis_index("ctx")
    fence = lax.optimization_barrier

    def shift(array, axis, by):
        size = lax.axis_size(axis)
        return lax.ppermute(array, axis, [(i, (i + by) % size) for i in range(size)])

    def exchange(chunks, sign):
        return [chunks[0]] + [shift(chunks[s], "head", sign * s) for s in range(1, splits)]

    def swap(array):
        return lax.all_to_all(array, "head", split_axis=0, concat_axis=0, tiled=True)

    def ids_of(turn):
        source = lax.rem(rank - turn + ranks, ranks)
        return lax.dynamic_slice_in_dim(stretch_ids, 2 * source, 2)

    ids = jnp.concatenate([ids_of(t) for t in range(WINDOW)] + [z.astype(jnp.int32)[None]])

    def for_device_ahead(s):
        start = lax.rem(z + s, splits) * (local * HEAD_SIZE)
        ahead = [
            lax.dynamic_slice_in_dim(array, start, local * HEAD_SIZE, 1) for array in (key, value)
        ]
        return jnp.concatenate(
            [
                array[:, j * HEAD_SIZE : (j + 1) * HEAD_SIZE]
                for j in range(local)
                for array in ahead
            ],
            axis=1,
        )

    parts = exchange([for_device_ahead(s) for s in range(splits)], 1)
    both = [
        jnp.stack(
            [
                array.reshape(rows, splits, local, GROUP * HEAD_SIZE)[:, :, j].swapaxes(0, 1)
                for array in (query, d_out)
            ],
            axis=1,
        )
        for j in range(local)
    ]
    *both, parts = fence((*both, parts))

    blocks = [jnp.stack(parts)]
    for _ in range(1, WINDOW):
        blocks.append(shift(blocks[-1], "ctx", 1))
    chunks = []
    for j in range(local):
        if j > 0:
            both[j], chunks[j - 1], blocks = fence((both[j], chunks[j - 1], blocks))
        chunks.append(swap(both[j]))

    def home(dkv):
        return [dkv[0]] + [shift(dkv[t], "ctx", -t) for t in range(1, WINDOW)]

    def add(dkv):
        return sum(d.astype(WIDE) for d in dkv).astype(LOW)

    dq, dkv = [], []
    for j in range(local):
        dq_j, dkv_j = attention(ids, chunks[j], blocks, j)
        if j + 1 < local:
            dq_j, chunks[j + 1] = fence((dq_j, chunks[j + 1]))
        if j > 0:
            dq_j, dkv_j, dq[j - 1], dkv[j - 1] = fence((dq_j, dkv_j, dq[j - 1], dkv[j - 1]))
        dq.append(swap(dq_j))
        dkv.append(home(dkv_j))

    dkv = jnp.stack([add(d) for d in dkv], axis=1)
    dkv, dq[-1] = fence((dkv, dq[-1]))
    dkv = exchange(list(dkv), -1)
    dq = in_columns(
        dq, z, lambda z, j, part: [(part[g], 0, g * local + j) for g in range(splits)], 1
    )
    dq, dkv = fence((dq, dkv))
    dk, dv = in_columns(
        dkv,
        z,
        lambda z, s, part: [
            (
                part[j, :, i * HEAD_SIZE : (i + 1) * HEAD_SIZE],
                i,
                lax.rem(z + s, splits) * local + j,
            )
            for j in range(local)
            for i in range(2)
        ],
        2,
    )
    return dq[0], dk, dv


def solution(mesh):
    spec = P(("ctx", "head"), None)
    return jax.shard_map(
        body,
        mesh=mesh,
        in_specs=(spec, spec, spec, spec, P()),
        out_specs=(spec, spec, spec),
        check_vma=False,
    )
```

time: 180 us -> 140 us (0.78)
  the two profiles are of different devices: /device:TPU:0 before, /device:TPU:11 now
where the time goes in v3:
time: 140 us
  waiting for transfers between devices  48.1 us (34%)
  starting transfers between devices  43.8 us (31%)
  Pallas kernels  34.5 us (25%)
  local copies, waits for them, and re-layouts  9.07 us (6%)
  other arithmetic  3.03 us (2%)
    ppermute x15, waiting for transfers between devices, shift(): lax.ppermute(array, axis, [(i, (i + by) % size) for i in range(size)])  37.4 us
    pallas_call x2, Pallas kernels, attention(): pl.pallas_call(kernel, grid=(heads // at_once,), in_specs=[pl.BlockSpec(m...  30.3 us
    ppermute x15, starting transfers between devices, shift(): lax.ppermute(array, axis, [(i, (i + by) % size) for i in range(size)])  22.4 us
    all_to_all x4, starting transfers between devices, swap(): lax.all_to_all(array, 'head', split_axis=0, concat_axis=0, tiled=True)  21.4 us
    all_to_all x4, waiting for transfers between devices, swap(): lax.all_to_all(array, 'head', split_axis=0, concat_axis=0, tiled=True)  10.7 us
    unnamed x52, local copies, waits for them, and re-layouts  5.66 us
    pallas_call x2, Pallas kernels, in_columns(): pl.pallas_call(kernel, in_specs=[pl.BlockSpec(memory_space=pltpu.SMEM)] +...  4.22 us
  transfers between devices with their start and end apart: 19, of which 12 were waited for; matrix products, arithmetic and copies ran while one was open for 4% of the time, Pallas kernels for 23%

profile of v3, /device:TPU:11, one launch (start us, length us, event | category | flops | bytes accessed | tf_op | source)
XLA Modules:
  0.0 139.6 jit_solution(14124562139413657618)
XLA Ops:
  0.7 1.8 %constant_dynamic-slice_fusion = (bf16[128,128]{1,0:T(8,128)(2,1)S(1)}, bf16[128,128]{1,0:T(8,128)(2,1)S(1)}, bf16[128,128]{1,0:T(8,128)(2,1)S(1)}, bf16[128,128...) fusion(bf16[128,1024]{1,0:T(8,128)(2,1)} %param.7, ...), kind=kLoop, calls=%fused_computation.16 | loop fusion | bytes 1048608 | tf_op jit(solution)/shard_map/slice | solution.py:298
  11.2 3.2 %collective-permute-done.1 = bf16[128,512]{1,0:T(8,128)(2,1)} collective-permute-done((bf16[128,512]{1,0:T(8,128)(2,1)S(1)}, bf16[128,512]{1,0:T(8,128)(2,1)}, u32[]{:S(2)}, u32[]{:S(2)}) %collective-permute-start.1) | collective-permute-done | bytes 131104 | tf_op jit(solution)/shard_map/ppermute | solution.py:277
  14.4 2.9 %collective-permute-done.2 = bf16[128,512]{1,0:T(8,128)(2,1)} collective-permute-done((bf16[128,512]{1,0:T(8,128)(2,1)S(1)}, bf16[128,512]{1,0:T(8,128)(2,1)}, u32[]{:S(2)}, u32[]{:S(2)}) %collective-permute-start.2) | collective-permute-done | bytes 131104 | tf_op jit(solution)/shard_map/ppermute | solution.py:277
  20.1 3.8 %all-to-all-start = ((bf16[4,2,128,512]{3,2,1,0:T(8,128)(2,1)}), bf16[4,2,128,512]{3,2,1,0:T(8,128)(2,1)S(1)}, u32[]{:S(2)}, u32[]{:S(2)}) async-start(bf16[4,2,128,512]{3,2,1,0:T(8,128)(2,1)} %get-tuple-element.47), calls=%async_computation | async-start | bytes 2097152 | tf_op jit(solution)/shard_map/all_to_all | solution.py:283
  23.9 2.3 %collective-permute-done.3.refs_3_ = bf16[4,128,512]{2,1,0:T(8,128)(2,1)S(1)} collective-permute-done((bf16[4,128,512]{2,1,0:T(8,128)(2,1)S(1)}, bf16[4,128,512]{2,1,0:T(8,128)(2,1)S(1)}, u32[]{:S(2)}, u32[]{:S(2)}) %collective-permute-start.3) | collective-permute-done | bytes 524320 | tf_op jit(solution)/shard_map/ppermute | solution.py:277
  26.2 3.4 %collective-permute-start.4 = (bf16[4,128,512]{2,1,0:T(8,128)(2,1)S(1)}, bf16[4,128,512]{2,1,0:T(8,128)(2,1)S(1)}, u32[]{:S(2)}, u32[]{:S(2)}) collective-permute-start(bf16[4,128,512]{2,1,0:T(8,128)(2,1)S(1)} %collective-permute-done.3.refs_3_), channel_id=1, source_target_pairs={{0,4},{4,8},{8,12},{12,16},{16,20},{20,24},{24,28},{28,0},{1,5},{5... | collective-permute-start | bytes 1572872 | tf_op jit(solution)/shard_map/ppermute | solution.py:277
  29.6 6.1 %collective-permute-done.4.refs_4_ = bf16[4,128,512]{2,1,0:T(8,128)(2,1)S(1)} collective-permute-done((bf16[4,128,512]{2,1,0:T(8,128)(2,1)S(1)}, bf16[4,128,512]{2,1,0:T(8,128)(2,1)S(1)}, u32[]{:S(2)}, u32[]{:S(2)}) %collective-permute-start.4) | collective-permute-done | bytes 524320 | tf_op jit(solution)/shard_map/ppermute | solution.py:277
  35.7 3.4 %collective-permute-start.5 = (bf16[4,128,512]{2,1,0:T(8,128)(2,1)S(1)}, bf16[4,128,512]{2,1,0:T(8,128)(2,1)S(1)}, u32[]{:S(2)}, u32[]{:S(2)}) collective-permute-start(bf16[4,128,512]{2,1,0:T(8,128)(2,1)S(1)} %collective-permute-done.4.refs_4_), channel_id=1, source_target_pairs={{0,4},{4,8},{8,12},{12,16},{16,20},{20,24},{24,28},{28,0},{1,5},{5... | collective-permute-start | bytes 1572872 | tf_op jit(solution)/shard_map/ppermute | solution.py:277
  39.1 7.8 %all-to-all-done.refs_1_ = bf16[4,2,128,512]{3,2,1,0:T(8,128)(2,1)S(1)} async-done(((bf16[4,2,128,512]{3,2,1,0:T(8,128)(2,1)}), bf16[4,2,128,512]{3,2,1,0:T(8,128)(2,1)S(1)}, u32[]{:S(2)}, u32[]{:S(2)}) %all-to-all-start) | async-done | bytes 1048608 | tf_op jit(solution)/shard_map/all_to_all | solution.py:283
  48.0 6.5 %all-to-all-start.1 = ((bf16[4,2,128,512]{3,2,1,0:T(8,128)(2,1)}), bf16[4,2,128,512]{3,2,1,0:T(8,128)(2,1)S(1)}, u32[]{:S(2)}, u32[]{:S(2)}) async-start(bf16[4,2,128,512]{3,2,1,0:T(8,128)(2,1)} %get-tuple-element.58), calls=%async_computation.1 | async-start | bytes 2097152 | tf_op jit(solution)/shard_map/all_to_all | solution.py:283
  55.2 15.2 %shard_map.76 = (bf16[4,128,512]{2,1,0:T(8,128)(2,1)}, bf16[4,128,256]{2,1,0:T(8,128)(2,1)}, bf16[4,128,256]{2,1,0:T(8,128)(2,1)}, bf16[4,128,256]{2,1,0:T(8,128)(2,1)}, bf16[4,128,256]{2,1,0:T(8,128)(2,1)}) custom-call(s32[9]{0:T(128)} %concatenate.15.refs_0_, bf16[4,2,128,512]{3,2,1,0:T(8,128)(2,1)} %copy-done.5, bf16[4,128,512]{2,1,0:T(8,128)(2,1)} %copy-done.6, ...), custom_call_target="tpu_custom_call" | custom-call | flops 12079595520 | bytes 4194304 | tf_op jit(solution)/shard_map/pallas_call | solution.py:211
  71.7 2.0 %collective-permute-start.8 = (bf16[4,128,256]{2,1,0:T(8,128)(2,1)}, bf16[4,128,256]{2,1,0:T(8,128)(2,1)S(1)}, u32[]{:S(2)}, u32[]{:S(2)}) collective-permute-start(bf16[4,128,256]{2,1,0:T(8,128)(2,1)} %get-tuple-element.69), channel_id=1, source_target_pairs={{0,20},{4,24},{8,28},{12,0},{16,4},{20,8},{24,12},{28,16},{1,21},{... | collective-permute-start | bytes 786440 | tf_op jit(solution)/shard_map/ppermute | solution.py:277
  73.7 2.9 %all-to-all-done.1.refs_1_ = bf16[4,2,128,512]{3,2,1,0:T(8,128)(2,1)S(1)} async-done(((bf16[4,2,128,512]{3,2,1,0:T(8,128)(2,1)}), bf16[4,2,128,512]{3,2,1,0:T(8,128)(2,1)S(1)}, u32[]{:S(2)}, u32[]{:S(2)}) %all-to-all-start.1) | async-done | bytes 1048608 | tf_op jit(solution)/shard_map/all_to_all | solution.py:283
  76.6 6.6 %all-to-all-start.2 = ((bf16[4,128,512]{2,1,0:T(8,128)(2,1)}), bf16[4,128,512]{2,1,0:T(8,128)(2,1)S(1)}, u32[]{:S(2)}, u32[]{:S(2)}) async-start(bf16[4,128,512]{2,1,0:T(8,128)(2,1)} %get-tuple-element.65), calls=%async_computation.2 | async-start | bytes 1048576 | tf_op jit(solution)/shard_map/all_to_all | solution.py:283
  83.2 15.2 %shard_map.77 = (bf16[4,128,512]{2,1,0:T(8,128)(2,1)}, bf16[4,128,256]{2,1,0:T(8,128)(2,1)}, bf16[4,128,256]{2,1,0:T(8,128)(2,1)}, bf16[4,128,256]{2,1,0:T(8,128)(2,1)}, bf16[4,128,256]{2,1,0:T(8,128)(2,1)}) custom-call(s32[9]{0:T(128)} %concatenate.15.refs_0_, bf16[4,2,128,512]{3,2,1,0:T(8,128)(2,1)} %copy-done.4, bf16[4,128,512]{2,1,0:T(8,128)(2,1)} %copy-done.6, ...), custom_call_target="tpu_custom_call" | custom-call | flops 12079595520 | bytes 4194304 | tf_op jit(solution)/shard_map/pallas_call | solution.py:211
  99.2 4.5 %all-to-all-start.3 = ((bf16[4,128,512]{2,1,0:T(8,128)(2,1)}), bf16[4,128,512]{2,1,0:T(8,128)(2,1)S(1)}, u32[]{:S(2)}, u32[]{:S(2)}) async-start(bf16[4,128,512]{2,1,0:T(8,128)(2,1)} %get-tuple-element.79), calls=%async_computation.3 | async-start | bytes 1048576 | tf_op jit(solution)/shard_map/all_to_all | solution.py:283
  103.7 2.3 %collective-permute-start.9 = (bf16[4,128,256]{2,1,0:T(8,128)(2,1)S(1)}, bf16[4,128,256]{2,1,0:T(8,128)(2,1)S(1)}, u32[]{:S(2)}, u32[]{:S(2)}) collective-permute-start(bf16[4,128,256]{2,1,0:T(8,128)(2,1)S(1)} %copy-done.22), channel_id=1, source_target_pairs={{0,28},{4,0},{8,4},{12,8},{16,12},{20,16},{24,20},{28,24},{1,29},{... | collective-permute-start | bytes 786440 | tf_op jit(solution)/shard_map/ppermute | solution.py:277
  107.1 6.0 %collective-permute-done.9 = bf16[4,128,256]{2,1,0:T(8,128)(2,1)S(1)} collective-permute-done((bf16[4,128,256]{2,1,0:T(8,128)(2,1)S(1)}, bf16[4,128,256]{2,1,0:T(8,128)(2,1)S(1)}, u32[]{:S(2)}, u32[]{:S(2)}) %collective-permute-start.9) | collective-permute-done | bytes 262176 | tf_op jit(solution)/shard_map/ppermute | solution.py:277
  113.1 2.2 %collective-permute-done.10 = bf16[4,128,256]{2,1,0:T(8,128)(2,1)S(1)} collective-permute-done((bf16[4,128,256]{2,1,0:T(8,128)(2,1)S(1)}, bf16[4,128,256]{2,1,0:T(8,128)(2,1)S(1)}, u32[]{:S(2)}, u32[]{:S(2)}) %collective-permute-start.10) | collective-permute-done | bytes 262176 | tf_op jit(solution)/shard_map/ppermute | solution.py:277
  115.3 7.1 %collective-permute-done.11 = bf16[4,128,256]{2,1,0:T(8,128)(2,1)S(1)} collective-permute-done((bf16[4,128,256]{2,1,0:T(8,128)(2,1)S(1)}, bf16[4,128,256]{2,1,0:T(8,128)(2,1)S(1)}, u32[]{:S(2)}, u32[]{:S(2)}) %collective-permute-start.11) | collective-permute-done | bytes 262176 | tf_op jit(solution)/shard_map/ppermute | solution.py:277
  127.0 2.2 %shard_map.78 = bf16[128,4096]{1,0:T(8,128)(2,1)} custom-call(s32[1]{0:T(128)} %bitcast.z_ref, bf16[4,128,512]{2,1,0:T(8,128)(2,1)} %copy-done, bf16[4,128,512]{2,1,0:T(8,128)(2,1)} %copy-done.1), custom_call_target="tpu_custom_call" | custom-call | tf_op jit(solution)/shard_map/pallas_call | solution.py:256
  129.3 4.1 %collective-permute-done.14.refs_3_ = bf16[2,128,256]{2,1,0:T(8,128)(2,1)S(1)} collective-permute-done((bf16[2,128,256]{2,1,0:T(8,128)(2,1)S(1)}, bf16[2,128,256]{2,1,0:T(8,128)(2,1)S(1)}, u32[]{:S(2)}, u32[]{:S(2)}) %collective-permute-start.14) | collective-permute-done | bytes 131104 | tf_op jit(solution)/shard_map/ppermute | solution.py:277
  133.4 2.2 %collective-permute-done.13.refs_2_ = bf16[2,128,256]{2,1,0:T(8,128)(2,1)S(1)} collective-permute-done((bf16[2,128,256]{2,1,0:T(8,128)(2,1)S(1)}, bf16[2,128,256]{2,1,0:T(8,128)(2,1)S(1)}, u32[]{:S(2)}, u32[]{:S(2)}) %collective-permute-start.13) | collective-permute-done | bytes 131104 | tf_op jit(solution)/shard_map/ppermute | solution.py:277
  137.6 2.0 %shard_map.79 = (bf16[128,1024]{1,0:T(8,128)(2,1)}, bf16[128,1024]{1,0:T(8,128)(2,1)}) custom-call(s32[1]{0:T(128)} %bitcast.z_ref, bf16[2,128,256]{2,1,0:T(8,128)(2,1)} %get-tuple-element.83.refs_0_, bf16[2,128,256]{2,1,0:T(8,128)(2,1)} %copy-done.11, bf16[2,128,256]{2,1,0:T(8,128)(2,1)} %copy-done.10, bf16[2,128,256]{2,1,0:T(8,128)(2,1)} %copy-done.9), custom_call_target="tpu_custom_call" | custom-call | tf_op jit(solution)/shard_map/pallas_call | solution.py:256
  (85 shorter events, 23.1 us)
Async XLA Ops:
  2.5 8.8 %collective-permute-start = (bf16[128,512]{1,0:T(8,128)(2,1)S(1)}, bf16[128,512]{1,0:T(8,128)(2,1)}, u32[]{:S(2)}, u32[]{:S(2)}) collective-permute-start(bf16[128,512]{1,0:T(8,128)(2,1)S(1)} %pad_maximum_fusion.5), channel_id=1, source_target_pairs={{0,1},{1,2},{2,3},{3,0},{4,5},{5,6},{6,7},{7,4},{8,9},{9,10},{10,1... | collective-permute-start | bytes 393224 | tf_op jit(solution)/shard_map/ppermute | solution.py:277
  3.8 10.6 %collective-permute-start.1 = (bf16[128,512]{1,0:T(8,128)(2,1)S(1)}, bf16[128,512]{1,0:T(8,128)(2,1)}, u32[]{:S(2)}, u32[]{:S(2)}) collective-permute-start(bf16[128,512]{1,0:T(8,128)(2,1)S(1)} %pad_maximum_fusion.6), channel_id=1, source_target_pairs={{0,2},{1,3},{2,0},{3,1},{4,6},{5,7},{6,4},{7,5},{8,10},{9,11},{10,... | collective-permute-start | bytes 393224 | tf_op jit(solution)/shard_map/ppermute | solution.py:277
  5.0 12.4 %collective-permute-start.2 = (bf16[128,512]{1,0:T(8,128)(2,1)S(1)}, bf16[128,512]{1,0:T(8,128)(2,1)}, u32[]{:S(2)}, u32[]{:S(2)}) collective-permute-start(bf16[128,512]{1,0:T(8,128)(2,1)S(1)} %pad_maximum_fusion.7), channel_id=1, source_target_pairs={{0,3},{1,0},{2,1},{3,2},{4,7},{5,4},{6,5},{7,6},{8,11},{9,8},{10,9... | collective-permute-start | bytes 393224 | tf_op jit(solution)/shard_map/ppermute | solution.py:277
  18.4 7.8 %collective-permute-start.3 = (bf16[4,128,512]{2,1,0:T(8,128)(2,1)S(1)}, bf16[4,128,512]{2,1,0:T(8,128)(2,1)S(1)}, u32[]{:S(2)}, u32[]{:S(2)}) collective-permute-start(bf16[4,128,512]{2,1,0:T(8,128)(2,1)S(1)} %pad_maximum_fusion.2.refs_2_), channel_id=1, source_target_pairs={{0,4},{4,8},{8,12},{12,16},{16,20},{20,24},{24,28},{28,0},{1,5},{5... | collective-permute-start | bytes 1572872 | tf_op jit(solution)/shard_map/ppermute | solution.py:277
  20.1 26.8 %all-to-all-start = ((bf16[4,2,128,512]{3,2,1,0:T(8,128)(2,1)}), bf16[4,2,128,512]{3,2,1,0:T(8,128)(2,1)S(1)}, u32[]{:S(2)}, u32[]{:S(2)}) async-start(bf16[4,2,128,512]{3,2,1,0:T(8,128)(2,1)} %get-tuple-element.47), calls=%async_computation | async-start | bytes 2097152 | tf_op jit(solution)/shard_map/all_to_all | solution.py:283
  26.2 20.7 %copy-start.17 = (bf16[4,128,512]{2,1,0:T(8,128)(2,1)}, bf16[4,128,512]{2,1,0:T(8,128)(2,1)S(1)}, u32[]{:S(2)}) copy-start(bf16[4,128,512]{2,1,0:T(8,128)(2,1)S(1)} %collective-permute-done.3.refs_3_) | copy-start | bytes 1572868
  26.2 9.5 %collective-permute-start.4 = (bf16[4,128,512]{2,1,0:T(8,128)(2,1)S(1)}, bf16[4,128,512]{2,1,0:T(8,128)(2,1)S(1)}, u32[]{:S(2)}, u32[]{:S(2)}) collective-permute-start(bf16[4,128,512]{2,1,0:T(8,128)(2,1)S(1)} %collective-permute-done.3.refs_3_), channel_id=1, source_target_pairs={{0,4},{4,8},{8,12},{12,16},{16,20},{20,24},{24,28},{28,0},{1,5},{5... | collective-permute-start | bytes 1572872 | tf_op jit(solution)/shard_map/ppermute | solution.py:277
  35.7 12.0 %copy-start.18 = (bf16[4,128,512]{2,1,0:T(8,128)(2,1)}, bf16[4,128,512]{2,1,0:T(8,128)(2,1)S(1)}, u32[]{:S(2)}) copy-start(bf16[4,128,512]{2,1,0:T(8,128)(2,1)S(1)} %collective-permute-done.4.refs_4_) | copy-start | bytes 1572868
  35.7 11.2 %collective-permute-start.5 = (bf16[4,128,512]{2,1,0:T(8,128)(2,1)S(1)}, bf16[4,128,512]{2,1,0:T(8,128)(2,1)S(1)}, u32[]{:S(2)}, u32[]{:S(2)}) collective-permute-start(bf16[4,128,512]{2,1,0:T(8,128)(2,1)S(1)} %collective-permute-done.4.refs_4_), channel_id=1, source_target_pairs={{0,4},{4,8},{8,12},{12,16},{16,20},{20,24},{24,28},{28,0},{1,5},{5... | collective-permute-start | bytes 1572872 | tf_op jit(solution)/shard_map/ppermute | solution.py:277
  48.0 28.6 %all-to-all-start.1 = ((bf16[4,2,128,512]{3,2,1,0:T(8,128)(2,1)}), bf16[4,2,128,512]{3,2,1,0:T(8,128)(2,1)S(1)}, u32[]{:S(2)}, u32[]{:S(2)}) async-start(bf16[4,2,128,512]{3,2,1,0:T(8,128)(2,1)} %get-tuple-element.58), calls=%async_computation.1 | async-start | bytes 2097152 | tf_op jit(solution)/shard_map/all_to_all | solution.py:283
  70.4 27.9 %collective-permute-start.6 = (bf16[4,128,256]{2,1,0:T(8,128)(2,1)}, bf16[4,128,256]{2,1,0:T(8,128)(2,1)S(1)}, u32[]{:S(2)}, u32[]{:S(2)}) collective-permute-start(bf16[4,128,256]{2,1,0:T(8,128)(2,1)} %get-tuple-element.67), channel_id=1, source_target_pairs={{0,28},{4,0},{8,4},{12,8},{16,12},{20,16},{24,20},{28,24},{1,29},{... | collective-permute-start | bytes 786440 | tf_op jit(solution)/shard_map/ppermute | solution.py:277
  71.5 26.9 %collective-permute-start.7 = (bf16[4,128,256]{2,1,0:T(8,128)(2,1)}, bf16[4,128,256]{2,1,0:T(8,128)(2,1)S(1)}, u32[]{:S(2)}, u32[]{:S(2)}) collective-permute-start(bf16[4,128,256]{2,1,0:T(8,128)(2,1)} %get-tuple-element.68), channel_id=1, source_target_pairs={{0,24},{4,28},{8,0},{12,4},{16,8},{20,12},{24,16},{28,20},{1,25},{... | collective-permute-start | bytes 786440 | tf_op jit(solution)/shard_map/ppermute | solution.py:277
  71.7 26.7 %collective-permute-start.8 = (bf16[4,128,256]{2,1,0:T(8,128)(2,1)}, bf16[4,128,256]{2,1,0:T(8,128)(2,1)S(1)}, u32[]{:S(2)}, u32[]{:S(2)}) collective-permute-start(bf16[4,128,256]{2,1,0:T(8,128)(2,1)} %get-tuple-element.69), channel_id=1, source_target_pairs={{0,20},{4,24},{8,28},{12,0},{16,4},{20,8},{24,12},{28,16},{1,21},{... | collective-permute-start | bytes 786440 | tf_op jit(solution)/shard_map/ppermute | solution.py:277
  76.6 21.8 %all-to-all-start.2 = ((bf16[4,128,512]{2,1,0:T(8,128)(2,1)}), bf16[4,128,512]{2,1,0:T(8,128)(2,1)S(1)}, u32[]{:S(2)}, u32[]{:S(2)}) async-start(bf16[4,128,512]{2,1,0:T(8,128)(2,1)} %get-tuple-element.65), calls=%async_computation.2 | async-start | bytes 1048576 | tf_op jit(solution)/shard_map/all_to_all | solution.py:283
  98.4 7.8 %copy-start.20 = (bf16[4,128,256]{2,1,0:T(8,128)(2,1)S(1)}, bf16[4,128,256]{2,1,0:T(8,128)(2,1)}, u32[]{:S(2)}) copy-start(bf16[4,128,256]{2,1,0:T(8,128)(2,1)} %get-tuple-element.78) | copy-start | bytes 786436
  98.4 8.6 %copy-start.7 = (bf16[4,128,256]{2,1,0:T(8,128)(2,1)S(1)}, bf16[4,128,256]{2,1,0:T(8,128)(2,1)}, u32[]{:S(2)}) copy-start(bf16[4,128,256]{2,1,0:T(8,128)(2,1)} %get-tuple-element.71) | copy-start | bytes 786436
  99.2 23.4 %all-to-all-start.3 = ((bf16[4,128,512]{2,1,0:T(8,128)(2,1)}), bf16[4,128,512]{2,1,0:T(8,128)(2,1)S(1)}, u32[]{:S(2)}, u32[]{:S(2)}) async-start(bf16[4,128,512]{2,1,0:T(8,128)(2,1)} %get-tuple-element.79), calls=%async_computation.3 | async-start | bytes 1048576 | tf_op jit(solution)/shard_map/all_to_all | solution.py:283
  103.7 18.7 %copy-start.8 = (bf16[4,128,256]{2,1,0:T(8,128)(2,1)S(1)}, bf16[4,128,256]{2,1,0:T(8,128)(2,1)}, u32[]{:S(2)}) copy-start(bf16[4,128,256]{2,1,0:T(8,128)(2,1)} %get-tuple-element.75) | copy-start | bytes 786436
  103.7 9.3 %collective-permute-start.9 = (bf16[4,128,256]{2,1,0:T(8,128)(2,1)S(1)}, bf16[4,128,256]{2,1,0:T(8,128)(2,1)S(1)}, u32[]{:S(2)}, u32[]{:S(2)}) collective-permute-start(bf16[4,128,256]{2,1,0:T(8,128)(2,1)S(1)} %copy-done.22), channel_id=1, source_target_pairs={{0,28},{4,0},{8,4},{12,8},{16,12},{20,16},{24,20},{28,24},{1,29},{... | collective-permute-start | bytes 786440 | tf_op jit(solution)/shard_map/ppermute | solution.py:277
  106.0 9.3 %collective-permute-start.10 = (bf16[4,128,256]{2,1,0:T(8,128)(2,1)S(1)}, bf16[4,128,256]{2,1,0:T(8,128)(2,1)S(1)}, u32[]{:S(2)}, u32[]{:S(2)}) collective-permute-start(bf16[4,128,256]{2,1,0:T(8,128)(2,1)S(1)} %copy-done.21), channel_id=1, source_target_pairs={{0,24},{4,28},{8,0},{12,4},{16,8},{20,12},{24,16},{28,20},{1,25},{... | collective-permute-start | bytes 786440 | tf_op jit(solution)/shard_map/ppermute | solution.py:277
  106.3 16.1 %collective-permute-start.11 = (bf16[4,128,256]{2,1,0:T(8,128)(2,1)S(1)}, bf16[4,128,256]{2,1,0:T(8,128)(2,1)S(1)}, u32[]{:S(2)}, u32[]{:S(2)}) collective-permute-start(bf16[4,128,256]{2,1,0:T(8,128)(2,1)S(1)} %copy-done.20), channel_id=1, source_target_pairs={{0,20},{4,24},{8,28},{12,0},{16,4},{20,8},{24,12},{28,16},{1,21},{... | collective-permute-start | bytes 786440 | tf_op jit(solution)/shard_map/ppermute | solution.py:277
  123.5 9.9 %collective-permute-start.14 = (bf16[2,128,256]{2,1,0:T(8,128)(2,1)S(1)}, bf16[2,128,256]{2,1,0:T(8,128)(2,1)S(1)}, u32[]{:S(2)}, u32[]{:S(2)}) collective-permute-start(bf16[2,128,256]{2,1,0:T(8,128)(2,1)S(1)} %get-tuple-element.93), channel_id=1, source_target_pairs={{0,1},{1,2},{2,3},{3,0},{4,5},{5,6},{6,7},{7,4},{8,9},{9,10},{10,1... | collective-permute-start | bytes 393224 | tf_op jit(solution)/shard_map/ppermute | solution.py:277
  124.7 10.9 %collective-permute-start.13 = (bf16[2,128,256]{2,1,0:T(8,128)(2,1)S(1)}, bf16[2,128,256]{2,1,0:T(8,128)(2,1)S(1)}, u32[]{:S(2)}, u32[]{:S(2)}) collective-permute-start(bf16[2,128,256]{2,1,0:T(8,128)(2,1)S(1)} %get-tuple-element.94), channel_id=1, source_target_pairs={{0,2},{1,3},{2,0},{3,1},{4,6},{5,7},{6,4},{7,5},{8,10},{9,11},{10,... | collective-permute-start | bytes 393224 | tf_op jit(solution)/shard_map/ppermute | solution.py:277
  125.6 11.4 %collective-permute-start.12 = (bf16[2,128,256]{2,1,0:T(8,128)(2,1)S(1)}, bf16[2,128,256]{2,1,0:T(8,128)(2,1)S(1)}, u32[]{:S(2)}, u32[]{:S(2)}) collective-permute-start(bf16[2,128,256]{2,1,0:T(8,128)(2,1)S(1)} %get-tuple-element.95), channel_id=1, source_target_pairs={{0,3},{1,0},{2,1},{3,2},{4,7},{5,4},{6,5},{7,6},{8,11},{9,8},{10,9... | collective-permute-start | bytes 393224 | tf_op jit(solution)/shard_map/ppermute | solution.py:277
  (18 other events, 51.3 us)

commit v4 on v3

--- a/solution.py
+++ b/solution.py
@@ -56,14 +56,15 @@
         )
 
 
-def attention_kernel(splits, heads, rows, at_once, head, ids_ref, *refs):
-    chunk_ref, block_refs = refs[0], refs[1 : 1 + WINDOW]
-    refs = refs[1 + WINDOW :]
-    dq_out, dkv_outs = refs[0], refs[1 : 1 + WINDOW]
+def attention_kernel(splits, heads, rows, at_once, head, came_apart, go_apart, ids_ref, *refs):
+    parts_in, parts_out = splits if came_apart else 1, splits if go_apart else 1
+    chunk_refs, block_refs = refs[:parts_in], refs[parts_in : parts_in + WINDOW]
+    refs = refs[parts_in + WINDOW :]
+    dq_outs, dkv_outs = refs[:parts_out], refs[parts_out : parts_out + WINDOW]
     (
         tile_ref, x_ref, kv_ref, qs_ref, gs_ref, st_ref, dp_ref, dqt_ref, dkv_ref,
         top_ref, total_ref, delta_ref, sem_ref,
-    ) = refs[1 + WINDOW :]
+    ) = refs[parts_out + WINDOW :]
     half = splits // 2
     stretch = half * rows
     width = at_once * stretch
@@ -79,7 +80,9 @@
     @pl.when(pl.program_id(0) == 0)
     def _():
         copies = [
-            pltpu.make_async_copy(chunk_ref.at[s], x_ref.at[s], sem_ref.at[s])
+            pltpu.make_async_copy(
+                chunk_refs[s] if came_apart else chunk_refs[0].at[s], x_ref.at[s], sem_ref.at[s]
+            )
             for s in range(splits)
         ]
         copies += [
@@ -101,8 +104,10 @@
         for j in range(half):
             for h in range(at_once):
                 at = pl.ds(h * stretch + j * rows, rows)
-                qs_ref[slot, at] = x_ref[slot * half + j, 0, :, lanes(h)]
-                gs_ref[slot, at] = x_ref[slot * half + j, 1, :, lanes(h)]
+                block = slot * half + j
+                s = place(block) if came_apart else block
+                qs_ref[slot, at] = x_ref[s, 0, :, lanes(h)]
+                gs_ref[slot, at] = x_ref[s, 1, :, lanes(h)]
 
     def part(which):
         return pl.ds(which * HEAD_SIZE, HEAD_SIZE)
@@ -134,7 +139,7 @@
         top_ref[slot] = jnp.maximum(top_ref[slot], fold(s, jnp.max))
         return carry
 
-    lax.fori_loop(2, TILES, scores, 0)
+    lax.fori_loop(2, TILES, scores, 0, unroll=TILES - 2)
     top_ref[...] = jnp.broadcast_to(
         jnp.max(top_ref[...], axis=1, keepdims=True) * (SCALE * LOG2_E), top_ref.shape
     )
@@ -143,57 +148,59 @@
     dqt_ref[...] = jnp.zeros_like(dqt_ref)
 
     def weights(i, carry):
-        slot, _, _ = tile(i)
+        slot, turn, key_slot = tile(i)
         p = jnp.exp2(st_ref[i] * (SCALE * LOG2_E) - top_ref[slot, 0:1])
         st_ref[i] = p
         total_ref[slot] += fold(p, jnp.sum)
+        dp = dot(keys(1, turn, key_slot), gs_ref[slot], NT)
+        dp_ref[i] = dp
+        delta_ref[slot] += fold(p * dp, jnp.sum)
         return carry
 
-    lax.fori_loop(0, TILES, weights, 0)
+    lax.fori_loop(0, TILES, weights, 0, unroll=3)
     total_ref[...] = jnp.broadcast_to(
         1.0 / jnp.sum(total_ref[...], axis=1, keepdims=True), total_ref.shape
     )
-
-    def values(i, carry):
+    delta_ref[...] = jnp.broadcast_to(
+        jnp.sum(delta_ref[...], axis=1, keepdims=True) * total_ref[...], delta_ref.shape
+    )
+
+    def grads(i, carry):
         slot, turn, key_slot = tile(i)
         p = st_ref[i] * total_ref[slot, 0:1]
-        st_ref[i] = p
-        dp = dot(keys(1, turn, key_slot), gs_ref[slot], NT)
-        dp_ref[i] = dp
+        ds = (p * (dp_ref[i] - delta_ref[slot, 0:1])).astype(LOW)
         add_keys(1, turn, key_slot, dot(p.astype(LOW), gs_ref[slot], NN))
-        delta_ref[slot] += fold(p * dp, jnp.sum)
-        return carry
-
-    lax.fori_loop(0, TILES, values, 0)
-    delta_ref[...] = jnp.broadcast_to(
-        jnp.sum(delta_ref[...], axis=1, keepdims=True), delta_ref.shape
-    )
-
-    def grads(i, carry):
-        slot, turn, key_slot = tile(i)
-        ds = (st_ref[i] * (dp_ref[i] - delta_ref[slot, 0:1])).astype(LOW)
         add_keys(0, turn, key_slot, dot(ds, qs_ref[slot], NN))
         dqt_ref[slot] += dot(keys(0, turn, key_slot), ds, TN)
         return carry
 
-    lax.fori_loop(0, TILES, grads, 0)
+    lax.fori_loop(0, TILES, grads, 0, unroll=TILES)
 
     for slot in range(2):
         dq = (dqt_ref[slot] * SCALE).T.astype(LOW)
         for j in range(half):
             for h in range(at_once):
                 at = h * stretch + j * rows
-                dq_out[slot * half + j, :, lanes(h)] = dq[at : at + rows]
+                block = slot * half + j
+                s = place(block) if go_apart else block
+                x_ref[s, 0, :, lanes(h)] = dq[at : at + rows]
 
     @pl.when(pl.program_id(0) == heads // at_once - 1)
     def _():
+        for s in range(splits):
+            if go_apart:
+                dq_outs[s][...] = x_ref[s, 0]
+            else:
+                dq_outs[0][s] = x_ref[s, 0]
         for t, out in enumerate(dkv_outs):
             out[:, :, part(0)] = (dkv_ref[t, :, :, part(0)] * SCALE).astype(LOW)
             out[:, :, part(1)] = dkv_ref[t, :, :, part(1)].astype(LOW)
 
 
-def attention(ids, chunk, blocks, head):
-    splits, _, rows, lanes = chunk.shape
+def attention(ids, chunk, blocks, head, go_apart):
+    came_apart = isinstance(chunk, list)
+    splits = len(chunk)
+    _, rows, lanes = chunk[0].shape
     heads = lanes // HEAD_SIZE
     stretch = splits // 2 * rows
     at_once = heads
@@ -202,23 +209,25 @@
     width = at_once * stretch
 
     def kernel(*refs):
-        attention_kernel(splits, heads, rows, at_once, head, *refs)
+        attention_kernel(splits, heads, rows, at_once, head, came_apart, go_apart, *refs)
 
     def whole(shape):
         return pl.BlockSpec(shape, lambda i: (0,) * len(shape), pipeline_mode=pl.Buffered(1))
 
-    dq_shape, dkv_shape = (splits, rows, lanes), (splits, rows, 2 * HEAD_SIZE)
+    chunk = chunk if came_apart else [chunk]
+    dq_shapes = [(rows, lanes)] * splits if go_apart else [(splits, rows, lanes)]
+    dkv_shape = (splits, rows, 2 * HEAD_SIZE)
     out = pl.pallas_call(
         kernel,
         grid=(heads // at_once,),
         in_specs=[pl.BlockSpec(memory_space=pltpu.SMEM)]
-        + [pl.BlockSpec(memory_space=pl.ANY)] * (1 + WINDOW),
-        out_specs=[whole(dq_shape)] + [whole(dkv_shape)] * WINDOW,
-        out_shape=[jax.ShapeDtypeStruct(dq_shape, LOW)]
+        + [pl.BlockSpec(memory_space=pl.ANY)] * (len(chunk) + WINDOW),
+        out_specs=[whole(shape) for shape in dq_shapes] + [whole(dkv_shape)] * WINDOW,
+        out_shape=[jax.ShapeDtypeStruct(shape, LOW) for shape in dq_shapes]
         + [jax.ShapeDtypeStruct(dkv_shape, LOW)] * WINDOW,
         scratch_shapes=[
             pltpu.SMEM((3 * TILES,), jnp.int32),
-            pltpu.VMEM(chunk.shape, LOW),
+            pltpu.VMEM((splits, 2, rows, lanes), LOW),
             pltpu.VMEM((WINDOW, splits, rows, 2 * HEAD_SIZE), LOW),
             pltpu.VMEM((2, width, HEAD_SIZE), LOW),
             pltpu.VMEM((2, width, HEAD_SIZE), LOW),
@@ -237,8 +246,8 @@
             bytes_accessed=1 << 22,
             transcendentals=0,
         ),
-    )(ids, chunk, *blocks)
-    return out[0], out[1:]
+    )(ids, *chunk, *blocks)
+    return out[:splits] if go_apart else out[0], out[-WINDOW:]
 
 
 def in_columns(parts, z, places, outs):
@@ -303,26 +312,35 @@
         )
 
     parts = exchange([for_device_ahead(s) for s in range(splits)], 1)
-    both = [
-        jnp.stack(
-            [
-                array.reshape(rows, splits, local, GROUP * HEAD_SIZE)[:, :, j].swapaxes(0, 1)
-                for array in (query, d_out)
-            ],
-            axis=1,
-        )
-        for j in range(local)
-    ]
+    def in_order(j):
+        split = [
+            array.reshape(rows, splits, local, GROUP * HEAD_SIZE)[:, :, j].swapaxes(0, 1)
+            for array in (query, d_out)
+        ]
+        return jnp.stack(split, axis=1)
+
+    def apart(j):
+        start = [(lax.rem(z + s, splits) * local + j) * GROUP * HEAD_SIZE for s in range(splits)]
+        return [
+            jnp.stack(
+                [
+                    lax.dynamic_slice_in_dim(array, at, GROUP * HEAD_SIZE, 1)
+                    for array in (query, d_out)
+                ]
+            )
+            for at in start
+        ]
+
+    both = [in_order(0)] + [apart(j) for j in range(1, local)]
     *both, parts = fence((*both, parts))
 
     blocks = [jnp.stack(parts)]
     for _ in range(1, WINDOW):
         blocks.append(shift(blocks[-1], "ctx", 1))
-    chunks = []
-    for j in range(local):
-        if j > 0:
-            both[j], chunks[j - 1], blocks = fence((both[j], chunks[j - 1], blocks))
-        chunks.append(swap(both[j]))
+    chunks = [swap(both[0])]
+    for j in range(1, local):
+        both[j], chunks[j - 1] = fence((both[j], chunks[j - 1]))
+        chunks.append(exchange(both[j], 1))
 
     def home(dkv):
         return [dkv[0]] + [shift(dkv[t], "ctx", -t) for t in range(1, WINDOW)]
@@ -332,19 +350,35 @@
 
     dq, dkv = [], []
     for j in range(local):
-        dq_j, dkv_j = attention(ids, chunks[j], blocks, j)
-        if j + 1 < local:
-            dq_j, chunks[j + 1] = fence((dq_j, chunks[j + 1]))
+        last = j > 0 and j == local - 1
+        dq_j, dkv_j = attention(ids, chunks[j], blocks, j, last)
         if j > 0:
-            dq_j, dkv_j, dq[j - 1], dkv[j - 1] = fence((dq_j, dkv_j, dq[j - 1], dkv[j - 1]))
-        dq.append(swap(dq_j))
+            dkv_j, dkv[j - 1] = fence((dkv_j, dkv[j - 1]))
+            dq_j, dq[j - 1] = fence((dq_j, dq[j - 1]))
+        dq.append(exchange(dq_j, -1) if last else swap(dq_j))
         dkv.append(home(dkv_j))
 
     dkv = jnp.stack([add(d) for d in dkv], axis=1)
     dkv, dq[-1] = fence((dkv, dq[-1]))
     dkv = exchange(list(dkv), -1)
+    columns, pieces = [], []
+    for j, part in enumerate(dq):
+        if isinstance(part, list):
+            columns += [[(s, j, None)] for s in range(splits)]
+            pieces += part
+        else:
+            columns.append([(g, j, g) for g in range(splits)])
+            pieces.append(part)
     dq = in_columns(
-        dq, z, lambda z, j, part: [(part[g], 0, g * local + j) for g in range(splits)], 1
+        pieces,
+        z,
+        lambda z, index, part: [
+            (part[...], 0, lax.rem(z + s, splits) * local + j)
+            if g is None
+            else (part[g], 0, g * local + j)
+            for s, j, g in columns[index]
+        ],
+        1,
     )
     dq, dkv = fence((dq, dkv))
     dk, dv = in_columns(

time: 140 us -> 124 us (0.89)
  the two profiles are of different devices: /device:TPU:11 before, /device:TPU:0 now
where the time goes in v4:
time: 124 us
  waiting for transfers between devices  42.5 us (34%)
  starting transfers between devices  39.9 us (32%)
  Pallas kernels  25.7 us (21%)
  local copies, waits for them, and re-layouts  11.3 us (9%)
  other arithmetic  3.36 us (3%)
    ppermute x21, waiting for transfers between devices, shift(): lax.ppermute(array, axis, [(i, (i + by) % size) for i in range(size)])  38.3 us
    ppermute x21, starting transfers between devices, shift(): lax.ppermute(array, axis, [(i, (i + by) % size) for i in range(size)])  31.2 us
    pallas_call x2, Pallas kernels, attention(): pl.pallas_call(kernel, grid=(heads // at_once,), in_specs=[pl.BlockSpec(m...  21.4 us
    all_to_all x2, starting transfers between devices, swap(): lax.all_to_all(array, 'head', split_axis=0, concat_axis=0, tiled=True)  8.73 us
    unnamed x58, local copies, waits for them, and re-layouts  6.37 us
    pallas_call x2, Pallas kernels, in_columns(): pl.pallas_call(kernel, in_specs=[pl.BlockSpec(memory_space=pltpu.SMEM)] +...  4.26 us
    all_to_all x2, waiting for transfers between devices, swap(): lax.all_to_all(array, 'head', split_axis=0, concat_axis=0, tiled=True)  4.13 us
  transfers between devices with their start and end apart: 23, of which 8 were waited for; matrix products, arithmetic and copies ran while one was open for 8% of the time, Pallas kernels for 19%

profile of v4, /device:TPU:0, one launch (start us, length us, event | category | flops | bytes accessed | tf_op | source)
XLA Modules:
  0.0 123.9 jit_solution(10726591514938165622)
XLA Ops:
  0.7 1.8 %constant_dynamic-slice_fusion = (bf16[128,128]{1,0:T(8,128)(2,1)S(1)}, bf16[128,128]{1,0:T(8,128)(2,1)S(1)}, bf16[128,128]{1,0:T(8,128)(2,1)S(1)}, bf16[128,128...) fusion(bf16[128,1024]{1,0:T(8,128)(2,1)} %param.7, ...), kind=kLoop, calls=%fused_computation.27 | loop fusion | bytes 1048608 | tf_op jit(solution)/shard_map/slice | solution.py:307
  2.5 3.1 %collective-permute-start = (bf16[128,512]{1,0:T(8,128)(2,1)S(1)}, bf16[128,512]{1,0:T(8,128)(2,1)}, u32[]{:S(2)}, u32[]{:S(2)}) collective-permute-start(bf16[128,512]{1,0:T(8,128)(2,1)S(1)} %pad_maximum_fusion.8), channel_id=1, source_target_pairs={{0,1},{1,2},{2,3},{3,0},{4,5},{5,6},{6,7},{7,4},{8,9},{9,10},{10,1... | collective-permute-start | bytes 393224 | tf_op jit(solution)/shard_map/ppermute | solution.py:286
  5.6 2.7 %collective-permute-start.1 = (bf16[128,512]{1,0:T(8,128)(2,1)S(1)}, bf16[128,512]{1,0:T(8,128)(2,1)}, u32[]{:S(2)}, u32[]{:S(2)}) collective-permute-start(bf16[128,512]{1,0:T(8,128)(2,1)S(1)} %pad_maximum_fusion.9), channel_id=1, source_target_pairs={{0,2},{1,3},{2,0},{3,1},{4,6},{5,7},{6,4},{7,5},{8,10},{9,11},{10,... | collective-permute-start | bytes 393224 | tf_op jit(solution)/shard_map/ppermute | solution.py:286
  11.2 2.1 %copy.12 = bf16[128,4,1,512]{3,0,1,2:T(8,128)(2,1)} copy(bf16[128,4,1,512]{0,3,2,1:T(8,128)(2,1)} %slice.72) | data formatting | bytes 1048576
  19.1 3.5 %all-to-all-start = ((bf16[4,2,128,512]{3,2,1,0:T(8,128)(2,1)}), bf16[4,2,128,512]{3,2,1,0:T(8,128)(2,1)S(1)}, u32[]{:S(2)}, u32[]{:S(2)}) async-start(bf16[4,2,128,512]{3,2,1,0:T(8,128)(2,1)} %pad_maximum_fusion), calls=%async_computation | async-start | bytes 2097152 | tf_op jit(solution)/shard_map/all_to_all | solution.py:292
  23.8 9.5 %collective-permute-done.6.refs_6_.refs_3_ = bf16[4,128,512]{2,1,0:T(8,128)(2,1)S(1)} collective-permute-done((bf16[4,128,512]{2,1,0:T(8,128)(2,1)S(1)}, bf16[4,128,512]{2,1,0:T(8,128)(2,1)S(1)}, u32[]{:S(2)}, u32[]{:S(2)}) %collective-permute-start.6) | collective-permute-done | bytes 524320 | tf_op jit(solution)/shard_map/ppermute | solution.py:286
  33.3 9.6 %collective-permute-done.7.refs_7_.refs_4_ = bf16[4,128,512]{2,1,0:T(8,128)(2,1)} collective-permute-done((bf16[4,128,512]{2,1,0:T(8,128)(2,1)S(1)}, bf16[4,128,512]{2,1,0:T(8,128)(2,1)}, u32[]{:S(2)}, u32[]{:S(2)}) %collective-permute-start.7) | collective-permute-done | bytes 524320 | tf_op jit(solution)/shard_map/ppermute | solution.py:286
  43.6 4.1 %all-to-all-done.refs_1_ = bf16[4,2,128,512]{3,2,1,0:T(8,128)(2,1)S(1)} async-done(((bf16[4,2,128,512]{3,2,1,0:T(8,128)(2,1)}), bf16[4,2,128,512]{3,2,1,0:T(8,128)(2,1)S(1)}, u32[]{:S(2)}, u32[]{:S(2)}) %all-to-all-start) | async-done | bytes 1048608 | tf_op jit(solution)/shard_map/all_to_all | solution.py:292
  47.7 2.4 %collective-permute-start.4 = (bf16[2,128,512]{2,1,0:T(8,128)(2,1)S(1)}, bf16[2,128,512]{2,1,0:T(8,128)(2,1)}, u32[]{:S(2)}, u32[]{:S(2)}) collective-permute-start(bf16[2,128,512]{2,1,0:T(8,128)(2,1)S(1)} %pad_maximum_fusion.5), channel_id=1, source_target_pairs={{0,2},{1,3},{2,0},{3,1},{4,6},{5,7},{6,4},{7,5},{8,10},{9,11},{10,... | collective-permute-start | bytes 786440 | tf_op jit(solution)/shard_map/ppermute | solution.py:286
  50.1 1.4 %collective-permute-start.5 = (bf16[2,128,512]{2,1,0:T(8,128)(2,1)S(1)}, bf16[2,128,512]{2,1,0:T(8,128)(2,1)}, u32[]{:S(2)}, u32[]{:S(2)}) collective-permute-start(bf16[2,128,512]{2,1,0:T(8,128)(2,1)S(1)} %pad_maximum_fusion.6), channel_id=1, source_target_pairs={{0,3},{1,0},{2,1},{3,2},{4,7},{5,4},{6,5},{7,6},{8,11},{9,8},{10,9... | collective-permute-start | bytes 786440 | tf_op jit(solution)/shard_map/ppermute | solution.py:286
  52.7 10.7 %shard_map.77 = (bf16[4,128,512]{2,1,0:T(8,128)(2,1)}, bf16[4,128,256]{2,1,0:T(8,128)(2,1)}, bf16[4,128,256]{2,1,0:T(8,128)(2,1)}, bf16[4,128,256]{2,1,0:T(8,128)(2,1)}, bf16[4,128,256]{2,1,0:T(8,128)(2,1)}) custom-call(s32[9]{0:T(128)} %concatenate.15.refs_0_, bf16[4,2,128,512]{3,2,1,0:T(8,128)(2,1)} %copy-done.4, bf16[4,128,512]{2,1,0:T(8,128)(2,1)} %copy-done.5, ...), custom_call_target="tpu_custom_call" | custom-call | flops 12079595520 | bytes 4194304 | tf_op jit(solution)/shard_map/pallas_call | solution.py:220
  63.4 5.2 %all-to-all-start.1 = ((bf16[4,128,512]{2,1,0:T(8,128)(2,1)}), bf16[4,128,512]{2,1,0:T(8,128)(2,1)S(1)}, u32[]{:S(2)}, u32[]{:S(2)}) async-start(bf16[4,128,512]{2,1,0:T(8,128)(2,1)} %get-tuple-element.73), calls=%async_computation.1 | async-start | bytes 1048576 | tf_op jit(solution)/shard_map/all_to_all | solution.py:292
  68.8 1.8 %collective-permute-start.11 = (bf16[4,128,256]{2,1,0:T(8,128)(2,1)S(1)}, bf16[4,128,256]{2,1,0:T(8,128)(2,1)S(1)}, u32[]{:S(2)}, u32[]{:S(2)}) collective-permute-start(bf16[4,128,256]{2,1,0:T(8,128)(2,1)S(1)} %copy-done.21), channel_id=1, source_target_pairs={{0,20},{4,24},{8,28},{12,0},{16,4},{20,8},{24,12},{28,16},{1,21},{... | collective-permute-start | bytes 786440 | tf_op jit(solution)/shard_map/ppermute | solution.py:286
  70.5 10.8 %shard_map.76 = (bf16[128,512]{1,0:T(8,128)(2,1)}, bf16[128,512]{1,0:T(8,128)(2,1)}, bf16[128,512]{1,0:T(8,128)(2,1)}, bf16[128,512]{1,0:T(8,128)(2,1)}, bf16[4,...) custom-call(s32[9]{0:T(128)} %concatenate.15.refs_0_, ...), custom_call_target="tpu_custom_call" | custom-call | flops 12079595520 | bytes 4194304 | tf_op jit(solution)/shard_map/pallas_call | solution.py:220
  81.4 5.1 %collective-permute-start.12 = (bf16[4,128,256]{2,1,0:T(8,128)(2,1)}, bf16[4,128,256]{2,1,0:T(8,128)(2,1)S(1)}, u32[]{:S(2)}, u32[]{:S(2)}) collective-permute-start(bf16[4,128,256]{2,1,0:T(8,128)(2,1)} %get-tuple-element.88), channel_id=1, source_target_pairs={{0,28},{4,0},{8,4},{12,8},{16,12},{20,16},{24,20},{28,24},{1,29},{... | collective-permute-start | bytes 786440 | tf_op jit(solution)/shard_map/ppermute | solution.py:286
  87.9 5.8 %collective-permute-start.15 = (bf16[128,512]{1,0:T(8,128)(2,1)S(1)}, bf16[128,512]{1,0:T(8,128)(2,1)S(1)}, u32[]{:S(2)}, u32[]{:S(2)}) collective-permute-start(bf16[128,512]{1,0:T(8,128)(2,1)S(1)} %copy-done.26), channel_id=1, source_target_pairs={{0,3},{1,0},{2,1},{3,2},{4,7},{5,4},{6,5},{7,6},{8,11},{9,8},{10,9... | collective-permute-start | bytes 393224 | tf_op jit(solution)/shard_map/ppermute | solution.py:286
  93.7 1.5 %collective-permute-start.16 = (bf16[128,512]{1,0:T(8,128)(2,1)S(1)}, bf16[128,512]{1,0:T(8,128)(2,1)S(1)}, u32[]{:S(2)}, u32[]{:S(2)}) collective-permute-start(bf16[128,512]{1,0:T(8,128)(2,1)S(1)} %copy-done.25), channel_id=1, source_target_pairs={{0,2},{1,3},{2,0},{3,1},{4,6},{5,7},{6,4},{7,5},{8,10},{9,11},{10,... | collective-permute-start | bytes 393224 | tf_op jit(solution)/shard_map/ppermute | solution.py:286
  96.0 2.6 %collective-permute-done.13 = bf16[4,128,256]{2,1,0:T(8,128)(2,1)S(1)} collective-permute-done((bf16[4,128,256]{2,1,0:T(8,128)(2,1)}, bf16[4,128,256]{2,1,0:T(8,128)(2,1)S(1)}, u32[]{:S(2)}, u32[]{:S(2)}) %collective-permute-start.13) | collective-permute-done | bytes 262176 | tf_op jit(solution)/shard_map/ppermute | solution.py:286
  98.9 8.8 %collective-permute-done.16.refs_3_ = bf16[128,512]{1,0:T(8,128)(2,1)S(1)} collective-permute-done((bf16[128,512]{1,0:T(8,128)(2,1)S(1)}, bf16[128,512]{1,0:T(8,128)(2,1)S(1)}, u32[]{:S(2)}, u32[]{:S(2)}) %collective-permute-start.16) | collective-permute-done | bytes 131104 | tf_op jit(solution)/shard_map/ppermute | solution.py:286
  109.2 3.1 %collective-permute-start.18 = (bf16[2,128,256]{2,1,0:T(8,128)(2,1)S(1)}, bf16[2,128,256]{2,1,0:T(8,128)(2,1)S(1)}, u32[]{:S(2)}, u32[]{:S(2)}) collective-permute-start(bf16[2,128,256]{2,1,0:T(8,128)(2,1)S(1)} %get-tuple-element.117), channel_id=1, source_target_pairs={{0,3},{1,0},{2,1},{3,2},{4,7},{5,4},{6,5},{7,6},{8,11},{9,8},{10,9... | collective-permute-start | bytes 393224 | tf_op jit(solution)/shard_map/ppermute | solution.py:286
  112.3 2.3 %shard_map.78 = bf16[128,4096]{1,0:T(8,128)(2,1)} custom-call(s32[1]{0:T(128)} %bitcast.z_ref, bf16[4,128,512]{2,1,0:T(8,128)(2,1)} %copy-done.2, bf16[128,512]{1,0:T(8,128)(2,1)} %get-tuple-element.95.refs_1_, bf16[128,512]{1,0:T(8,128)(2,1)} %copy-done.8, bf16[128,512]{1,0:T(8,128)(2,1)} %copy-done.9, bf16[128,512]{1,0:T(8,128)(2,1)} %copy-done.10), custom_call_target="tpu_custom_call" | custom-call | tf_op jit(solution)/shard_map/pallas_call | solution.py:265
  114.6 2.1 %collective-permute-done.20.refs_3_ = bf16[2,128,256]{2,1,0:T(8,128)(2,1)S(1)} collective-permute-done((bf16[2,128,256]{2,1,0:T(8,128)(2,1)S(1)}, bf16[2,128,256]{2,1,0:T(8,128)(2,1)S(1)}, u32[]{:S(2)}, u32[]{:S(2)}) %collective-permute-start.20) | collective-permute-done | bytes 131104 | tf_op jit(solution)/shard_map/ppermute | solution.py:286
  116.7 4.5 %collective-permute-done.19.refs_2_ = bf16[2,128,256]{2,1,0:T(8,128)(2,1)S(1)} collective-permute-done((bf16[2,128,256]{2,1,0:T(8,128)(2,1)S(1)}, bf16[2,128,256]{2,1,0:T(8,128)(2,1)S(1)}, u32[]{:S(2)}, u32[]{:S(2)}) %collective-permute-start.19) | collective-permute-done | bytes 131104 | tf_op jit(solution)/shard_map/ppermute | solution.py:286
  121.9 2.0 %shard_map.79 = (bf16[128,1024]{1,0:T(8,128)(2,1)}, bf16[128,1024]{1,0:T(8,128)(2,1)}) custom-call(s32[1]{0:T(128)} %bitcast.z_ref, bf16[2,128,256]{2,1,0:T(8,128)(2,1)} %get-tuple-element.101.refs_0_, bf16[2,128,256]{2,1,0:T(8,128)(2,1)} %copy-done.13, bf16[2,128,256]{2,1,0:T(8,128)(2,1)} %copy-done.12, bf16[2,128,256]{2,1,0:T(8,128)(2,1)} %copy-done.11), custom_call_target="tpu_custom_call" | custom-call | tf_op jit(solution)/shard_map/pallas_call | solution.py:265
  (104 shorter events, 16.4 us)
Async XLA Ops:
  2.5 16.6 %collective-permute-start = (bf16[128,512]{1,0:T(8,128)(2,1)S(1)}, bf16[128,512]{1,0:T(8,128)(2,1)}, u32[]{:S(2)}, u32[]{:S(2)}) collective-permute-start(bf16[128,512]{1,0:T(8,128)(2,1)S(1)} %pad_maximum_fusion.8), channel_id=1, source_target_pairs={{0,1},{1,2},{2,3},{3,0},{4,5},{5,6},{6,7},{7,4},{8,9},{9,10},{10,1... | collective-permute-start | bytes 393224 | tf_op jit(solution)/shard_map/ppermute | solution.py:286
  5.6 13.5 %collective-permute-start.1 = (bf16[128,512]{1,0:T(8,128)(2,1)S(1)}, bf16[128,512]{1,0:T(8,128)(2,1)}, u32[]{:S(2)}, u32[]{:S(2)}) collective-permute-start(bf16[128,512]{1,0:T(8,128)(2,1)S(1)} %pad_maximum_fusion.9), channel_id=1, source_target_pairs={{0,2},{1,3},{2,0},{3,1},{4,6},{5,7},{6,4},{7,5},{8,10},{9,11},{10,... | collective-permute-start | bytes 393224 | tf_op jit(solution)/shard_map/ppermute | solution.py:286
  8.2 10.8 %collective-permute-start.2 = (bf16[128,512]{1,0:T(8,128)(2,1)S(1)}, bf16[128,512]{1,0:T(8,128)(2,1)}, u32[]{:S(2)}, u32[]{:S(2)}) collective-permute-start(bf16[128,512]{1,0:T(8,128)(2,1)S(1)} %pad_maximum_fusion.10), channel_id=1, source_target_pairs={{0,3},{1,0},{2,1},{3,2},{4,7},{5,4},{6,5},{7,6},{8,11},{9,8},{10,9... | collective-permute-start | bytes 393224 | tf_op jit(solution)/shard_map/ppermute | solution.py:286
  19.1 28.7 %all-to-all-start = ((bf16[4,2,128,512]{3,2,1,0:T(8,128)(2,1)}), bf16[4,2,128,512]{3,2,1,0:T(8,128)(2,1)S(1)}, u32[]{:S(2)}, u32[]{:S(2)}) async-start(bf16[4,2,128,512]{3,2,1,0:T(8,128)(2,1)} %pad_maximum_fusion), calls=%async_computation | async-start | bytes 2097152 | tf_op jit(solution)/shard_map/all_to_all | solution.py:292
  23.7 29.0 %copy-start.5 = (bf16[4,128,512]{2,1,0:T(8,128)(2,1)}, bf16[4,128,512]{2,1,0:T(8,128)(2,1)S(1)}, u32[]{:S(2)}) copy-start(bf16[4,128,512]{2,1,0:T(8,128)(2,1)S(1)} %pad_maximum_fusion.1.refs_5_.refs_2_) | copy-start | bytes 1572868
  23.7 9.6 %collective-permute-start.6 = (bf16[4,128,512]{2,1,0:T(8,128)(2,1)S(1)}, bf16[4,128,512]{2,1,0:T(8,128)(2,1)S(1)}, u32[]{:S(2)}, u32[]{:S(2)}) collective-permute-start(bf16[4,128,512]{2,1,0:T(8,128)(2,1)S(1)} %pad_maximum_fusion.1.refs_5_.refs_2_), channel_id=1, source_target_pairs={{0,4},{4,8},{8,12},{12,16},{16,20},{20,24},{24,28},{28,0},{1,5},{5... | collective-permute-start | bytes 1572872 | tf_op jit(solution)/shard_map/ppermute | solution.py:286
  33.3 9.6 %collective-permute-start.7 = (bf16[4,128,512]{2,1,0:T(8,128)(2,1)S(1)}, bf16[4,128,512]{2,1,0:T(8,128)(2,1)}, u32[]{:S(2)}, u32[]{:S(2)}) collective-permute-start(bf16[4,128,512]{2,1,0:T(8,128)(2,1)S(1)} %collective-permute-done.6.refs_6_.refs_3_), channel_id=1, source_target_pairs={{0,4},{4,8},{8,12},{12,16},{16,20},{20,24},{24,28},{28,0},{1,5},{5... | collective-permute-start | bytes 1572872 | tf_op jit(solution)/shard_map/ppermute | solution.py:286
  42.9 9.8 %collective-permute-start.8 = (bf16[4,128,512]{2,1,0:T(8,128)(2,1)}, bf16[4,128,512]{2,1,0:T(8,128)(2,1)}, u32[]{:S(2)}, u32[]{:S(2)}) collective-permute-start(bf16[4,128,512]{2,1,0:T(8,128)(2,1)} %collective-permute-done.7.refs_7_.refs_4_), channel_id=1, source_target_pairs={{0,4},{4,8},{8,12},{12,16},{16,20},{20,24},{24,28},{28,0},{1,5},{5... | collective-permute-start | bytes 1572872 | tf_op jit(solution)/shard_map/ppermute | solution.py:286
  47.7 21.0 %collective-permute-start.3 = (bf16[2,128,512]{2,1,0:T(8,128)(2,1)S(1)}, bf16[2,128,512]{2,1,0:T(8,128)(2,1)S(1)}, u32[]{:S(2)}, u32[]{:S(2)}) collective-permute-start(bf16[2,128,512]{2,1,0:T(8,128)(2,1)S(1)} %pad_maximum_fusion.4), channel_id=1, source_target_pairs={{0,1},{1,2},{2,3},{3,0},{4,5},{5,6},{6,7},{7,4},{8,9},{9,10},{10,1... | collective-permute-start | bytes 786440 | tf_op jit(solution)/shard_map/ppermute | solution.py:286
  47.7 22.8 %collective-permute-start.4 = (bf16[2,128,512]{2,1,0:T(8,128)(2,1)S(1)}, bf16[2,128,512]{2,1,0:T(8,128)(2,1)}, u32[]{:S(2)}, u32[]{:S(2)}) collective-permute-start(bf16[2,128,512]{2,1,0:T(8,128)(2,1)S(1)} %pad_maximum_fusion.5), channel_id=1, source_target_pairs={{0,2},{1,3},{2,0},{3,1},{4,6},{5,7},{6,4},{7,5},{8,10},{9,11},{10,... | collective-permute-start | bytes 786440 | tf_op jit(solution)/shard_map/ppermute | solution.py:286
  50.1 20.4 %collective-permute-start.5 = (bf16[2,128,512]{2,1,0:T(8,128)(2,1)S(1)}, bf16[2,128,512]{2,1,0:T(8,128)(2,1)}, u32[]{:S(2)}, u32[]{:S(2)}) collective-permute-start(bf16[2,128,512]{2,1,0:T(8,128)(2,1)S(1)} %pad_maximum_fusion.6), channel_id=1, source_target_pairs={{0,3},{1,0},{2,1},{3,2},{4,7},{5,4},{6,5},{7,6},{8,11},{9,8},{10,9... | collective-permute-start | bytes 786440 | tf_op jit(solution)/shard_map/ppermute | solution.py:286
  63.4 24.5 %all-to-all-start.1 = ((bf16[4,128,512]{2,1,0:T(8,128)(2,1)}), bf16[4,128,512]{2,1,0:T(8,128)(2,1)S(1)}, u32[]{:S(2)}, u32[]{:S(2)}) async-start(bf16[4,128,512]{2,1,0:T(8,128)(2,1)} %get-tuple-element.73), calls=%async_computation.1 | async-start | bytes 1048576 | tf_op jit(solution)/shard_map/all_to_all | solution.py:292
  68.6 12.7 %collective-permute-start.9 = (bf16[4,128,256]{2,1,0:T(8,128)(2,1)S(1)}, bf16[4,128,256]{2,1,0:T(8,128)(2,1)S(1)}, u32[]{:S(2)}, u32[]{:S(2)}) collective-permute-start(bf16[4,128,256]{2,1,0:T(8,128)(2,1)S(1)} %copy-done.23), channel_id=1, source_target_pairs={{0,28},{4,0},{8,4},{12,8},{16,12},{20,16},{24,20},{28,24},{1,29},{... | collective-permute-start | bytes 786440 | tf_op jit(solution)/shard_map/ppermute | solution.py:286
  68.6 12.7 %collective-permute-start.10 = (bf16[4,128,256]{2,1,0:T(8,128)(2,1)S(1)}, bf16[4,128,256]{2,1,0:T(8,128)(2,1)S(1)}, u32[]{:S(2)}, u32[]{:S(2)}) collective-permute-start(bf16[4,128,256]{2,1,0:T(8,128)(2,1)S(1)} %copy-done.22), channel_id=1, source_target_pairs={{0,24},{4,28},{8,0},{12,4},{16,8},{20,12},{24,16},{28,20},{1,25},{... | collective-permute-start | bytes 786440 | tf_op jit(solution)/shard_map/ppermute | solution.py:286
  68.8 12.6 %collective-permute-start.11 = (bf16[4,128,256]{2,1,0:T(8,128)(2,1)S(1)}, bf16[4,128,256]{2,1,0:T(8,128)(2,1)S(1)}, u32[]{:S(2)}, u32[]{:S(2)}) collective-permute-start(bf16[4,128,256]{2,1,0:T(8,128)(2,1)S(1)} %copy-done.21), channel_id=1, source_target_pairs={{0,20},{4,24},{8,28},{12,0},{16,4},{20,8},{24,12},{28,16},{1,21},{... | collective-permute-start | bytes 786440 | tf_op jit(solution)/shard_map/ppermute | solution.py:286
  81.4 13.9 %collective-permute-start.12 = (bf16[4,128,256]{2,1,0:T(8,128)(2,1)}, bf16[4,128,256]{2,1,0:T(8,128)(2,1)S(1)}, u32[]{:S(2)}, u32[]{:S(2)}) collective-permute-start(bf16[4,128,256]{2,1,0:T(8,128)(2,1)} %get-tuple-element.88), channel_id=1, source_target_pairs={{0,28},{4,0},{8,4},{12,8},{16,12},{20,16},{24,20},{28,24},{1,29},{... | collective-permute-start | bytes 786440 | tf_op jit(solution)/shard_map/ppermute | solution.py:286
  86.5 12.2 %collective-permute-start.13 = (bf16[4,128,256]{2,1,0:T(8,128)(2,1)}, bf16[4,128,256]{2,1,0:T(8,128)(2,1)S(1)}, u32[]{:S(2)}, u32[]{:S(2)}) collective-permute-start(bf16[4,128,256]{2,1,0:T(8,128)(2,1)} %get-tuple-element.89), channel_id=1, source_target_pairs={{0,24},{4,28},{8,0},{12,4},{16,8},{20,12},{24,16},{28,20},{1,25},{... | collective-permute-start | bytes 786440 | tf_op jit(solution)/shard_map/ppermute | solution.py:286
  86.5 12.2 %collective-permute-start.14 = (bf16[4,128,256]{2,1,0:T(8,128)(2,1)}, bf16[4,128,256]{2,1,0:T(8,128)(2,1)S(1)}, u32[]{:S(2)}, u32[]{:S(2)}) collective-permute-start(bf16[4,128,256]{2,1,0:T(8,128)(2,1)} %get-tuple-element.90), channel_id=1, source_target_pairs={{0,20},{4,24},{8,28},{12,0},{16,4},{20,8},{24,12},{28,16},{1,21},{... | collective-permute-start | bytes 786440 | tf_op jit(solution)/shard_map/ppermute | solution.py:286
  87.9 10.9 %collective-permute-start.15 = (bf16[128,512]{1,0:T(8,128)(2,1)S(1)}, bf16[128,512]{1,0:T(8,128)(2,1)S(1)}, u32[]{:S(2)}, u32[]{:S(2)}) collective-permute-start(bf16[128,512]{1,0:T(8,128)(2,1)S(1)} %copy-done.26), channel_id=1, source_target_pairs={{0,3},{1,0},{2,1},{3,2},{4,7},{5,4},{6,5},{7,6},{8,11},{9,8},{10,9... | collective-permute-start | bytes 393224 | tf_op jit(solution)/shard_map/ppermute | solution.py:286
  93.7 14.0 %collective-permute-start.16 = (bf16[128,512]{1,0:T(8,128)(2,1)S(1)}, bf16[128,512]{1,0:T(8,128)(2,1)S(1)}, u32[]{:S(2)}, u32[]{:S(2)}) collective-permute-start(bf16[128,512]{1,0:T(8,128)(2,1)S(1)} %copy-done.25), channel_id=1, source_target_pairs={{0,2},{1,3},{2,0},{3,1},{4,6},{5,7},{6,4},{7,5},{8,10},{9,11},{10,... | collective-permute-start | bytes 393224 | tf_op jit(solution)/shard_map/ppermute | solution.py:286
  95.3 12.4 %collective-permute-start.17 = (bf16[128,512]{1,0:T(8,128)(2,1)S(1)}, bf16[128,512]{1,0:T(8,128)(2,1)S(1)}, u32[]{:S(2)}, u32[]{:S(2)}) collective-permute-start(bf16[128,512]{1,0:T(8,128)(2,1)S(1)} %copy-done.24), channel_id=1, source_target_pairs={{0,1},{1,2},{2,3},{3,0},{4,5},{5,6},{6,7},{7,4},{8,9},{9,10},{10,1... | collective-permute-start | bytes 393224 | tf_op jit(solution)/shard_map/ppermute | solution.py:286
  108.4 8.3 %collective-permute-start.20 = (bf16[2,128,256]{2,1,0:T(8,128)(2,1)S(1)}, bf16[2,128,256]{2,1,0:T(8,128)(2,1)S(1)}, u32[]{:S(2)}, u32[]{:S(2)}) collective-permute-start(bf16[2,128,256]{2,1,0:T(8,128)(2,1)S(1)} %get-tuple-element.115), channel_id=1, source_target_pairs={{0,1},{1,2},{2,3},{3,0},{4,5},{5,6},{6,7},{7,4},{8,9},{9,10},{10,1... | collective-permute-start | bytes 393224 | tf_op jit(solution)/shard_map/ppermute | solution.py:286
  108.5 12.7 %collective-permute-start.19 = (bf16[2,128,256]{2,1,0:T(8,128)(2,1)S(1)}, bf16[2,128,256]{2,1,0:T(8,128)(2,1)S(1)}, u32[]{:S(2)}, u32[]{:S(2)}) collective-permute-start(bf16[2,128,256]{2,1,0:T(8,128)(2,1)S(1)} %get-tuple-element.116), channel_id=1, source_target_pairs={{0,2},{1,3},{2,0},{3,1},{4,6},{5,7},{6,4},{7,5},{8,10},{9,11},{10,... | collective-permute-start | bytes 393224 | tf_op jit(solution)/shard_map/ppermute | solution.py:286
  109.2 12.0 %collective-permute-start.18 = (bf16[2,128,256]{2,1,0:T(8,128)(2,1)S(1)}, bf16[2,128,256]{2,1,0:T(8,128)(2,1)S(1)}, u32[]{:S(2)}, u32[]{:S(2)}) collective-permute-start(bf16[2,128,256]{2,1,0:T(8,128)(2,1)S(1)} %get-tuple-element.117), channel_id=1, source_target_pairs={{0,3},{1,0},{2,1},{3,2},{4,7},{5,4},{6,5},{7,6},{8,11},{9,8},{10,9... | collective-permute-start | bytes 393224 | tf_op jit(solution)/shard_map/ppermute | solution.py:286
  (26 other events, 175.3 us)

commit v5 on v4

--- a/solution.py
+++ b/solution.py
@@ -268,7 +268,7 @@
         + [pl.BlockSpec(memory_space=pltpu.VMEM)] * len(parts),
         out_specs=[pl.BlockSpec(memory_space=pltpu.VMEM)] * outs,
         out_shape=[jax.ShapeDtypeStruct((rows, size), LOW)] * outs,
-        compiler_params=pltpu.CompilerParams(vmem_limit_bytes=VMEM_LIMIT),
+        compiler_params=pltpu.CompilerParams(vmem_limit_bytes=8 * 1024 * 1024),
     )(z.astype(jnp.int32)[None], *parts)
 
 
@@ -348,10 +348,17 @@
     def add(dkv):
         return sum(d.astype(WIDE) for d in dkv).astype(LOW)
 
+    near = [s for s in range(1, splits) if 2 * s != splits]
     dq, dkv = [], []
     for j in range(local):
         last = j > 0 and j == local - 1
         dq_j, dkv_j = attention(ids, chunks[j], blocks, j, last)
+        if j + 1 < local:
+            came = chunks[j + 1]
+            came = [came[s] for s in near]
+            dq_j, came = fence((dq_j, came))
+            for s, part in zip(near, came):
+                chunks[j + 1][s] = part
         if j > 0:
             dkv_j, dkv[j - 1] = fence((dkv_j, dkv[j - 1]))
             dq_j, dq[j - 1] = fence((dq_j, dq[j - 1]))

time: 124 us -> 115 us (0.927)
  starting transfers between devices: 39.9 us -> 34.2 us
  Pallas kernels: 25.7 us -> 23.4 us
    ppermute x21, starting transfers between devices: 31.2 us -> 25.7 us  [shift(): lax.ppermute(array, axis, [(i, (i + by) % size) for i in range(size)])]
    pallas_call x2, Pallas kernels: 4.26 us -> 1.94 us  [in_columns(): pl.pallas_call(kernel, in_specs=[pl.BlockSpec(memory_space=pltpu.SMEM)] +...]
    unnamed x58 -> x42, local copies, waits for them, and re-layouts: 6.37 us -> 6.37 us
  transfers between devices with their start and end apart: 23 -> 23, of which waited for: 8 -> 9; matrix products, arithmetic and copies ran while one was open for 8% -> 9% of each run, Pallas kernels for 19% -> 20%
where the time goes in v5:
time: 115 us; the launch traced here: 114 us
  waiting for transfers between devices  41.8 us (36%)
  starting transfers between devices  34.2 us (30%)
  Pallas kernels  23.4 us (20%)
  local copies, waits for them, and re-layouts  10.6 us (9%)
  other arithmetic  3.37 us (3%)
    ppermute x21, waiting for transfers between devices, shift(): lax.ppermute(array, axis, [(i, (i + by) % size) for i in range(size)])  37.7 us
    ppermute x21, starting transfers between devices, shift(): lax.ppermute(array, axis, [(i, (i + by) % size) for i in range(size)])  25.7 us
    pallas_call x2, Pallas kernels, attention(): pl.pallas_call(kernel, grid=(heads // at_once,), in_specs=[pl.BlockSpec(m...  21.4 us
    all_to_all x2, starting transfers between devices, swap(): lax.all_to_all(array, 'head', split_axis=0, concat_axis=0, tiled=True)  8.58 us
    unnamed x42, local copies, waits for them, and re-layouts  6.37 us
    all_to_all x2, waiting for transfers between devices, swap(): lax.all_to_all(array, 'head', split_axis=0, concat_axis=0, tiled=True)  4.15 us
  transfers between devices with their start and end apart: 23, of which 9 were waited for; matrix products, arithmetic and copies ran while one was open for 9% of the time, Pallas kernels for 20%

profile of v5, /device:TPU:0, one launch (start us, length us, event | category | flops | bytes accessed | tf_op | source)
XLA Modules:
  0.0 114.5 jit_solution(13150717223995393353)
XLA Ops:
  0.7 1.8 %constant_dynamic-slice_fusion = (bf16[128,128]{1,0:T(8,128)(2,1)S(1)}, bf16[128,128]{1,0:T(8,128)(2,1)S(1)}, bf16[128,128]{1,0:T(8,128)(2,1)S(1)}, bf16[128,128...) fusion(bf16[128,1024]{1,0:T(8,128)(2,1)} %param.7, ...), kind=kLoop, calls=%fused_computation.27 | loop fusion | bytes 1048608 | tf_op jit(solution)/shard_map/slice | solution.py:307
  2.5 3.1 %collective-permute-start = (bf16[128,512]{1,0:T(8,128)(2,1)S(1)}, bf16[128,512]{1,0:T(8,128)(2,1)}, u32[]{:S(2)}, u32[]{:S(2)}) collective-permute-start(bf16[128,512]{1,0:T(8,128)(2,1)S(1)} %pad_maximum_fusion.8), channel_id=1, source_target_pairs={{0,1},{1,2},{2,3},{3,0},{4,5},{5,6},{6,7},{7,4},{8,9},{9,10},{10,1... | collective-permute-start | bytes 393224 | tf_op jit(solution)/shard_map/ppermute | solution.py:286
  5.6 2.7 %collective-permute-start.1 = (bf16[128,512]{1,0:T(8,128)(2,1)S(1)}, bf16[128,512]{1,0:T(8,128)(2,1)}, u32[]{:S(2)}, u32[]{:S(2)}) collective-permute-start(bf16[128,512]{1,0:T(8,128)(2,1)S(1)} %pad_maximum_fusion.9), channel_id=1, source_target_pairs={{0,2},{1,3},{2,0},{3,1},{4,6},{5,7},{6,4},{7,5},{8,10},{9,11},{10,... | collective-permute-start | bytes 393224 | tf_op jit(solution)/shard_map/ppermute | solution.py:286
  8.2 1.4 %collective-permute-start.2 = (bf16[128,512]{1,0:T(8,128)(2,1)S(1)}, bf16[128,512]{1,0:T(8,128)(2,1)}, u32[]{:S(2)}, u32[]{:S(2)}) collective-permute-start(bf16[128,512]{1,0:T(8,128)(2,1)S(1)} %pad_maximum_fusion.10), channel_id=1, source_target_pairs={{0,3},{1,0},{2,1},{3,2},{4,7},{5,4},{6,5},{7,6},{8,11},{9,8},{10,9... | collective-permute-start | bytes 393224 | tf_op jit(solution)/shard_map/ppermute | solution.py:286
  11.2 2.0 %copy.12 = bf16[128,4,1,512]{3,0,1,2:T(8,128)(2,1)} copy(bf16[128,4,1,512]{0,3,2,1:T(8,128)(2,1)} %slice.72) | data formatting | bytes 1048576
  19.1 3.5 %all-to-all-start = ((bf16[4,2,128,512]{3,2,1,0:T(8,128)(2,1)}), bf16[4,2,128,512]{3,2,1,0:T(8,128)(2,1)S(1)}, u32[]{:S(2)}, u32[]{:S(2)}) async-start(bf16[4,2,128,512]{3,2,1,0:T(8,128)(2,1)} %pad_maximum_fusion), calls=%async_computation | async-start | bytes 2097152 | tf_op jit(solution)/shard_map/all_to_all | solution.py:292
  23.8 9.5 %collective-permute-done.3.refs_3_.refs_6_ = bf16[4,128,512]{2,1,0:T(8,128)(2,1)S(1)} collective-permute-done((bf16[4,128,512]{2,1,0:T(8,128)(2,1)S(1)}, bf16[4,128,512]{2,1,0:T(8,128)(2,1)S(1)}, u32[]{:S(2)}, u32[]{:S(2)}) %collective-permute-start.3) | collective-permute-done | bytes 524320 | tf_op jit(solution)/shard_map/ppermute | solution.py:286
  33.3 9.6 %collective-permute-done.4.refs_4_.refs_7_ = bf16[4,128,512]{2,1,0:T(8,128)(2,1)} collective-permute-done((bf16[4,128,512]{2,1,0:T(8,128)(2,1)S(1)}, bf16[4,128,512]{2,1,0:T(8,128)(2,1)}, u32[]{:S(2)}, u32[]{:S(2)}) %collective-permute-start.4) | collective-permute-done | bytes 524320 | tf_op jit(solution)/shard_map/ppermute | solution.py:286
  43.6 4.2 %all-to-all-done.refs_1_ = bf16[4,2,128,512]{3,2,1,0:T(8,128)(2,1)S(1)} async-done(((bf16[4,2,128,512]{3,2,1,0:T(8,128)(2,1)}), bf16[4,2,128,512]{3,2,1,0:T(8,128)(2,1)S(1)}, u32[]{:S(2)}, u32[]{:S(2)}) %all-to-all-start) | async-done | bytes 1048608 | tf_op jit(solution)/shard_map/all_to_all | solution.py:292
  47.7 3.8 %collective-permute-start.7 = (bf16[2,128,512]{2,1,0:T(8,128)(2,1)S(1)}, bf16[2,128,512]{2,1,0:T(8,128)(2,1)S(1)}, u32[]{:S(2)}, u32[]{:S(2)}) collective-permute-start(bf16[2,128,512]{2,1,0:T(8,128)(2,1)S(1)} %pad_maximum_fusion.6), channel_id=1, source_target_pairs={{0,3},{1,0},{2,1},{3,2},{4,7},{5,4},{6,5},{7,6},{8,11},{9,8},{10,9... | collective-permute-start | bytes 786440 | tf_op jit(solution)/shard_map/ppermute | solution.py:286
  52.7 10.7 %shard_map.76 = (bf16[4,128,512]{2,1,0:T(8,128)(2,1)}, bf16[4,128,256]{2,1,0:T(8,128)(2,1)}, bf16[4,128,256]{2,1,0:T(8,128)(2,1)}, bf16[4,128,256]{2,1,0:T(8,128)(2,1)}, bf16[4,128,256]{2,1,0:T(8,128)(2,1)}) custom-call(s32[9]{0:T(128)} %concatenate.15.refs_0_, bf16[4,2,128,512]{3,2,1,0:T(8,128)(2,1)} %copy-done.4, bf16[4,128,512]{2,1,0:T(8,128)(2,1)} %copy-done.5, ...), custom_call_target="tpu_custom_call" | custom-call | flops 12079595520 | bytes 4194304 | tf_op jit(solution)/shard_map/pallas_call | solution.py:220
  63.5 1.4 %collective-permute-start.10 = (bf16[4,128,256]{2,1,0:T(8,128)(2,1)}, bf16[4,128,256]{2,1,0:T(8,128)(2,1)S(1)}, u32[]{:S(2)}, u32[]{:S(2)}) collective-permute-start(bf16[4,128,256]{2,1,0:T(8,128)(2,1)} %get-tuple-element.87), channel_id=1, source_target_pairs={{0,24},{4,28},{8,0},{12,4},{16,8},{20,12},{24,16},{28,20},{1,25},{... | collective-permute-start | bytes 786440 | tf_op jit(solution)/shard_map/ppermute | solution.py:286
  65.9 5.1 %all-to-all-start.1 = ((bf16[4,128,512]{2,1,0:T(8,128)(2,1)}), bf16[4,128,512]{2,1,0:T(8,128)(2,1)S(1)}, u32[]{:S(2)}, u32[]{:S(2)}) async-start(bf16[4,128,512]{2,1,0:T(8,128)(2,1)} %get-tuple-element.79), calls=%async_computation.1 | async-start | bytes 1048576 | tf_op jit(solution)/shard_map/all_to_all | solution.py:292
  71.7 10.8 %shard_map.77 = (bf16[128,512]{1,0:T(8,128)(2,1)}, bf16[128,512]{1,0:T(8,128)(2,1)}, bf16[128,512]{1,0:T(8,128)(2,1)}, bf16[128,512]{1,0:T(8,128)(2,1)}, bf16[4,...) custom-call(s32[9]{0:T(128)} %concatenate.15.refs_0_, ...), custom_call_target="tpu_custom_call" | custom-call | flops 12079595520 | bytes 4194304 | tf_op jit(solution)/shard_map/pallas_call | solution.py:220
  83.1 2.3 %collective-permute-start.13 = (bf16[4,128,256]{2,1,0:T(8,128)(2,1)}, bf16[4,128,256]{2,1,0:T(8,128)(2,1)S(1)}, u32[]{:S(2)}, u32[]{:S(2)}) collective-permute-start(bf16[4,128,256]{2,1,0:T(8,128)(2,1)} %get-tuple-element.95), channel_id=1, source_target_pairs={{0,24},{4,28},{8,0},{12,4},{16,8},{20,12},{24,16},{28,20},{1,25},{... | collective-permute-start | bytes 786440 | tf_op jit(solution)/shard_map/ppermute | solution.py:286
  85.4 1.3 %collective-permute-start.14 = (bf16[4,128,256]{2,1,0:T(8,128)(2,1)}, bf16[4,128,256]{2,1,0:T(8,128)(2,1)S(1)}, u32[]{:S(2)}, u32[]{:S(2)}) collective-permute-start(bf16[4,128,256]{2,1,0:T(8,128)(2,1)} %get-tuple-element.96), channel_id=1, source_target_pairs={{0,20},{4,24},{8,28},{12,0},{16,4},{20,8},{24,12},{28,16},{1,21},{... | collective-permute-start | bytes 786440 | tf_op jit(solution)/shard_map/ppermute | solution.py:286
  86.8 2.2 %collective-permute-start.15 = (bf16[128,512]{1,0:T(8,128)(2,1)S(1)}, bf16[128,512]{1,0:T(8,128)(2,1)S(1)}, u32[]{:S(2)}, u32[]{:S(2)}) collective-permute-start(bf16[128,512]{1,0:T(8,128)(2,1)S(1)} %copy-done.18), channel_id=1, source_target_pairs={{0,3},{1,0},{2,1},{3,2},{4,7},{5,4},{6,5},{7,6},{8,11},{9,8},{10,9... | collective-permute-start | bytes 393224 | tf_op jit(solution)/shard_map/ppermute | solution.py:286
  89.0 1.3 %collective-permute-start.17 = (bf16[128,512]{1,0:T(8,128)(2,1)S(1)}, bf16[128,512]{1,0:T(8,128)(2,1)S(1)}, u32[]{:S(2)}, u32[]{:S(2)}) collective-permute-start(bf16[128,512]{1,0:T(8,128)(2,1)S(1)} %copy-done.16), channel_id=1, source_target_pairs={{0,1},{1,2},{2,3},{3,0},{4,5},{5,6},{6,7},{7,4},{8,9},{9,10},{10,1... | collective-permute-start | bytes 393224 | tf_op jit(solution)/shard_map/ppermute | solution.py:286
  90.3 7.9 %collective-permute-done.13 = bf16[4,128,256]{2,1,0:T(8,128)(2,1)S(1)} collective-permute-done((bf16[4,128,256]{2,1,0:T(8,128)(2,1)}, bf16[4,128,256]{2,1,0:T(8,128)(2,1)S(1)}, u32[]{:S(2)}, u32[]{:S(2)}) %collective-permute-start.13) | collective-permute-done | bytes 262176 | tf_op jit(solution)/shard_map/ppermute | solution.py:286
  98.4 2.4 %collective-permute-done.16.refs_3_ = bf16[128,512]{1,0:T(8,128)(2,1)S(1)} collective-permute-done((bf16[128,512]{1,0:T(8,128)(2,1)S(1)}, bf16[128,512]{1,0:T(8,128)(2,1)S(1)}, u32[]{:S(2)}, u32[]{:S(2)}) %collective-permute-start.16) | collective-permute-done | bytes 131104 | tf_op jit(solution)/shard_map/ppermute | solution.py:286
  101.4 2.0 %collective-permute-start.19 = (bf16[2,128,256]{2,1,0:T(8,128)(2,1)S(1)}, bf16[2,128,256]{2,1,0:T(8,128)(2,1)S(1)}, u32[]{:S(2)}, u32[]{:S(2)}) collective-permute-start(bf16[2,128,256]{2,1,0:T(8,128)(2,1)S(1)} %get-tuple-element.122), channel_id=1, source_target_pairs={{0,2},{1,3},{2,0},{3,1},{4,6},{5,7},{6,4},{7,5},{8,10},{9,11},{10,... | collective-permute-start | bytes 393224 | tf_op jit(solution)/shard_map/ppermute | solution.py:286
  103.4 2.8 %collective-permute-start.18 = (bf16[2,128,256]{2,1,0:T(8,128)(2,1)S(1)}, bf16[2,128,256]{2,1,0:T(8,128)(2,1)S(1)}, u32[]{:S(2)}, u32[]{:S(2)}) collective-permute-start(bf16[2,128,256]{2,1,0:T(8,128)(2,1)S(1)} %get-tuple-element.123), channel_id=1, source_target_pairs={{0,3},{1,0},{2,1},{3,2},{4,7},{5,4},{6,5},{7,6},{8,11},{9,8},{10,9... | collective-permute-start | bytes 393224 | tf_op jit(solution)/shard_map/ppermute | solution.py:286
  107.3 1.9 %collective-permute-done.20.refs_3_ = bf16[2,128,256]{2,1,0:T(8,128)(2,1)S(1)} collective-permute-done((bf16[2,128,256]{2,1,0:T(8,128)(2,1)S(1)}, bf16[2,128,256]{2,1,0:T(8,128)(2,1)S(1)}, u32[]{:S(2)}, u32[]{:S(2)}) %collective-permute-start.20) | collective-permute-done | bytes 131104 | tf_op jit(solution)/shard_map/ppermute | solution.py:286
  109.2 4.4 %collective-permute-done.19.refs_2_ = bf16[2,128,256]{2,1,0:T(8,128)(2,1)S(1)} collective-permute-done((bf16[2,128,256]{2,1,0:T(8,128)(2,1)S(1)}, bf16[2,128,256]{2,1,0:T(8,128)(2,1)S(1)}, u32[]{:S(2)}, u32[]{:S(2)}) %collective-permute-start.19) | collective-permute-done | bytes 131104 | tf_op jit(solution)/shard_map/ppermute | solution.py:286
  (88 shorter events, 15.5 us)
Async XLA Ops:
  2.5 16.6 %collective-permute-start = (bf16[128,512]{1,0:T(8,128)(2,1)S(1)}, bf16[128,512]{1,0:T(8,128)(2,1)}, u32[]{:S(2)}, u32[]{:S(2)}) collective-permute-start(bf16[128,512]{1,0:T(8,128)(2,1)S(1)} %pad_maximum_fusion.8), channel_id=1, source_target_pairs={{0,1},{1,2},{2,3},{3,0},{4,5},{5,6},{6,7},{7,4},{8,9},{9,10},{10,1... | collective-permute-start | bytes 393224 | tf_op jit(solution)/shard_map/ppermute | solution.py:286
  5.6 13.5 %collective-permute-start.1 = (bf16[128,512]{1,0:T(8,128)(2,1)S(1)}, bf16[128,512]{1,0:T(8,128)(2,1)}, u32[]{:S(2)}, u32[]{:S(2)}) collective-permute-start(bf16[128,512]{1,0:T(8,128)(2,1)S(1)} %pad_maximum_fusion.9), channel_id=1, source_target_pairs={{0,2},{1,3},{2,0},{3,1},{4,6},{5,7},{6,4},{7,5},{8,10},{9,11},{10,... | collective-permute-start | bytes 393224 | tf_op jit(solution)/shard_map/ppermute | solution.py:286
  8.2 10.8 %collective-permute-start.2 = (bf16[128,512]{1,0:T(8,128)(2,1)S(1)}, bf16[128,512]{1,0:T(8,128)(2,1)}, u32[]{:S(2)}, u32[]{:S(2)}) collective-permute-start(bf16[128,512]{1,0:T(8,128)(2,1)S(1)} %pad_maximum_fusion.10), channel_id=1, source_target_pairs={{0,3},{1,0},{2,1},{3,2},{4,7},{5,4},{6,5},{7,6},{8,11},{9,8},{10,9... | collective-permute-start | bytes 393224 | tf_op jit(solution)/shard_map/ppermute | solution.py:286
  19.1 28.7 %all-to-all-start = ((bf16[4,2,128,512]{3,2,1,0:T(8,128)(2,1)}), bf16[4,2,128,512]{3,2,1,0:T(8,128)(2,1)S(1)}, u32[]{:S(2)}, u32[]{:S(2)}) async-start(bf16[4,2,128,512]{3,2,1,0:T(8,128)(2,1)} %pad_maximum_fusion), calls=%async_computation | async-start | bytes 2097152 | tf_op jit(solution)/shard_map/all_to_all | solution.py:292
  23.7 29.0 %copy-start.5 = (bf16[4,128,512]{2,1,0:T(8,128)(2,1)}, bf16[4,128,512]{2,1,0:T(8,128)(2,1)S(1)}, u32[]{:S(2)}) copy-start(bf16[4,128,512]{2,1,0:T(8,128)(2,1)S(1)} %pad_maximum_fusion.1.refs_2_.refs_5_) | copy-start | bytes 1572868
  23.7 9.6 %collective-permute-start.3 = (bf16[4,128,512]{2,1,0:T(8,128)(2,1)S(1)}, bf16[4,128,512]{2,1,0:T(8,128)(2,1)S(1)}, u32[]{:S(2)}, u32[]{:S(2)}) collective-permute-start(bf16[4,128,512]{2,1,0:T(8,128)(2,1)S(1)} %pad_maximum_fusion.1.refs_2_.refs_5_), channel_id=1, source_target_pairs={{0,4},{4,8},{8,12},{12,16},{16,20},{20,24},{24,28},{28,0},{1,5},{5... | collective-permute-start | bytes 1572872 | tf_op jit(solution)/shard_map/ppermute | solution.py:286
  33.3 9.6 %collective-permute-start.4 = (bf16[4,128,512]{2,1,0:T(8,128)(2,1)S(1)}, bf16[4,128,512]{2,1,0:T(8,128)(2,1)}, u32[]{:S(2)}, u32[]{:S(2)}) collective-permute-start(bf16[4,128,512]{2,1,0:T(8,128)(2,1)S(1)} %collective-permute-done.3.refs_3_.refs_6_), channel_id=1, source_target_pairs={{0,4},{4,8},{8,12},{12,16},{16,20},{20,24},{24,28},{28,0},{1,5},{5... | collective-permute-start | bytes 1572872 | tf_op jit(solution)/shard_map/ppermute | solution.py:286
  42.9 9.8 %collective-permute-start.5 = (bf16[4,128,512]{2,1,0:T(8,128)(2,1)}, bf16[4,128,512]{2,1,0:T(8,128)(2,1)}, u32[]{:S(2)}, u32[]{:S(2)}) collective-permute-start(bf16[4,128,512]{2,1,0:T(8,128)(2,1)} %collective-permute-done.4.refs_4_.refs_7_), channel_id=1, source_target_pairs={{0,4},{4,8},{8,12},{12,16},{16,20},{20,24},{24,28},{28,0},{1,5},{5... | collective-permute-start | bytes 1572872 | tf_op jit(solution)/shard_map/ppermute | solution.py:286
  47.7 17.1 %collective-permute-start.6 = (bf16[2,128,512]{2,1,0:T(8,128)(2,1)S(1)}, bf16[2,128,512]{2,1,0:T(8,128)(2,1)S(1)}, u32[]{:S(2)}, u32[]{:S(2)}) collective-permute-start(bf16[2,128,512]{2,1,0:T(8,128)(2,1)S(1)} %pad_maximum_fusion.4), channel_id=1, source_target_pairs={{0,1},{1,2},{2,3},{3,0},{4,5},{5,6},{6,7},{7,4},{8,9},{9,10},{10,1... | collective-permute-start | bytes 786440 | tf_op jit(solution)/shard_map/ppermute | solution.py:286
  47.7 17.4 %collective-permute-start.7 = (bf16[2,128,512]{2,1,0:T(8,128)(2,1)S(1)}, bf16[2,128,512]{2,1,0:T(8,128)(2,1)S(1)}, u32[]{:S(2)}, u32[]{:S(2)}) collective-permute-start(bf16[2,128,512]{2,1,0:T(8,128)(2,1)S(1)} %pad_maximum_fusion.6), channel_id=1, source_target_pairs={{0,3},{1,0},{2,1},{3,2},{4,7},{5,4},{6,5},{7,6},{8,11},{9,8},{10,9... | collective-permute-start | bytes 786440 | tf_op jit(solution)/shard_map/ppermute | solution.py:286
  51.6 20.2 %collective-permute-start.8 = (bf16[2,128,512]{2,1,0:T(8,128)(2,1)S(1)}, bf16[2,128,512]{2,1,0:T(8,128)(2,1)}, u32[]{:S(2)}, u32[]{:S(2)}) collective-permute-start(bf16[2,128,512]{2,1,0:T(8,128)(2,1)S(1)} %pad_maximum_fusion.5), channel_id=1, source_target_pairs={{0,2},{1,3},{2,0},{3,1},{4,6},{5,7},{6,4},{7,5},{8,10},{9,11},{10,... | collective-permute-start | bytes 786440 | tf_op jit(solution)/shard_map/ppermute | solution.py:286
  63.4 19.1 %collective-permute-start.9 = (bf16[4,128,256]{2,1,0:T(8,128)(2,1)}, bf16[4,128,256]{2,1,0:T(8,128)(2,1)S(1)}, u32[]{:S(2)}, u32[]{:S(2)}) collective-permute-start(bf16[4,128,256]{2,1,0:T(8,128)(2,1)} %get-tuple-element.86), channel_id=1, source_target_pairs={{0,28},{4,0},{8,4},{12,8},{16,12},{20,16},{24,20},{28,24},{1,29},{... | collective-permute-start | bytes 786440 | tf_op jit(solution)/shard_map/ppermute | solution.py:286
  63.5 19.1 %collective-permute-start.10 = (bf16[4,128,256]{2,1,0:T(8,128)(2,1)}, bf16[4,128,256]{2,1,0:T(8,128)(2,1)S(1)}, u32[]{:S(2)}, u32[]{:S(2)}) collective-permute-start(bf16[4,128,256]{2,1,0:T(8,128)(2,1)} %get-tuple-element.87), channel_id=1, source_target_pairs={{0,24},{4,28},{8,0},{12,4},{16,8},{20,12},{24,16},{28,20},{1,25},{... | collective-permute-start | bytes 786440 | tf_op jit(solution)/shard_map/ppermute | solution.py:286
  64.8 17.7 %collective-permute-start.11 = (bf16[4,128,256]{2,1,0:T(8,128)(2,1)}, bf16[4,128,256]{2,1,0:T(8,128)(2,1)S(1)}, u32[]{:S(2)}, u32[]{:S(2)}) collective-permute-start(bf16[4,128,256]{2,1,0:T(8,128)(2,1)} %get-tuple-element.88), channel_id=1, source_target_pairs={{0,20},{4,24},{8,28},{12,0},{16,4},{20,8},{24,12},{28,16},{1,21},{... | collective-permute-start | bytes 786440 | tf_op jit(solution)/shard_map/ppermute | solution.py:286
  65.9 20.9 %all-to-all-start.1 = ((bf16[4,128,512]{2,1,0:T(8,128)(2,1)}), bf16[4,128,512]{2,1,0:T(8,128)(2,1)S(1)}, u32[]{:S(2)}, u32[]{:S(2)}) async-start(bf16[4,128,512]{2,1,0:T(8,128)(2,1)} %get-tuple-element.79), calls=%async_computation.1 | async-start | bytes 1048576 | tf_op jit(solution)/shard_map/all_to_all | solution.py:292
  82.6 6.4 %collective-permute-start.12 = (bf16[4,128,256]{2,1,0:T(8,128)(2,1)}, bf16[4,128,256]{2,1,0:T(8,128)(2,1)S(1)}, u32[]{:S(2)}, u32[]{:S(2)}) collective-permute-start(bf16[4,128,256]{2,1,0:T(8,128)(2,1)} %get-tuple-element.94), channel_id=1, source_target_pairs={{0,28},{4,0},{8,4},{12,8},{16,12},{20,16},{24,20},{28,24},{1,29},{... | collective-permute-start | bytes 786440 | tf_op jit(solution)/shard_map/ppermute | solution.py:286
  83.1 15.1 %collective-permute-start.13 = (bf16[4,128,256]{2,1,0:T(8,128)(2,1)}, bf16[4,128,256]{2,1,0:T(8,128)(2,1)S(1)}, u32[]{:S(2)}, u32[]{:S(2)}) collective-permute-start(bf16[4,128,256]{2,1,0:T(8,128)(2,1)} %get-tuple-element.95), channel_id=1, source_target_pairs={{0,24},{4,28},{8,0},{12,4},{16,8},{20,12},{24,16},{28,20},{1,25},{... | collective-permute-start | bytes 786440 | tf_op jit(solution)/shard_map/ppermute | solution.py:286
  85.4 12.8 %collective-permute-start.14 = (bf16[4,128,256]{2,1,0:T(8,128)(2,1)}, bf16[4,128,256]{2,1,0:T(8,128)(2,1)S(1)}, u32[]{:S(2)}, u32[]{:S(2)}) collective-permute-start(bf16[4,128,256]{2,1,0:T(8,128)(2,1)} %get-tuple-element.96), channel_id=1, source_target_pairs={{0,20},{4,24},{8,28},{12,0},{16,4},{20,8},{24,12},{28,16},{1,21},{... | collective-permute-start | bytes 786440 | tf_op jit(solution)/shard_map/ppermute | solution.py:286
  86.8 11.6 %collective-permute-start.15 = (bf16[128,512]{1,0:T(8,128)(2,1)S(1)}, bf16[128,512]{1,0:T(8,128)(2,1)S(1)}, u32[]{:S(2)}, u32[]{:S(2)}) collective-permute-start(bf16[128,512]{1,0:T(8,128)(2,1)S(1)} %copy-done.18), channel_id=1, source_target_pairs={{0,3},{1,0},{2,1},{3,2},{4,7},{5,4},{6,5},{7,6},{8,11},{9,8},{10,9... | collective-permute-start | bytes 393224 | tf_op jit(solution)/shard_map/ppermute | solution.py:286
  89.0 11.8 %collective-permute-start.16 = (bf16[128,512]{1,0:T(8,128)(2,1)S(1)}, bf16[128,512]{1,0:T(8,128)(2,1)S(1)}, u32[]{:S(2)}, u32[]{:S(2)}) collective-permute-start(bf16[128,512]{1,0:T(8,128)(2,1)S(1)} %copy-done.17), channel_id=1, source_target_pairs={{0,2},{1,3},{2,0},{3,1},{4,6},{5,7},{6,4},{7,5},{8,10},{9,11},{10,... | collective-permute-start | bytes 393224 | tf_op jit(solution)/shard_map/ppermute | solution.py:286
  89.0 11.8 %collective-permute-start.17 = (bf16[128,512]{1,0:T(8,128)(2,1)S(1)}, bf16[128,512]{1,0:T(8,128)(2,1)S(1)}, u32[]{:S(2)}, u32[]{:S(2)}) collective-permute-start(bf16[128,512]{1,0:T(8,128)(2,1)S(1)} %copy-done.16), channel_id=1, source_target_pairs={{0,1},{1,2},{2,3},{3,0},{4,5},{5,6},{6,7},{7,4},{8,9},{9,10},{10,1... | collective-permute-start | bytes 393224 | tf_op jit(solution)/shard_map/ppermute | solution.py:286
  100.9 8.3 %collective-permute-start.20 = (bf16[2,128,256]{2,1,0:T(8,128)(2,1)S(1)}, bf16[2,128,256]{2,1,0:T(8,128)(2,1)S(1)}, u32[]{:S(2)}, u32[]{:S(2)}) collective-permute-start(bf16[2,128,256]{2,1,0:T(8,128)(2,1)S(1)} %get-tuple-element.121), channel_id=1, source_target_pairs={{0,1},{1,2},{2,3},{3,0},{4,5},{5,6},{6,7},{7,4},{8,9},{9,10},{10,1... | collective-permute-start | bytes 393224 | tf_op jit(solution)/shard_map/ppermute | solution.py:286
  101.4 12.2 %collective-permute-start.19 = (bf16[2,128,256]{2,1,0:T(8,128)(2,1)S(1)}, bf16[2,128,256]{2,1,0:T(8,128)(2,1)S(1)}, u32[]{:S(2)}, u32[]{:S(2)}) collective-permute-start(bf16[2,128,256]{2,1,0:T(8,128)(2,1)S(1)} %get-tuple-element.122), channel_id=1, source_target_pairs={{0,2},{1,3},{2,0},{3,1},{4,6},{5,7},{6,4},{7,5},{8,10},{9,11},{10,... | collective-permute-start | bytes 393224 | tf_op jit(solution)/shard_map/ppermute | solution.py:286
  103.4 10.2 %collective-permute-start.18 = (bf16[2,128,256]{2,1,0:T(8,128)(2,1)S(1)}, bf16[2,128,256]{2,1,0:T(8,128)(2,1)S(1)}, u32[]{:S(2)}, u32[]{:S(2)}) collective-permute-start(bf16[2,128,256]{2,1,0:T(8,128)(2,1)S(1)} %get-tuple-element.123), channel_id=1, source_target_pairs={{0,3},{1,0},{2,1},{3,2},{4,7},{5,4},{6,5},{7,6},{8,11},{9,8},{10,9... | collective-permute-start | bytes 393224 | tf_op jit(solution)/shard_map/ppermute | solution.py:286
  (18 other events, 119.2 us)

commit v6 on v5

--- a/solution.py
+++ b/solution.py
@@ -250,6 +250,37 @@
     return out[:splits] if go_apart else out[0], out[-WINDOW:]
 
 
+def from_columns(z, arrays, starts, width, apart):
+    rows, count = arrays[0].shape[0], len(starts(0))
+    shape = (len(arrays), rows, width)
+
+    def kernel(z_ref, *refs):
+        array_refs, out_refs, sem_ref = refs[: len(arrays)], refs[len(arrays) : -1], refs[-1]
+        copies = []
+        for i, start in enumerate(starts(z_ref[0])):
+            at = pl.ds(pl.multiple_of(start, HEAD_SIZE), width)
+            out = out_refs[i] if apart else out_refs[0].at[i]
+            copies += [
+                pltpu.make_async_copy(array.at[:, at], out.at[k], sem_ref.at[i, k])
+                for k, array in enumerate(array_refs)
+            ]
+        for copy in copies:
+            copy.start()
+        for copy in copies:
+            copy.wait()
+
+    shapes = [shape] * count if apart else [(count,) + shape]
+    return pl.pallas_call(
+        kernel,
+        in_specs=[pl.BlockSpec(memory_space=pltpu.SMEM)]
+        + [pl.BlockSpec(memory_space=pl.ANY)] * len(arrays),
+        out_specs=[pl.BlockSpec(memory_space=pltpu.VMEM)] * len(shapes),
+        out_shape=[jax.ShapeDtypeStruct(one, LOW) for one in shapes],
+        scratch_shapes=[pltpu.SemaphoreType.DMA((count, len(arrays)))],
+        compiler_params=pltpu.CompilerParams(vmem_limit_bytes=8 * 1024 * 1024),
+    )(z.astype(jnp.int32)[None], *arrays)
+
+
 def in_columns(parts, z, places, outs):
     rows = parts[0].shape[-2]
 
@@ -312,27 +343,25 @@
         )
 
     parts = exchange([for_device_ahead(s) for s in range(splits)], 1)
+    group = GROUP * HEAD_SIZE
+
     def in_order(j):
-        split = [
-            array.reshape(rows, splits, local, GROUP * HEAD_SIZE)[:, :, j].swapaxes(0, 1)
-            for array in (query, d_out)
-        ]
-        return jnp.stack(split, axis=1)
+        def starts(_):
+            return [(g * local + j) * group for g in range(splits)]
+
+        return from_columns(z, (query, d_out), starts, group, False)[0]
 
     def apart(j):
-        start = [(lax.rem(z + s, splits) * local + j) * GROUP * HEAD_SIZE for s in range(splits)]
-        return [
-            jnp.stack(
-                [
-                    lax.dynamic_slice_in_dim(array, at, GROUP * HEAD_SIZE, 1)
-                    for array in (query, d_out)
-                ]
-            )
-            for at in start
-        ]
-
+        def starts(place):
+            return [(lax.rem(place + s, splits) * local + j) * group for s in range(splits)]
+
+        return from_columns(z, (query, d_out), starts, group, True)
+
+    near = [s for s in range(1, splits) if 2 * s != splits]
     both = [in_order(0)] + [apart(j) for j in range(1, local)]
-    *both, parts = fence((*both, parts))
+    *both, came = fence((*both, [parts[s] for s in near]))
+    for s, part in zip(near, came):
+        parts[s] = part
 
     blocks = [jnp.stack(parts)]
     for _ in range(1, WINDOW):
@@ -348,7 +377,6 @@
     def add(dkv):
         return sum(d.astype(WIDE) for d in dkv).astype(LOW)
 
-    near = [s for s in range(1, splits) if 2 * s != splits]
     dq, dkv = [], []
     for j in range(local):
         last = j > 0 and j == local - 1

time: 115 us -> 110 us (0.957)
  local copies, waits for them, and re-layouts: 10.6 us -> 4.58 us
  other arithmetic: 3.37 us -> 0.46 us
  starting transfers between devices: 34.2 us -> 36.2 us
  Pallas kernels: 23.4 us -> 24.8 us
    unnamed x42 -> x30, local copies, waits for them, and re-layouts: 6.37 us -> 2.72 us
    another operation x5 -> x0, other arithmetic: 1.88 us -> none  [the longest x1 1.06 us: in_order(): return jnp.stack(split, axis=1)]
    all_to_all x2, starting transfers between devices: 8.58 us -> 10.4 us  [swap(): lax.all_to_all(array, 'head', split_axis=0, concat_axis=0, tiled=True)]
    slice x2 -> x0, local copies, waits for them, and re-layouts: 1.66 us -> none  [in_order(): array.reshape(rows, splits, local, GROUP * HEAD_SIZE)[:, :, j]]
    pallas_call x0 -> x2, Pallas kernels: none -> 1.46 us  [from_columns(): pl.pallas_call(kernel, in_specs=[pl.BlockSpec(memory_space=pltpu.SMEM)] +...]
  transfers between devices with their start and end apart: 23 -> 23, of which waited for: 9 -> 12; matrix products, arithmetic and copies ran while one was open for 9% -> 1% of each run, Pallas kernels for 20% -> 22%
where the time goes in v6:
time: 110 us; the launch traced here: 109 us
  waiting for transfers between devices  41.8 us (38%)
  starting transfers between devices  36.2 us (33%)
  Pallas kernels  24.8 us (23%)
  local copies, waits for them, and re-layouts  4.58 us (4%)
    ppermute x21, waiting for transfers between devices, shift(): lax.ppermute(array, axis, [(i, (i + by) % size) for i in range(size)])  38.7 us
    ppermute x21, starting transfers between devices, shift(): lax.ppermute(array, axis, [(i, (i + by) % size) for i in range(size)])  25.8 us
    pallas_call x2, Pallas kernels, attention(): pl.pallas_call(kernel, grid=(heads // at_once,), in_specs=[pl.BlockSpec(m...  21.4 us
    all_to_all x2, starting transfers between devices, swap(): lax.all_to_all(array, 'head', split_axis=0, concat_axis=0, tiled=True)  10.4 us
    all_to_all x2, waiting for transfers between devices, swap(): lax.all_to_all(array, 'head', split_axis=0, concat_axis=0, tiled=True)  3.07 us
    unnamed x30, local copies, waits for them, and re-layouts  2.72 us
  transfers between devices with their start and end apart: 23, of which 12 were waited for; matrix products, arithmetic and copies ran while one was open for 1% of the time, Pallas kernels for 22%

profile of v6, /device:TPU:0, one launch (start us, length us, event | category | flops | bytes accessed | tf_op | source)
XLA Modules:
  0.0 108.8 jit_solution(1359468905493171542)
XLA Ops:
  1.8 3.1 %collective-permute-start = (bf16[128,512]{1,0:T(8,128)(2,1)S(1)}, bf16[128,512]{1,0:T(8,128)(2,1)S(1)}, u32[]{:S(2)}, u32[]{:S(2)}) collective-permute-start(bf16[128,512]{1,0:T(8,128)(2,1)S(1)} %pad_maximum_fusion.2), channel_id=1, source_target_pairs={{0,1},{1,2},{2,3},{3,0},{4,5},{5,6},{6,7},{7,4},{8,9},{9,10},{10,1... | collective-permute-start | bytes 393224 | tf_op jit(solution)/shard_map/ppermute | solution.py:317
  4.9 2.1 %collective-permute-start.1 = (bf16[128,512]{1,0:T(8,128)(2,1)S(1)}, bf16[128,512]{1,0:T(8,128)(2,1)S(1)}, u32[]{:S(2)}, u32[]{:S(2)}) collective-permute-start(bf16[128,512]{1,0:T(8,128)(2,1)S(1)} %pad_maximum_fusion.3), channel_id=1, source_target_pairs={{0,3},{1,0},{2,1},{3,2},{4,7},{5,4},{6,5},{7,6},{8,11},{9,8},{10,9... | collective-permute-start | bytes 393224 | tf_op jit(solution)/shard_map/ppermute | solution.py:317
  8.1 1.2 %copy-done.1 = bf16[128,4096]{1,0:T(8,128)(2,1)S(1)} copy-done((bf16[128,4096]{1,0:T(8,128)(2,1)S(1)}, bf16[128,4096]{1,0:T(8,128)(2,1)}, u32[]{:S(2)}) %copy-start.1) | copy-done | bytes 1048600
  9.3 1.2 %shard_map.76 = bf16[4,2,128,512]{3,2,1,0:T(8,128)(2,1)} custom-call(s32[1]{0:T(128)} %bitcast.z_ref, bf16[128,4096]{1,0:T(8,128)(2,1)S(1)} %copy-done, bf16[128,4096]{1,0:T(8,128)(2,1)S(1)} %copy-done.1), custom_call_target="tpu_custom_call" | custom-call | tf_op jit(solution)/shard_map/pallas_call | solution.py:273
  11.6 1.2 %collective-permute-done.1 = bf16[128,512]{1,0:T(8,128)(2,1)S(1)} collective-permute-done((bf16[128,512]{1,0:T(8,128)(2,1)S(1)}, bf16[128,512]{1,0:T(8,128)(2,1)S(1)}, u32[]{:S(2)}, u32[]{:S(2)}) %collective-permute-start.1) | collective-permute-done | bytes 131104 | tf_op jit(solution)/shard_map/ppermute | solution.py:317
  12.8 5.7 %all-to-all-start = ((bf16[4,2,128,512]{3,2,1,0:T(8,128)(2,1)}), bf16[4,2,128,512]{3,2,1,0:T(8,128)(2,1)S(1)}, u32[]{:S(2)}, u32[]{:S(2)}) async-start(bf16[4,2,128,512]{3,2,1,0:T(8,128)(2,1)} %shard_map.76), calls=%async_computation | async-start | bytes 2097152 | tf_op jit(solution)/shard_map/all_to_all | solution.py:323
  19.0 9.5 %collective-permute-done.3.refs_3_.refs_6_ = bf16[4,128,512]{2,1,0:T(8,128)(2,1)S(1)} collective-permute-done((bf16[4,128,512]{2,1,0:T(8,128)(2,1)S(1)}, bf16[4,128,512]{2,1,0:T(8,128)(2,1)S(1)}, u32[]{:S(2)}, u32[]{:S(2)}) %collective-permute-start.3) | collective-permute-done | bytes 524320 | tf_op jit(solution)/shard_map/ppermute | solution.py:317
  28.5 9.6 %collective-permute-done.4.refs_4_.refs_7_ = bf16[4,128,512]{2,1,0:T(8,128)(2,1)} collective-permute-done((bf16[4,128,512]{2,1,0:T(8,128)(2,1)S(1)}, bf16[4,128,512]{2,1,0:T(8,128)(2,1)}, u32[]{:S(2)}, u32[]{:S(2)}) %collective-permute-start.4) | collective-permute-done | bytes 524320 | tf_op jit(solution)/shard_map/ppermute | solution.py:317
  38.8 3.1 %all-to-all-done.refs_1_ = bf16[4,2,128,512]{3,2,1,0:T(8,128)(2,1)S(1)} async-done(((bf16[4,2,128,512]{3,2,1,0:T(8,128)(2,1)}), bf16[4,2,128,512]{3,2,1,0:T(8,128)(2,1)S(1)}, u32[]{:S(2)}, u32[]{:S(2)}) %all-to-all-start) | async-done | bytes 1048608 | tf_op jit(solution)/shard_map/all_to_all | solution.py:323
  41.9 3.8 %collective-permute-start.7 = (bf16[2,128,512]{2,1,0:T(8,128)(2,1)S(1)}, bf16[2,128,512]{2,1,0:T(8,128)(2,1)S(1)}, u32[]{:S(2)}, u32[]{:S(2)}) collective-permute-start(bf16[2,128,512]{2,1,0:T(8,128)(2,1)S(1)} %get-tuple-element.75), channel_id=1, source_target_pairs={{0,3},{1,0},{2,1},{3,2},{4,7},{5,4},{6,5},{7,6},{8,11},{9,8},{10,9... | collective-permute-start | bytes 786440 | tf_op jit(solution)/shard_map/ppermute | solution.py:317
  45.7 2.2 %collective-permute-done.5.refs_5_.refs_8_ = bf16[4,128,512]{2,1,0:T(8,128)(2,1)} collective-permute-done((bf16[4,128,512]{2,1,0:T(8,128)(2,1)}, bf16[4,128,512]{2,1,0:T(8,128)(2,1)}, u32[]{:S(2)}, u32[]{:S(2)}) %collective-permute-start.5) | collective-permute-done | bytes 524320 | tf_op jit(solution)/shard_map/ppermute | solution.py:317
  48.0 10.7 %shard_map.78 = (bf16[4,128,512]{2,1,0:T(8,128)(2,1)}, bf16[4,128,256]{2,1,0:T(8,128)(2,1)}, bf16[4,128,256]{2,1,0:T(8,128)(2,1)}, bf16[4,128,256]{2,1,0:T(8,128)(2,1)}, bf16[4,128,256]{2,1,0:T(8,128)(2,1)}) custom-call(s32[9]{0:T(128)} %concatenate.15.refs_0_, bf16[4,2,128,512]{3,2,1,0:T(8,128)(2,1)} %copy-done.4, bf16[4,128,512]{2,1,0:T(8,128)(2,1)} %copy-done.5, ...), custom_call_target="tpu_custom_call" | custom-call | flops 12079595520 | bytes 4194304 | tf_op jit(solution)/shard_map/pallas_call | solution.py:220
  59.0 1.3 %collective-permute-start.11 = (bf16[4,128,256]{2,1,0:T(8,128)(2,1)}, bf16[4,128,256]{2,1,0:T(8,128)(2,1)S(1)}, u32[]{:S(2)}, u32[]{:S(2)}) collective-permute-start(bf16[4,128,256]{2,1,0:T(8,128)(2,1)} %get-tuple-element.92), channel_id=1, source_target_pairs={{0,20},{4,24},{8,28},{12,0},{16,4},{20,8},{24,12},{28,16},{1,21},{... | collective-permute-start | bytes 786440 | tf_op jit(solution)/shard_map/ppermute | solution.py:317
  61.1 4.7 %all-to-all-start.1 = ((bf16[4,128,512]{2,1,0:T(8,128)(2,1)}), bf16[4,128,512]{2,1,0:T(8,128)(2,1)S(1)}, u32[]{:S(2)}, u32[]{:S(2)}) async-start(bf16[4,128,512]{2,1,0:T(8,128)(2,1)} %get-tuple-element.83), calls=%async_computation.1 | async-start | bytes 1048576 | tf_op jit(solution)/shard_map/all_to_all | solution.py:323
  66.1 10.8 %shard_map.79 = (bf16[128,512]{1,0:T(8,128)(2,1)}, bf16[128,512]{1,0:T(8,128)(2,1)}, bf16[128,512]{1,0:T(8,128)(2,1)}, bf16[128,512]{1,0:T(8,128)(2,1)}, bf16[4,...) custom-call(s32[9]{0:T(128)} %concatenate.15.refs_0_, ...), custom_call_target="tpu_custom_call" | custom-call | flops 12079595520 | bytes 4194304 | tf_op jit(solution)/shard_map/pallas_call | solution.py:220
  76.9 1.7 %collective-permute-start.12 = (bf16[4,128,256]{2,1,0:T(8,128)(2,1)}, bf16[4,128,256]{2,1,0:T(8,128)(2,1)S(1)}, u32[]{:S(2)}, u32[]{:S(2)}) collective-permute-start(bf16[4,128,256]{2,1,0:T(8,128)(2,1)} %get-tuple-element.98), channel_id=1, source_target_pairs={{0,28},{4,0},{8,4},{12,8},{16,12},{20,16},{24,20},{28,24},{1,29},{... | collective-permute-start | bytes 786440 | tf_op jit(solution)/shard_map/ppermute | solution.py:317
  78.6 1.6 %collective-permute-start.13 = (bf16[4,128,256]{2,1,0:T(8,128)(2,1)}, bf16[4,128,256]{2,1,0:T(8,128)(2,1)S(1)}, u32[]{:S(2)}, u32[]{:S(2)}) collective-permute-start(bf16[4,128,256]{2,1,0:T(8,128)(2,1)} %get-tuple-element.99), channel_id=1, source_target_pairs={{0,24},{4,28},{8,0},{12,4},{16,8},{20,12},{24,16},{28,20},{1,25},{... | collective-permute-start | bytes 786440 | tf_op jit(solution)/shard_map/ppermute | solution.py:317
  80.3 1.3 %collective-permute-start.14 = (bf16[4,128,256]{2,1,0:T(8,128)(2,1)}, bf16[4,128,256]{2,1,0:T(8,128)(2,1)S(1)}, u32[]{:S(2)}, u32[]{:S(2)}) collective-permute-start(bf16[4,128,256]{2,1,0:T(8,128)(2,1)} %get-tuple-element.100), channel_id=1, source_target_pairs={{0,20},{4,24},{8,28},{12,0},{16,4},{20,8},{24,12},{28,16},{1,21},{... | collective-permute-start | bytes 786440 | tf_op jit(solution)/shard_map/ppermute | solution.py:317
  81.7 2.1 %collective-permute-start.15 = (bf16[128,512]{1,0:T(8,128)(2,1)S(1)}, bf16[128,512]{1,0:T(8,128)(2,1)S(1)}, u32[]{:S(2)}, u32[]{:S(2)}) collective-permute-start(bf16[128,512]{1,0:T(8,128)(2,1)S(1)} %copy-done.14), channel_id=1, source_target_pairs={{0,3},{1,0},{2,1},{3,2},{4,7},{5,4},{6,5},{7,6},{8,11},{9,8},{10,9... | collective-permute-start | bytes 393224 | tf_op jit(solution)/shard_map/ppermute | solution.py:317
  85.7 7.4 %collective-permute-done.13 = bf16[4,128,256]{2,1,0:T(8,128)(2,1)S(1)} collective-permute-done((bf16[4,128,256]{2,1,0:T(8,128)(2,1)}, bf16[4,128,256]{2,1,0:T(8,128)(2,1)S(1)}, u32[]{:S(2)}, u32[]{:S(2)}) %collective-permute-start.13) | collective-permute-done | bytes 262176 | tf_op jit(solution)/shard_map/ppermute | solution.py:317
  93.3 2.0 %collective-permute-done.16.refs_3_ = bf16[128,512]{1,0:T(8,128)(2,1)S(1)} collective-permute-done((bf16[128,512]{1,0:T(8,128)(2,1)S(1)}, bf16[128,512]{1,0:T(8,128)(2,1)S(1)}, u32[]{:S(2)}, u32[]{:S(2)}) %collective-permute-start.16) | collective-permute-done | bytes 131104 | tf_op jit(solution)/shard_map/ppermute | solution.py:317
  96.5 2.0 %collective-permute-start.19 = (bf16[2,128,256]{2,1,0:T(8,128)(2,1)S(1)}, bf16[2,128,256]{2,1,0:T(8,128)(2,1)S(1)}, u32[]{:S(2)}, u32[]{:S(2)}) collective-permute-start(bf16[2,128,256]{2,1,0:T(8,128)(2,1)S(1)} %get-tuple-element.118), channel_id=1, source_target_pairs={{0,2},{1,3},{2,0},{3,1},{4,6},{5,7},{6,4},{7,5},{8,10},{9,11},{10,... | collective-permute-start | bytes 393224 | tf_op jit(solution)/shard_map/ppermute | solution.py:317
  98.5 2.8 %collective-permute-start.18 = (bf16[2,128,256]{2,1,0:T(8,128)(2,1)S(1)}, bf16[2,128,256]{2,1,0:T(8,128)(2,1)S(1)}, u32[]{:S(2)}, u32[]{:S(2)}) collective-permute-start(bf16[2,128,256]{2,1,0:T(8,128)(2,1)S(1)} %get-tuple-element.119), channel_id=1, source_target_pairs={{0,3},{1,0},{2,1},{3,2},{4,7},{5,4},{6,5},{7,6},{8,11},{9,8},{10,9... | collective-permute-start | bytes 393224 | tf_op jit(solution)/shard_map/ppermute | solution.py:317
  102.9 5.0 %collective-permute-done.19.refs_2_ = bf16[2,128,256]{2,1,0:T(8,128)(2,1)S(1)} collective-permute-done((bf16[2,128,256]{2,1,0:T(8,128)(2,1)S(1)}, bf16[2,128,256]{2,1,0:T(8,128)(2,1)S(1)}, u32[]{:S(2)}, u32[]{:S(2)}) %collective-permute-start.19) | collective-permute-done | bytes 131104 | tf_op jit(solution)/shard_map/ppermute | solution.py:317
  (70 shorter events, 11.7 us)
Async XLA Ops:
  1.8 9.7 %collective-permute-start = (bf16[128,512]{1,0:T(8,128)(2,1)S(1)}, bf16[128,512]{1,0:T(8,128)(2,1)S(1)}, u32[]{:S(2)}, u32[]{:S(2)}) collective-permute-start(bf16[128,512]{1,0:T(8,128)(2,1)S(1)} %pad_maximum_fusion.2), channel_id=1, source_target_pairs={{0,1},{1,2},{2,3},{3,0},{4,5},{5,6},{6,7},{7,4},{8,9},{9,10},{10,1... | collective-permute-start | bytes 393224 | tf_op jit(solution)/shard_map/ppermute | solution.py:317
  4.9 7.8 %collective-permute-start.1 = (bf16[128,512]{1,0:T(8,128)(2,1)S(1)}, bf16[128,512]{1,0:T(8,128)(2,1)S(1)}, u32[]{:S(2)}, u32[]{:S(2)}) collective-permute-start(bf16[128,512]{1,0:T(8,128)(2,1)S(1)} %pad_maximum_fusion.3), channel_id=1, source_target_pairs={{0,3},{1,0},{2,1},{3,2},{4,7},{5,4},{6,5},{7,6},{8,11},{9,8},{10,9... | collective-permute-start | bytes 393224 | tf_op jit(solution)/shard_map/ppermute | solution.py:317
  7.1 11.8 %collective-permute-start.2 = (bf16[128,512]{1,0:T(8,128)(2,1)S(1)}, bf16[128,512]{1,0:T(8,128)(2,1)S(1)}, u32[]{:S(2)}, u32[]{:S(2)}) collective-permute-start(bf16[128,512]{1,0:T(8,128)(2,1)S(1)} %pad_maximum_fusion.4), channel_id=1, source_target_pairs={{0,2},{1,3},{2,0},{3,1},{4,6},{5,7},{6,4},{7,5},{8,10},{9,11},{10,... | collective-permute-start | bytes 393224 | tf_op jit(solution)/shard_map/ppermute | solution.py:317
  12.8 29.1 %all-to-all-start = ((bf16[4,2,128,512]{3,2,1,0:T(8,128)(2,1)}), bf16[4,2,128,512]{3,2,1,0:T(8,128)(2,1)S(1)}, u32[]{:S(2)}, u32[]{:S(2)}) async-start(bf16[4,2,128,512]{3,2,1,0:T(8,128)(2,1)} %shard_map.76), calls=%async_computation | async-start | bytes 2097152 | tf_op jit(solution)/shard_map/all_to_all | solution.py:323
  18.9 29.0 %copy-start.5 = (bf16[4,128,512]{2,1,0:T(8,128)(2,1)}, bf16[4,128,512]{2,1,0:T(8,128)(2,1)S(1)}, u32[]{:S(2)}) copy-start(bf16[4,128,512]{2,1,0:T(8,128)(2,1)S(1)} %pad_maximum_fusion.refs_2_.refs_5_) | copy-start | bytes 1572868
  19.0 9.6 %collective-permute-start.3 = (bf16[4,128,512]{2,1,0:T(8,128)(2,1)S(1)}, bf16[4,128,512]{2,1,0:T(8,128)(2,1)S(1)}, u32[]{:S(2)}, u32[]{:S(2)}) collective-permute-start(bf16[4,128,512]{2,1,0:T(8,128)(2,1)S(1)} %pad_maximum_fusion.refs_2_.refs_5_), channel_id=1, source_target_pairs={{0,4},{4,8},{8,12},{12,16},{16,20},{20,24},{24,28},{28,0},{1,5},{5... | collective-permute-start | bytes 1572872 | tf_op jit(solution)/shard_map/ppermute | solution.py:317
  28.5 9.6 %collective-permute-start.4 = (bf16[4,128,512]{2,1,0:T(8,128)(2,1)S(1)}, bf16[4,128,512]{2,1,0:T(8,128)(2,1)}, u32[]{:S(2)}, u32[]{:S(2)}) collective-permute-start(bf16[4,128,512]{2,1,0:T(8,128)(2,1)S(1)} %collective-permute-done.3.refs_3_.refs_6_), channel_id=1, source_target_pairs={{0,4},{4,8},{8,12},{12,16},{16,20},{20,24},{24,28},{28,0},{1,5},{5... | collective-permute-start | bytes 1572872 | tf_op jit(solution)/shard_map/ppermute | solution.py:317
  38.1 9.8 %collective-permute-start.5 = (bf16[4,128,512]{2,1,0:T(8,128)(2,1)}, bf16[4,128,512]{2,1,0:T(8,128)(2,1)}, u32[]{:S(2)}, u32[]{:S(2)}) collective-permute-start(bf16[4,128,512]{2,1,0:T(8,128)(2,1)} %collective-permute-done.4.refs_4_.refs_7_), channel_id=1, source_target_pairs={{0,4},{4,8},{8,12},{12,16},{16,20},{20,24},{24,28},{28,0},{1,5},{5... | collective-permute-start | bytes 1572872 | tf_op jit(solution)/shard_map/ppermute | solution.py:317
  41.9 17.1 %collective-permute-start.6 = (bf16[2,128,512]{2,1,0:T(8,128)(2,1)S(1)}, bf16[2,128,512]{2,1,0:T(8,128)(2,1)S(1)}, u32[]{:S(2)}, u32[]{:S(2)}) collective-permute-start(bf16[2,128,512]{2,1,0:T(8,128)(2,1)S(1)} %get-tuple-element.74), channel_id=1, source_target_pairs={{0,1},{1,2},{2,3},{3,0},{4,5},{5,6},{6,7},{7,4},{8,9},{9,10},{10,1... | collective-permute-start | bytes 786440 | tf_op jit(solution)/shard_map/ppermute | solution.py:317
  41.9 18.5 %collective-permute-start.7 = (bf16[2,128,512]{2,1,0:T(8,128)(2,1)S(1)}, bf16[2,128,512]{2,1,0:T(8,128)(2,1)S(1)}, u32[]{:S(2)}, u32[]{:S(2)}) collective-permute-start(bf16[2,128,512]{2,1,0:T(8,128)(2,1)S(1)} %get-tuple-element.75), channel_id=1, source_target_pairs={{0,3},{1,0},{2,1},{3,2},{4,7},{5,4},{6,5},{7,6},{8,11},{9,8},{10,9... | collective-permute-start | bytes 786440 | tf_op jit(solution)/shard_map/ppermute | solution.py:317
  45.7 20.3 %collective-permute-start.8 = (bf16[2,128,512]{2,1,0:T(8,128)(2,1)S(1)}, bf16[2,128,512]{2,1,0:T(8,128)(2,1)}, u32[]{:S(2)}, u32[]{:S(2)}) collective-permute-start(bf16[2,128,512]{2,1,0:T(8,128)(2,1)S(1)} %get-tuple-element.77), channel_id=1, source_target_pairs={{0,2},{1,3},{2,0},{3,1},{4,6},{5,7},{6,4},{7,5},{8,10},{9,11},{10,... | collective-permute-start | bytes 786440 | tf_op jit(solution)/shard_map/ppermute | solution.py:317
  58.6 18.2 %collective-permute-start.9 = (bf16[4,128,256]{2,1,0:T(8,128)(2,1)}, bf16[4,128,256]{2,1,0:T(8,128)(2,1)S(1)}, u32[]{:S(2)}, u32[]{:S(2)}) collective-permute-start(bf16[4,128,256]{2,1,0:T(8,128)(2,1)} %get-tuple-element.90), channel_id=1, source_target_pairs={{0,28},{4,0},{8,4},{12,8},{16,12},{20,16},{24,20},{28,24},{1,29},{... | collective-permute-start | bytes 786440 | tf_op jit(solution)/shard_map/ppermute | solution.py:317
  58.7 18.2 %collective-permute-start.10 = (bf16[4,128,256]{2,1,0:T(8,128)(2,1)}, bf16[4,128,256]{2,1,0:T(8,128)(2,1)S(1)}, u32[]{:S(2)}, u32[]{:S(2)}) collective-permute-start(bf16[4,128,256]{2,1,0:T(8,128)(2,1)} %get-tuple-element.91), channel_id=1, source_target_pairs={{0,24},{4,28},{8,0},{12,4},{16,8},{20,12},{24,16},{28,20},{1,25},{... | collective-permute-start | bytes 786440 | tf_op jit(solution)/shard_map/ppermute | solution.py:317
  59.0 17.8 %collective-permute-start.11 = (bf16[4,128,256]{2,1,0:T(8,128)(2,1)}, bf16[4,128,256]{2,1,0:T(8,128)(2,1)S(1)}, u32[]{:S(2)}, u32[]{:S(2)}) collective-permute-start(bf16[4,128,256]{2,1,0:T(8,128)(2,1)} %get-tuple-element.92), channel_id=1, source_target_pairs={{0,20},{4,24},{8,28},{12,0},{16,4},{20,8},{24,12},{28,16},{1,21},{... | collective-permute-start | bytes 786440 | tf_op jit(solution)/shard_map/ppermute | solution.py:317
  61.1 20.6 %all-to-all-start.1 = ((bf16[4,128,512]{2,1,0:T(8,128)(2,1)}), bf16[4,128,512]{2,1,0:T(8,128)(2,1)S(1)}, u32[]{:S(2)}, u32[]{:S(2)}) async-start(bf16[4,128,512]{2,1,0:T(8,128)(2,1)} %get-tuple-element.83), calls=%async_computation.1 | async-start | bytes 1048576 | tf_op jit(solution)/shard_map/all_to_all | solution.py:323
  76.9 7.7 %collective-permute-start.12 = (bf16[4,128,256]{2,1,0:T(8,128)(2,1)}, bf16[4,128,256]{2,1,0:T(8,128)(2,1)S(1)}, u32[]{:S(2)}, u32[]{:S(2)}) collective-permute-start(bf16[4,128,256]{2,1,0:T(8,128)(2,1)} %get-tuple-element.98), channel_id=1, source_target_pairs={{0,28},{4,0},{8,4},{12,8},{16,12},{20,16},{24,20},{28,24},{1,29},{... | collective-permute-start | bytes 786440 | tf_op jit(solution)/shard_map/ppermute | solution.py:317
  78.6 14.5 %collective-permute-start.13 = (bf16[4,128,256]{2,1,0:T(8,128)(2,1)}, bf16[4,128,256]{2,1,0:T(8,128)(2,1)S(1)}, u32[]{:S(2)}, u32[]{:S(2)}) collective-permute-start(bf16[4,128,256]{2,1,0:T(8,128)(2,1)} %get-tuple-element.99), channel_id=1, source_target_pairs={{0,24},{4,28},{8,0},{12,4},{16,8},{20,12},{24,16},{28,20},{1,25},{... | collective-permute-start | bytes 786440 | tf_op jit(solution)/shard_map/ppermute | solution.py:317
  80.3 12.8 %collective-permute-start.14 = (bf16[4,128,256]{2,1,0:T(8,128)(2,1)}, bf16[4,128,256]{2,1,0:T(8,128)(2,1)S(1)}, u32[]{:S(2)}, u32[]{:S(2)}) collective-permute-start(bf16[4,128,256]{2,1,0:T(8,128)(2,1)} %get-tuple-element.100), channel_id=1, source_target_pairs={{0,20},{4,24},{8,28},{12,0},{16,4},{20,8},{24,12},{28,16},{1,21},{... | collective-permute-start | bytes 786440 | tf_op jit(solution)/shard_map/ppermute | solution.py:317
  81.7 11.6 %collective-permute-start.15 = (bf16[128,512]{1,0:T(8,128)(2,1)S(1)}, bf16[128,512]{1,0:T(8,128)(2,1)S(1)}, u32[]{:S(2)}, u32[]{:S(2)}) collective-permute-start(bf16[128,512]{1,0:T(8,128)(2,1)S(1)} %copy-done.14), channel_id=1, source_target_pairs={{0,3},{1,0},{2,1},{3,2},{4,7},{5,4},{6,5},{7,6},{8,11},{9,8},{10,9... | collective-permute-start | bytes 393224 | tf_op jit(solution)/shard_map/ppermute | solution.py:317
  83.9 11.5 %collective-permute-start.16 = (bf16[128,512]{1,0:T(8,128)(2,1)S(1)}, bf16[128,512]{1,0:T(8,128)(2,1)S(1)}, u32[]{:S(2)}, u32[]{:S(2)}) collective-permute-start(bf16[128,512]{1,0:T(8,128)(2,1)S(1)} %copy-done.13), channel_id=1, source_target_pairs={{0,2},{1,3},{2,0},{3,1},{4,6},{5,7},{6,4},{7,5},{8,10},{9,11},{10,... | collective-permute-start | bytes 393224 | tf_op jit(solution)/shard_map/ppermute | solution.py:317
  84.6 10.8 %collective-permute-start.17 = (bf16[128,512]{1,0:T(8,128)(2,1)S(1)}, bf16[128,512]{1,0:T(8,128)(2,1)S(1)}, u32[]{:S(2)}, u32[]{:S(2)}) collective-permute-start(bf16[128,512]{1,0:T(8,128)(2,1)S(1)} %copy-done.12), channel_id=1, source_target_pairs={{0,1},{1,2},{2,3},{3,0},{4,5},{5,6},{6,7},{7,4},{8,9},{9,10},{10,1... | collective-permute-start | bytes 393224 | tf_op jit(solution)/shard_map/ppermute | solution.py:317
  95.4 7.5 %collective-permute-start.20 = (bf16[2,128,256]{2,1,0:T(8,128)(2,1)S(1)}, bf16[2,128,256]{2,1,0:T(8,128)(2,1)S(1)}, u32[]{:S(2)}, u32[]{:S(2)}) collective-permute-start(bf16[2,128,256]{2,1,0:T(8,128)(2,1)S(1)} %get-tuple-element.117), channel_id=1, source_target_pairs={{0,1},{1,2},{2,3},{3,0},{4,5},{5,6},{6,7},{7,4},{8,9},{9,10},{10,1... | collective-permute-start | bytes 393224 | tf_op jit(solution)/shard_map/ppermute | solution.py:317
  96.5 11.3 %collective-permute-start.19 = (bf16[2,128,256]{2,1,0:T(8,128)(2,1)S(1)}, bf16[2,128,256]{2,1,0:T(8,128)(2,1)S(1)}, u32[]{:S(2)}, u32[]{:S(2)}) collective-permute-start(bf16[2,128,256]{2,1,0:T(8,128)(2,1)S(1)} %get-tuple-element.118), channel_id=1, source_target_pairs={{0,2},{1,3},{2,0},{3,1},{4,6},{5,7},{6,4},{7,5},{8,10},{9,11},{10,... | collective-permute-start | bytes 393224 | tf_op jit(solution)/shard_map/ppermute | solution.py:317
  98.5 9.4 %collective-permute-start.18 = (bf16[2,128,256]{2,1,0:T(8,128)(2,1)S(1)}, bf16[2,128,256]{2,1,0:T(8,128)(2,1)S(1)}, u32[]{:S(2)}, u32[]{:S(2)}) collective-permute-start(bf16[2,128,256]{2,1,0:T(8,128)(2,1)S(1)} %get-tuple-element.119), channel_id=1, source_target_pairs={{0,3},{1,0},{2,1},{3,2},{4,7},{5,4},{6,5},{7,6},{8,11},{9,8},{10,9... | collective-permute-start | bytes 393224 | tf_op jit(solution)/shard_map/ppermute | solution.py:317
  (14 other events, 115.9 us)
